TPU v7x, 256 devices: a whole 4x4x8 slice. The times are simulated.
256 devices in a mesh: tok: 32 (over x, y, core), col: 8 (over z).
Axes of the slice: x: 4, y: 4, z: 8, core: 2. Of those that a mesh axis runs over, the one named last changes fastest.
Arguments:
- features: bfloat16 [8192, 8192], P('tok', 'col'), may hold values from -6 to 6
- out_grad: bfloat16 [8192, 8192], P('tok', 'col'), may hold values from -6 to 6
- gate_pre: bfloat16 [8192, 14336], P('tok', 'col'), may hold values from -8 to 8
- up_pre: bfloat16 [8192, 14336], P('tok', 'col'), may hold values from -6 to 6
- hidden_grad: bfloat16 [8192, 14336], P('tok', 'col'), may hold values from -6 to 6
- block_hidden: int32 [3, 144], replicated, may hold values from 0 to 111, as said below
- block_feature: int32 [3, 144], replicated, may hold values from 0 to 63
- block_slot: int32 [3, 144], replicated, may hold values from 0 to 127, as said below
Outputs:
- block_grads: float32 [8, 128, 128, 128], P('col', 'tok')
Inputs may be any that keep to these rules, and one draw needn't show every extreme that they name: `block_hidden`: within one matrix no (hidden, feature) pair repeats. Each shard of 14 consecutive hidden blocks holds at most 36 blocks of one matrix, and one shard holds exactly 36 blocks of each of the three matrices. `block_slot`: among the blocks of all three matrices whose hidden blocks lie in one shard the slots are distinct; slot // 4 is the owner; no owner holds more than 4 slots of one shard, and some owner holds exactly 4.
All inputs are finite; a program needn't handle non-finite values.
Results may differ from a plain program's by a relative error of at most 0.0029.
Values may be sent and summed in bfloat16 or wider, within the bound.
No kernel may reach another device: no remote copies, remote signals or barrier semaphores. Data moves between devices by JAX's collectives and lax.ppermute only.
A program may use at most 128 MiB of HBM per device.

v0:
```python
import math

import jax
import jax.numpy as jnp
from jax import lax
from jax.sharding import PartitionSpec as P

BS = 128


def sent_together(arrays, axis, dim, along):
    widths = [a.shape[along] for a in arrays]
    both = jnp.concatenate(arrays, axis=along)
    out = lax.all_gather(both, axis, axis=dim, tiled=True)
    return tuple(jnp.split(out, [sum(widths[:k]) for k in range(1, len(widths))], axis=along))


def pick_slots(hid_row, feat_row, slot_row, column, hid_per, capacity, slot_total):
    in_shard = hid_row // hid_per == column
    order_rank = jnp.cumsum(in_shard.astype(jnp.int32)) - 1
    wanted = jnp.arange(capacity, dtype=jnp.int32)[:, None]
    select = (in_shard[None, :] & (order_rank[None, :] == wanted)).astype(jnp.int32)
    valid_slot = jnp.sum(select, axis=1) > 0
    hid_local = jnp.sum(select * (hid_row - column * hid_per)[None, :], axis=1)
    feat_index = jnp.sum(select * feat_row[None, :], axis=1)
    dest_index = jnp.where(valid_slot, jnp.sum(select * slot_row[None, :], axis=1), slot_total)
    return (valid_slot, hid_local, feat_index, dest_index)


def on_device(
    features, out_grad, gate_pre, up_pre, hidden_grad, block_hidden, block_feature, block_slot
):
    tok_rows = features.shape[0]
    tok_count = lax.axis_size("tok")
    col_count = lax.axis_size("col")
    scaling = 1.0 / math.sqrt(tok_rows * tok_count)
    wide_feat, wide_grad = sent_together((features, out_grad), "col", 1, 0)
    gate_val = gate_pre.astype(jnp.float32)
    up_val = up_pre.astype(jnp.float32)
    grad_val = hidden_grad.astype(jnp.float32)
    sig_val = jax.nn.sigmoid(gate_val)
    act_val = gate_val * sig_val
    gate_grad = (grad_val * up_val * sig_val * (1.0 + gate_val * (1.0 - sig_val))).astype(
        jnp.bfloat16
    )
    up_grad = (grad_val * act_val).astype(jnp.bfloat16)
    hidden = (act_val * up_val).astype(jnp.bfloat16)
    hid_per = gate_pre.shape[1] // BS
    feat_blocks = wide_feat.shape[1] // BS
    column = lax.axis_index("col")
    capacity = 2 * block_hidden.shape[1] // col_count
    owner_cap = (3 * capacity + tok_count - 1) // tok_count
    slot_total = tok_count * owner_cap
    hid_sources = (gate_grad, up_grad, hidden)
    feat_sources = (wide_feat, wide_feat, wide_grad)
    tile_list = []
    dest_list = []
    for matrix in range(3):
        valid_slot, hid_local, feat_index, dest_index = pick_slots(
            block_hidden[matrix],
            block_feature[matrix],
            block_slot[matrix],
            column,
            hid_per,
            capacity,
            slot_total,
        )
        hid_cols = jnp.take(hid_sources[matrix].reshape(tok_rows, hid_per, BS), hid_local, axis=1)
        feat_cols = jnp.take(
            feat_sources[matrix].reshape(tok_rows, feat_blocks, BS), feat_index, axis=1
        )
        if matrix < 2:
            tile_set = jnp.einsum(
                "tsa,tsb->sab", feat_cols, hid_cols, preferred_element_type=jnp.float32
            )
        else:
            tile_set = jnp.einsum(
                "tsa,tsb->sab", hid_cols, feat_cols, preferred_element_type=jnp.float32
            )
        tile_set = jnp.where(valid_slot[:, None, None], tile_set * scaling, 0.0)
        tile_list.append(tile_set)
        dest_list.append(dest_index)
    all_tiles = jnp.concatenate(tile_list, axis=0)
    all_dest = jnp.concatenate(dest_list, axis=0)
    buffer = jnp.zeros((slot_total, BS, BS), jnp.float32).at[all_dest].set(all_tiles, mode="drop")
    owned = lax.psum_scatter(buffer, "tok", scatter_dimension=0, tiled=True)
    return owned[None]


def solution(mesh):
    in_specs = (
        P("tok", "col"),
        P("tok", "col"),
        P("tok", "col"),
        P("tok", "col"),
        P("tok", "col"),
        P(),
        P(),
        P(),
    )
    out_specs = P("col", "tok", None, None)
    return jax.shard_map(
        on_device, mesh=mesh, in_specs=in_specs, out_specs=out_specs, check_vma=False
    )
```

profile of v0, /device:TPU:6, one launch (start us, length us, event | category | flops | bytes accessed | tf_op | source)
XLA Modules:
  0.0 280.6 jit_solution(14652239381112132964)
XLA Ops:
  6.5 1.2 copy.32
  7.8 1.3 copy.33
  9.2 1.2 pad_maximum_fusion.1
  12.3 1.3 copy.36
  13.6 1.3 copy.35
  14.9 3.5 %fusion.24 = (bf16[256,1792]{0,1:T(8,128)(2,1)S(1)}, bf16[256,1792]{0,1:T(8,128)(2,1)S(1)}, bf16[256,1792]{0,1:T(8,128)(2,1)}) fusion(bf16[256,1792]{0,1:T(8,128)(2,1)} %copy.36, bf16[256,1792]{0,1:T(8,128)(2,1)} %copy.35, bf16[256,1792]{0,1:T(8,128)(2,1)S(1)} %copy.37), kind=kLoop, calls=%fused_computation.41 | loop fusion | flops 8257536 | bytes 5505024 | tf_op jit(solution)/shard_map/convert_element_type | solution.py:43
  19.7 1.6 copy.43
  21.7 2.5 gather_fusion.4
  24.5 2.4 gather_fusion.3
  27.3 2.4 gather_fusion.1
  30.0 77.7 %all-gather.2.cloned.1.call-done = bf16[512,8192]{0,1:T(8,128)(2,1)} async-done(((bf16[512,1024]{0,1:T(8,128)(2,1)}), bf16[512,8192]{0,1:T(8,128)(2,1)}) %all-gather.2.cloned.1.call-update) | async-done | bytes 8388624 | tf_op jit(solution)/shard_map/all_gather | solution.py:14
  107.7 5.7 %fusion.58 = (bf16[256,8192]{0,1:T(8,128)(2,1)}, bf16[256,8192]{0,1:T(8,128)(2,1)}) fusion(bf16[512,8192]{0,1:T(8,128)(2,1)} %all-gather.2.cloned.1.call-done), kind=kLoop, calls=%fused_computation.134 | loop fusion | bytes 16777216 | tf_op jit(solution)/shard_map/split | solution.py:15
  113.4 6.4 %copy.34 = bf16[256,64,128]{2,0,1:T(8,128)(2,1)} copy(bf16[256,64,128]{0,2,1:T(8,128)(2,1)} %bitcast.70) | data formatting | bytes 8388608 | tf_op jit(solution)/shard_map/reshape | solution.py:70
  119.8 6.4 %copy.44 = bf16[256,64,128]{2,0,1:T(8,128)(2,1)} copy(bf16[256,64,128]{0,2,1:T(8,128)(2,1)} %bitcast.69) | data formatting | bytes 8388608 | tf_op jit(solution)/shard_map/reshape | solution.py:70
  126.2 4.6 %gather_fusion.2 = bf16[36,256,128]{2,1,0:T(8,128)(2,1)} fusion(bf16[256,64,128]{2,0,1:T(8,128)(2,1)} %copy.34, s32[1024]{0:T(1024)S(1)} %pad_clamp_fusion.3), kind=kCustom, calls=%fused_computation.2.clone | custom fusion | bytes 4718736 | tf_op jit(solution)/shard_map/jit(_take)/gather | solution.py:69
  130.8 4.7 %gather_fusion = bf16[36,256,128]{2,1,0:T(8,128)(2,1)} fusion(bf16[256,64,128]{2,0,1:T(8,128)(2,1)} %copy.34, s32[1024]{0:T(1024)S(1)} %pad_clamp_fusion.5), kind=kCustom, calls=%fused_computation.clone | custom fusion | bytes 4718736 | tf_op jit(solution)/shard_map/jit(_take)/gather | solution.py:69
  135.5 4.7 %gather_fusion.5 = bf16[36,256,128]{2,1,0:T(8,128)(2,1)} fusion(bf16[256,64,128]{2,0,1:T(8,128)(2,1)} %copy.44, s32[1024]{0:T(1024)S(1)} %pad_clamp_fusion), kind=kCustom, calls=%fused_computation.3.clone | custom fusion | bytes 4718736 | tf_op jit(solution)/shard_map/jit(_take)/gather | solution.py:69
  140.3 3.0 %multiply_select_fusion = f32[36,128,128]{2,1,0:T(8,128)S(1)} fusion(bf16[36,256,128]{2,1,0:T(8,128)(2,1)} %gather_fusion.5, pred[36]{0:T(512)(128)(4,1)S(1)} %get-tuple-element.51, bf16[36,256,128]{2,1,0:T(8,128)(2,1)S(1)} %copy-done, pred[36]{0:T(512)(128)(4,1)S(1)} %get-tuple-element.52, pred[36]{0:T(512)(128)(4,1)S(1)} %broadcast_compare_fusion), kind=kOutput, calls=%fused_computation.26 | convolution fusion | flops 305528832 | bytes 7077996 | tf_op jit(solution)/shard_map/tsa,tsb->sab/dot_general | solution.py:77
  143.4 1.4 multiply_select_fusion.1
  145.7 1.4 multiply_select_fusion.2
  147.2 3.1 %pad_maximum_fusion = f32[108,128,128]{2,1,0:T(8,128)} fusion(f32[36,128,128]{2,1,0:T(8,128)S(1)} %multiply_select_fusion, f32[36,128,128]{2,1,0:T(8,128)S(1)} %multiply_select_fusion.1, f32[36,128,128]{2,1,0:T(8,128)S(1)} %multiply_select_fusion.2), kind=kLoop, calls=%fused_computation.7 | loop fusion | flops 3538944 | bytes 14155776 | tf_op jit(solution)/shard_map/concatenate | solution.py:83
  150.2 4.3 %broadcast_in_dim.70 = f32[128,128,128]{2,1,0:T(8,128)} broadcast(f32[]{:T(128)} %constant.64.clone.1), dimensions={} | broadcast | bytes 8388612 | tf_op jit(solution)/shard_map/broadcast_in_dim | solution.py:85
  154.5 19.4 %scatter_fusion = f32[128,128,128]{2,1,0:T(8,128)} fusion(f32[128,128,128]{2,1,0:T(8,128)} %broadcast_in_dim.70, s32[108]{0:T(128)S(1)} %fusion.54, f32[108,128,128]{2,1,0:T(8,128)} %pad_maximum_fusion), kind=kCustom, calls=%fused_computation.6 | custom fusion | bytes 21234096 | tf_op jit(solution)/shard_map/scatter | solution.py:85
  173.9 99.9 %reduce-scatter.2.cloned.1.call-done = f32[4,128,128]{2,1,0:T(8,128)} async-done(((f32[128,128,128]{2,1,0:T(8,128)}), f32[4,128,128]{2,1,0:T(8,128)}) %reduce-scatter.2.cloned.1.call-update) | async-done | bytes 262160 | tf_op jit(solution)/shard_map/reduce_scatter | solution.py:86
  (83 shorter events, 5.5 us)
Async XLA Ops:
  6.5 101.2 %all-gather.2.cloned.1.call-start = ((), (), s32[]{:S(2)}) async-start(), calls=%async_computation.1 | async-start | bytes 9437184 | tf_op jit(solution)/shard_map/all_gather | solution.py:14
  7.8 2.6 copy-start.8
  7.8 4.0 %copy-start.5 = (bf16[256,1792]{1,0:T(8,128)(2,1)S(1)}, bf16[256,1792]{1,0:T(8,128)(2,1)}, u32[]{:S(2)}) copy-start(bf16[256,1792]{1,0:T(8,128)(2,1)} %param.14) | copy-start | bytes 2752516
  9.1 3.2 %copy-start.6 = (bf16[256,1792]{1,0:T(8,128)(2,1)S(1)}, bf16[256,1792]{1,0:T(8,128)(2,1)}, u32[]{:S(2)}) copy-start(bf16[256,1792]{1,0:T(8,128)(2,1)} %param.15) | copy-start | bytes 2752516
  10.3 263.4 %reduce-scatter.2.cloned.1.call-start = ((), (), s32[]{:S(2)}) async-start(), calls=%async_computation.2 | async-start | bytes 8650752 | tf_op jit(solution)/shard_map/reduce_scatter | solution.py:86
  12.3 1.3 copy-start.7
  18.4 3.0 %copy-start.9 = (s32[3,144]{1,0:T(4,128)S(1)}, s32[3,144]{1,0:T(4,128)}, u32[]{:S(2)}) copy-start(s32[3,144]{1,0:T(4,128)} %param.18) | copy-start | bytes 5188
  18.4 3.0 %copy-start.10 = (s32[3,144]{1,0:T(4,128)S(1)}, s32[3,144]{1,0:T(4,128)}, u32[]{:S(2)}) copy-start(s32[3,144]{1,0:T(4,128)} %param.19) | copy-start | bytes 5188
  135.5 4.7 %copy-start = (bf16[36,256,128]{2,1,0:T(8,128)(2,1)S(1)}, bf16[36,256,128]{2,1,0:T(8,128)(2,1)}, u32[]{:S(2)}) copy-start(bf16[36,256,128]{2,1,0:T(8,128)(2,1)} %gather_fusion.4) | copy-start | bytes 7077892
  140.3 3.0 %copy-start.1 = (bf16[36,256,128]{2,1,0:T(8,128)(2,1)S(1)}, bf16[36,256,128]{2,1,0:T(8,128)(2,1)}, u32[]{:S(2)}) copy-start(bf16[36,256,128]{2,1,0:T(8,128)(2,1)} %gather_fusion.3) | copy-start | bytes 7077892
  140.3 3.1 %copy-start.4 = (bf16[36,256,128]{2,1,0:T(8,128)(2,1)S(1)}, bf16[36,256,128]{2,1,0:T(8,128)(2,1)}, u32[]{:S(2)}) copy-start(bf16[36,256,128]{2,1,0:T(8,128)(2,1)} %gather_fusion.2) | copy-start | bytes 7077892
  143.4 1.7 copy-start.2
  143.4 2.4 copy-start.3
Sparse Core Ops, SparseCore 0:
  10.4 97.2 all-gather.1
  174.0 99.6 reduce-scatter.1
where the time goes:
time: 281 us
  waiting for transfers between devices  178 us (63%)
  local copies, waits for them, and re-layouts  73.6 us (26%)
  between operations  13.7 us (5%)
  other arithmetic  9.79 us (3%)
  matrix products  5.85 us (2%)
    reduce_scatter x1, waiting for transfers between devices, on_device(): owned = lax.psum_scatter(buffer, 'tok', scatter_dimension=0, tiled=True)  99.9 us
    all_gather x1, waiting for transfers between devices, sent_together(): out = lax.all_gather(both, axis, axis=dim, tiled=True)  77.7 us
    scatter x1, local copies, waits for them, and re-layouts, on_device(): jnp.zeros((slot_total, BS, BS), jnp.float32).at[all_dest]  19.4 us
    gather x3, local copies, waits for them, and re-layouts, on_device(): jnp.take(feat_sources[matrix].reshape(tok_rows, feat_blocks, BS), feat_in...  14.1 us
    reshape x2, local copies, waits for them, and re-layouts, on_device(): feat_sources[matrix].reshape(tok_rows, feat_blocks, BS)  12.8 us
    gather x3, local copies, waits for them, and re-layouts, on_device(): jnp.take(hid_sources[matrix].reshape(tok_rows, hid_per, BS), hid_local, a...  7.33 us
    unnamed x27, local copies, waits for them, and re-layouts  6.72 us
    split x1, local copies, waits for them, and re-layouts, sent_together(): jnp.split(out, [sum(widths[:k]) for k in range(1, len(widths))], axis=along)  5.72 us
  transfers between devices with their start and end apart: 2, of which 2 were waited for; matrix products, arithmetic and copies ran while one was open for 7% of the time, Pallas kernels for 0%

commit v1 on v0

v1 whole, which is shorter than its diff:
```python
import math

import jax
import jax.numpy as jnp
from jax import lax
from jax.experimental import pallas as pl
from jax.experimental.pallas import tpu as pltpu
from jax.sharding import PartitionSpec as P

BS = 128
NX, NY, NC = 4, 4, 2
CAPO = 4
F32, BF16 = jnp.float32, jnp.bfloat16
ANY = pl.BlockSpec(memory_space=pl.ANY)


def gate_kernel(gate_ref, up_ref, grad_ref, out_ref):
    gate = gate_ref[...].astype(F32)
    up = up_ref[...].astype(F32)
    grad = grad_ref[...].astype(F32)
    sig = jax.nn.sigmoid(gate)
    act = gate * sig
    out_ref[0, 0] = (grad * up * sig * (1.0 + gate * (1.0 - sig))).astype(BF16)
    out_ref[1, 0] = (grad * act).astype(BF16)
    out_ref[2, 0] = (act * up).astype(BF16)


def hidden_blocks(gate_pre, up_pre, hidden_grad):
    rows, width = gate_pre.shape
    blocks = width // BS
    spec = pl.BlockSpec((rows, BS), lambda i: (0, i))
    out = pl.pallas_call(
        gate_kernel,
        grid=(blocks,),
        in_specs=[spec] * 3,
        out_specs=pl.BlockSpec((3, 1, rows, BS), lambda i: (0, i, 0, 0)),
        out_shape=jax.ShapeDtypeStruct((3, blocks, rows, BS), BF16),
        cost_estimate=pl.CostEstimate(flops=0, bytes_accessed=6 * rows * width * 2, transcendentals=0),
        name="gate_blocks",
    )(gate_pre, up_pre, hidden_grad)
    return out.reshape(3 * blocks, rows, BS)


def tile_kernel(n_chunk, per, n_hid, scale, code_ref, *refs):
    chunks, (hid_ref, own_ref, send_ref, blk, sems) = refs[:n_chunk], refs[n_chunk:]
    copies = []
    for i, chunk in enumerate(chunks):
        for k in range(per):
            at = i * per + k
            copies.append(
                pltpu.make_async_copy(chunk.at[:, pl.ds(k * BS, BS)], blk.at[at], sems.at[at])
            )
    at = n_chunk * per
    copies.append(pltpu.make_async_copy(hid_ref, blk.at[pl.ds(at, n_hid)], sems.at[at]))
    for copy in copies:
        copy.start()
    for copy in copies:
        copy.wait()

    def tile(p):
        code = code_ref[p]
        found = jnp.maximum(code - 1, 0)
        left = blk[found // 256]
        right = blk[found % 256]
        out = lax.dot_general(left, right, (((0,), (0,)), ((), ())), preferred_element_type=F32)
        return out * jnp.where(code > 0, scale, 0.0)

    half = own_ref.shape[0]
    step = 4

    def own_body(i, carry):
        for k in range(step):
            own_ref[i * step + k] = tile(i * step + k)
        return carry

    def send_body(i, carry):
        for k in range(step):
            send_ref[i * step + k] = tile(half + i * step + k).astype(BF16)
        return carry

    lax.fori_loop(0, half // step, send_body, 0)
    lax.fori_loop(0, half // step, own_body, 0)


def make_tiles(codes, chunks, hid, scale):
    rows, width = chunks[0].shape
    per = width // BS
    n_chunk, n_hid = len(chunks), hid.shape[0]
    half = codes.shape[0] // 2
    blocks = n_chunk * per + n_hid

    def body(*refs):
        tile_kernel(n_chunk, per, n_hid, scale, *refs)

    return pl.pallas_call(
        body,
        in_specs=[pl.BlockSpec(memory_space=pltpu.SMEM)] + [ANY] * (n_chunk + 1),
        out_specs=[pl.BlockSpec(memory_space=pltpu.VMEM)] * 2,
        out_shape=[
            jax.ShapeDtypeStruct((half, BS, BS), F32),
            jax.ShapeDtypeStruct((half, BS, BS), BF16),
        ],
        scratch_shapes=[
            pltpu.VMEM((blocks, rows, BS), BF16),
            pltpu.SemaphoreType.DMA((n_chunk * per + 1,)),
        ],
        compiler_params=pltpu.CompilerParams(vmem_limit_bytes=40 * 2**20),
        name="tiles",
    )(codes, *chunks, hid)


def place():
    me = lax.axis_index("tok")
    return me // (NY * NC), (me // NC) % NY, me % NC


def shift_perm(axis, by):
    pairs = []
    for i in range(NX * NY * NC):
        x, y, c = i // (NY * NC), (i // NC) % NY, i % NC
        if axis == "x":
            x = (x + by) % NX
        elif axis == "y":
            y = (y + by) % NY
        else:
            c = (c + by) % NC
        pairs.append((i, (x * NY + y) * NC + c))
    return pairs


def shift(value, axis, by):
    return lax.ppermute(value, "tok", shift_perm(axis, by))


def slot_order():
    x, y, c = place()
    p = jnp.arange(NX * NY * NC * CAPO, dtype=jnp.int32)
    core, half, d1, d2, j = p // 64, (p // 32) % 2, (p // 8) % 4, (p // 2) % 4, p % 2
    to_x = (x + jnp.where(half == 0, d1, d2)) % NX
    to_y = (y + jnp.where(half == 0, d2, d1)) % NY
    to_c = (c + core) % NC
    return ((to_x * NY + to_y) * NC + to_c) * CAPO + half * 2 + j


def tile_codes(block_hidden, block_feature, block_slot, n_col, per, hid_per):
    col = lax.axis_index("col")
    matrix = jnp.arange(3, dtype=jnp.int32)[:, None]
    source = block_feature // per
    x_at = ((col - source) % n_col) * per + block_feature % per
    y_at = n_col * per + ((source - col) % n_col) * per + block_feature % per
    h_at = 2 * n_col * per + matrix * hid_per + block_hidden % hid_per
    left = jnp.where(matrix == 2, h_at, x_at)
    right = jnp.where(matrix == 2, y_at, h_at)
    here = block_hidden // hid_per == col
    value = jnp.where(here, 1 + left * 256 + right, 0).reshape(-1)
    hit = slot_order()[:, None] == block_slot.reshape(-1)[None, :]
    return jnp.sum(jnp.where(hit, value[None, :], 0), axis=1)


def first_stage(total, axis):
    cut = total.shape[1] // 2
    far = total[2].astype(BF16)
    up_far = shift(far[:cut], axis, 1)
    down_far = shift(far[cut:], axis, -1)
    near_up = jnp.concatenate([total[1, :cut] + up_far.astype(F32), total[1, cut:]]).astype(BF16)
    near_down = jnp.concatenate([total[3, :cut], total[3, cut:] + down_far.astype(F32)]).astype(BF16)
    from_down = shift(near_up, axis, 1)
    from_up = shift(near_down, axis, -1)
    return total[0] + from_down.astype(F32) + from_up.astype(F32)


def second_stage(total, axis):
    sent = total.astype(BF16)
    got = [shift(sent[k], axis, k) for k in (2, 1, 3)]
    out = total[0]
    for g in got:
        out = out + g.astype(F32)
    return out


def on_device(
    features, out_grad, gate_pre, up_pre, hidden_grad, block_hidden, block_feature, block_slot
):
    tok_rows = features.shape[0]
    n_col = lax.axis_size("col")
    scale = 1.0 / math.sqrt(tok_rows * lax.axis_size("tok"))
    forward = [(i, (i + 1) % n_col) for i in range(n_col)]
    back = [(i, (i - 1) % n_col) for i in range(n_col)]
    xs, ys = [features], [out_grad]
    for _ in range(n_col - 1):
        xs.append(lax.ppermute(xs[-1], "col", forward))
        ys.append(lax.ppermute(ys[-1], "col", back))
    hid = hidden_blocks(gate_pre, up_pre, hidden_grad)
    codes = tile_codes(
        block_hidden, block_feature, block_slot, n_col, features.shape[1] // BS, gate_pre.shape[1] // BS
    )
    own, send = make_tiles(codes, xs + ys, hid, scale)
    total = own + shift(send, "core", 1).astype(F32)
    total = total.reshape(2, 4, 4, 2, BS, BS)
    half_x = first_stage(total[0], "x")
    half_y = first_stage(total[1], "y")
    out_x = second_stage(half_x, "y")
    out_y = second_stage(half_y, "x")
    return jnp.concatenate([out_x, out_y])[None]


def solution(mesh):
    in_specs = (P("tok", "col"),) * 5 + (P(), P(), P())
    return jax.shard_map(
        on_device,
        mesh=mesh,
        in_specs=in_specs,
        out_specs=P("col", "tok", None, None),
        check_vma=False,
    )
```

time: 281 us -> 163 us (0.58)
  waiting for transfers between devices: 178 us -> 71 us
  local copies, waits for them, and re-layouts: 73.6 us -> 14.1 us
  starting transfers between devices: 0.04 us -> 45.6 us
  Pallas kernels: 0 us -> 24.8 us
  between operations: 13.7 us -> 0.24 us
  matrix products: 5.85 us -> 0 us
  other arithmetic: 9.79 us -> 5.69 us
    reduce_scatter x1 -> x0, waiting for transfers between devices: 99.9 us -> none  [on_device(): owned = lax.psum_scatter(buffer, 'tok', scatter_dimension=0, tiled=True)]
    all_gather x1 -> x0, waiting for transfers between devices: 77.7 us -> none  [sent_together(): out = lax.all_gather(both, axis, axis=dim, tiled=True)]
    ppermute x0 -> x29, waiting for transfers between devices: none -> 71 us  [the longest x7 54.5 us: on_device(): xs.append(lax.ppermute(xs[-1], 'col', forward))]
    ppermute x0 -> x29, starting transfers between devices: none -> 45.6 us  [the longest x7 23.9 us: on_device(): ys.append(lax.ppermute(ys[-1], 'col', back))]
    pallas_call x0 -> x2, Pallas kernels: none -> 24.8 us  [the longest x1 15.7 us: make_tiles(): pl.pallas_call(body, in_specs=[pl.BlockSpec(memory_space=pltpu.SMEM)] + [...]
    gather x6 -> x0, local copies, waits for them, and re-layouts: 21.4 us -> none  [the longest x3 14.1 us: on_device(): jnp.take(feat_sources[matrix].reshape(tok_rows, feat_blocks, BS), feat_in...]
    scatter x1 -> x0, local copies, waits for them, and re-layouts: 19.4 us -> none  [on_device(): jnp.zeros((slot_total, BS, BS), jnp.float32).at[all_dest]]
    reshape x5 -> x0, local copies, waits for them, and re-layouts: 15.5 us -> none  [the longest x2 12.8 us: on_device(): feat_sources[matrix].reshape(tok_rows, feat_blocks, BS)]
  transfers between devices with their start and end apart: 2 -> 29, of which waited for: 2 -> 14; matrix products, arithmetic and copies ran while one was open for 7% -> 2% of each run, Pallas kernels for 0% -> 6%
where the time goes in v1:
time: 163 us; the launch traced here: 161 us
  waiting for transfers between devices  71 us (44%)
  starting transfers between devices  45.6 us (28%)
  Pallas kernels  24.8 us (15%)
  local copies, waits for them, and re-layouts  14.1 us (9%)
  other arithmetic  5.69 us (3%)
    ppermute x7, waiting for transfers between devices, on_device(): xs.append(lax.ppermute(xs[-1], 'col', forward))  54.5 us
    ppermute x7, starting transfers between devices, on_device(): ys.append(lax.ppermute(ys[-1], 'col', back))  23.9 us
    ppermute x15, starting transfers between devices, shift(): return lax.ppermute(value, 'tok', shift_perm(axis, by))  19.8 us
    ppermute x15, waiting for transfers between devices, shift(): return lax.ppermute(value, 'tok', shift_perm(axis, by))  16 us
    pallas_call x1, Pallas kernels, make_tiles(): pl.pallas_call(body, in_specs=[pl.BlockSpec(memory_space=pltpu.SMEM)] + [...  15.7 us
    unnamed x30, local copies, waits for them, and re-layouts  12.8 us
    pallas_call x1, Pallas kernels, hidden_blocks(): pl.pallas_call(gate_kernel, grid=(blocks,), in_specs=[spec] * 3, out_spec...  9.14 us
    another operation x5, other arithmetic  3.62 us
  transfers between devices with their start and end apart: 29, of which 14 were waited for; matrix products, arithmetic and copies ran while one was open for 2% of the time, Pallas kernels for 6%

profile of v1, /device:TPU:6, one launch (start us, length us, event | category | flops | bytes accessed | tf_op | source)
XLA Modules:
  0.0 161.5 jit_solution(6364796807613122217)
XLA Ops:
  0.0 1.9 %collective-permute-start = (bf16[256,1024]{1,0:T(8,128)(2,1)}, bf16[256,1024]{1,0:T(8,128)(2,1)S(1)}, u32[]{:S(2)}, u32[]{:S(2)}) collective-permute-start(bf16[256,1024]{1,0:T(8,128)(2,1)} %refs_1_.1), channel_id=1, source_target_pairs={{0,1},{1,2},{2,3},{3,4},{4,5},{5,6},{6,7},{7,0},{8,9},{9,10},{10,1... | collective-permute-start | bytes 1572872 | tf_op jit(solution)/shard_map/ppermute | solution.py:191
  1.9 3.9 %collective-permute-start.7 = (bf16[256,1024]{1,0:T(8,128)(2,1)}, bf16[256,1024]{1,0:T(8,128)(2,1)S(1)}, u32[]{:S(2)}, u32[]{:S(2)}) collective-permute-start(bf16[256,1024]{1,0:T(8,128)(2,1)} %refs_9_.1), channel_id=1, source_target_pairs={{0,7},{1,0},{2,1},{3,2},{4,3},{5,4},{6,5},{7,6},{8,15},{9,8},{10,9... | collective-permute-start | bytes 1572872 | tf_op jit(solution)/shard_map/ppermute | solution.py:192
  5.9 12.1 %collective-permute-done.refs_2_ = bf16[256,1024]{1,0:T(8,128)(2,1)S(1)} collective-permute-done((bf16[256,1024]{1,0:T(8,128)(2,1)}, bf16[256,1024]{1,0:T(8,128)(2,1)S(1)}, u32[]{:S(2)}, u32[]{:S(2)}) %collective-permute-start) | collective-permute-done | bytes 524320 | tf_op jit(solution)/shard_map/ppermute | solution.py:191
  18.0 3.2 %collective-permute-start.8 = (bf16[256,1024]{1,0:T(8,128)(2,1)S(1)}, bf16[256,1024]{1,0:T(8,128)(2,1)S(1)}, u32[]{:S(2)}, u32[]{:S(2)}) collective-permute-start(bf16[256,1024]{1,0:T(8,128)(2,1)S(1)} %collective-permute-done.7.refs_10_), channel_id=1, source_target_pairs={{0,7},{1,0},{2,1},{3,2},{4,3},{5,4},{6,5},{7,6},{8,15},{9,8},{10,9... | collective-permute-start | bytes 1572872 | tf_op jit(solution)/shard_map/ppermute | solution.py:192
  21.2 11.1 %collective-permute-done.1.refs_3_ = bf16[256,1024]{1,0:T(8,128)(2,1)S(1)} collective-permute-done((bf16[256,1024]{1,0:T(8,128)(2,1)S(1)}, bf16[256,1024]{1,0:T(8,128)(2,1)S(1)}, u32[]{:S(2)}, u32[]{:S(2)}) %collective-permute-start.1) | collective-permute-done | bytes 524320 | tf_op jit(solution)/shard_map/ppermute | solution.py:191
  32.3 3.2 %collective-permute-start.9 = (bf16[256,1024]{1,0:T(8,128)(2,1)S(1)}, bf16[256,1024]{1,0:T(8,128)(2,1)S(1)}, u32[]{:S(2)}, u32[]{:S(2)}) collective-permute-start(bf16[256,1024]{1,0:T(8,128)(2,1)S(1)} %collective-permute-done.8.refs_11_), channel_id=1, source_target_pairs={{0,7},{1,0},{2,1},{3,2},{4,3},{5,4},{6,5},{7,6},{8,15},{9,8},{10,9... | collective-permute-start | bytes 1572872 | tf_op jit(solution)/shard_map/ppermute | solution.py:192
  35.6 10.2 %collective-permute-done.2.refs_4_ = bf16[256,1024]{1,0:T(8,128)(2,1)S(1)} collective-permute-done((bf16[256,1024]{1,0:T(8,128)(2,1)S(1)}, bf16[256,1024]{1,0:T(8,128)(2,1)S(1)}, u32[]{:S(2)}, u32[]{:S(2)}) %collective-permute-start.2) | collective-permute-done | bytes 524320 | tf_op jit(solution)/shard_map/ppermute | solution.py:191
  46.5 3.2 %collective-permute-start.10 = (bf16[256,1024]{1,0:T(8,128)(2,1)S(1)}, bf16[256,1024]{1,0:T(8,128)(2,1)S(1)}, u32[]{:S(2)}, u32[]{:S(2)}) collective-permute-start(bf16[256,1024]{1,0:T(8,128)(2,1)S(1)} %collective-permute-done.9.refs_12_), channel_id=1, source_target_pairs={{0,7},{1,0},{2,1},{3,2},{4,3},{5,4},{6,5},{7,6},{8,15},{9,8},{10,9... | collective-permute-start | bytes 1572872 | tf_op jit(solution)/shard_map/ppermute | solution.py:192
  50.5 7.6 %collective-permute-done.3.refs_5_ = bf16[256,1024]{1,0:T(8,128)(2,1)S(1)} collective-permute-done((bf16[256,1024]{1,0:T(8,128)(2,1)S(1)}, bf16[256,1024]{1,0:T(8,128)(2,1)S(1)}, u32[]{:S(2)}, u32[]{:S(2)}) %collective-permute-start.3) | collective-permute-done | bytes 524320 | tf_op jit(solution)/shard_map/ppermute | solution.py:191
  59.0 3.2 %collective-permute-start.11 = (bf16[256,1024]{1,0:T(8,128)(2,1)S(1)}, bf16[256,1024]{1,0:T(8,128)(2,1)S(1)}, u32[]{:S(2)}, u32[]{:S(2)}) collective-permute-start(bf16[256,1024]{1,0:T(8,128)(2,1)S(1)} %collective-permute-done.10.refs_13_), channel_id=1, source_target_pairs={{0,7},{1,0},{2,1},{3,2},{4,3},{5,4},{6,5},{7,6},{8,15},{9,8},{10,9... | collective-permute-start | bytes 1572872 | tf_op jit(solution)/shard_map/ppermute | solution.py:192
  63.0 7.2 %collective-permute-done.4.refs_6_ = bf16[256,1024]{1,0:T(8,128)(2,1)S(1)} collective-permute-done((bf16[256,1024]{1,0:T(8,128)(2,1)S(1)}, bf16[256,1024]{1,0:T(8,128)(2,1)S(1)}, u32[]{:S(2)}, u32[]{:S(2)}) %collective-permute-start.4) | collective-permute-done | bytes 524320 | tf_op jit(solution)/shard_map/ppermute | solution.py:191
  71.1 3.2 %collective-permute-start.12 = (bf16[256,1024]{1,0:T(8,128)(2,1)S(1)}, bf16[256,1024]{1,0:T(8,128)(2,1)}, u32[]{:S(2)}, u32[]{:S(2)}) collective-permute-start(bf16[256,1024]{1,0:T(8,128)(2,1)S(1)} %collective-permute-done.11.refs_14_), channel_id=1, source_target_pairs={{0,7},{1,0},{2,1},{3,2},{4,3},{5,4},{6,5},{7,6},{8,15},{9,8},{10,9... | collective-permute-start | bytes 1572872 | tf_op jit(solution)/shard_map/ppermute | solution.py:192
  75.9 6.3 %collective-permute-done.5.refs_7_ = bf16[256,1024]{1,0:T(8,128)(2,1)} collective-permute-done((bf16[256,1024]{1,0:T(8,128)(2,1)S(1)}, bf16[256,1024]{1,0:T(8,128)(2,1)}, u32[]{:S(2)}, u32[]{:S(2)}) %collective-permute-start.5) | collective-permute-done | bytes 524320 | tf_op jit(solution)/shard_map/ppermute | solution.py:191
  82.6 3.8 %collective-permute-start.13 = (bf16[256,1024]{1,0:T(8,128)(2,1)}, bf16[256,1024]{1,0:T(8,128)(2,1)}, u32[]{:S(2)}, u32[]{:S(2)}) collective-permute-start(bf16[256,1024]{1,0:T(8,128)(2,1)} %collective-permute-done.12.refs_15_), channel_id=1, source_target_pairs={{0,7},{1,0},{2,1},{3,2},{4,3},{5,4},{6,5},{7,6},{8,15},{9,8},{10,9... | collective-permute-start | bytes 1572872 | tf_op jit(solution)/shard_map/ppermute | solution.py:192
  87.3 9.1 %gate_blocks.1 = bf16[3,14,256,128]{3,2,1,0:T(8,128)(2,1)} custom-call(bf16[256,1792]{1,0:T(8,128)(2,1)} %gate_ref.1, bf16[256,1792]{1,0:T(8,128)(2,1)} %up_ref.1, bf16[256,1792]{1,0:T(8,128)(2,1)} %grad_ref.1), custom_call_target="tpu_custom_call" | custom-call | bytes 5505024 | tf_op jit(solution)/shard_map/gate_blocks/pallas_call | solution.py:32
  104.7 15.7 %tiles.1 = (f32[64,128,128]{2,1,0:T(8,128)}, bf16[64,128,128]{2,1,0:T(8,128)(2,1)S(1)}) custom-call(s32[128]{0:T(128)S(1)} %select_reduce_fusion.refs_0_, bf16[256,1024]{1,0:T(8,128)(2,1)S(1)} %copy-done.1, bf16[256,1024]{1,0:T(8,128)(2,1)S(1)} %collective-permute-done.refs_2_, bf16[256,1024]{1,0:T(8,128)(2,1)S(1)} %collective-permute-done.1.refs_3_, ...), custom_call_target="tpu_custom_call" | custom-call | tf_op jit(solution)/shard_map/tiles/pallas_call | solution.py:95
  120.5 4.1 %collective-permute-done.14 = bf16[64,128,128]{2,1,0:T(8,128)(2,1)S(1)} collective-permute-done((bf16[64,128,128]{2,1,0:T(8,128)(2,1)S(1)}, bf16[64,128,128]{2,1,0:T(8,128)(2,1)S(1)}, u32[]{:S(2)}, u32[]{:S(2)}) %collective-permute-start.14) | collective-permute-done | bytes 2097184 | tf_op jit(solution)/shard_map/ppermute | solution.py:132
  124.7 3.2 %fusion.47 = (bf16[64,128,128]{2,1,0:T(8,128)(2,1)S(1)}, f32[64,128,128]{2,1,0:T(8,128)S(1)}) fusion(f32[64,128,128]{2,1,0:T(8,128)} %get-tuple-element.7, bf16[64,128,128]{2,1,0:T(8,128)(2,1)S(1)} %collective-permute-done.14), kind=kLoop, calls=%fused_computation.124 | loop fusion | flops 3145728 | bytes 12582912 | tf_op jit(solution)/shard_map/convert.17
  128.3 3.1 %collective-permute-start.24 = (bf16[2,2,128,128]{3,2,1,0:T(8,128)(2,1)S(1)}, bf16[2,2,128,128]{3,2,1,0:T(8,128)(2,1)S(1)}, u32[]{:S(2)}, u32[]{:S(2)}) collective-permute-start(bf16[2,2,128,128]{3,2,1,0:T(8,128)(2,1)S(1)} %bitcast.79), channel_id=1, source_target_pairs={{0,48},{8,56},{16,0},{24,8},{32,16},{40,24},{48,32},{56,40},{64,11... | collective-permute-start | bytes 393224 | tf_op jit(solution)/shard_map/ppermute | solution.py:132
  133.7 2.8 %collective-permute-done.15 = bf16[2,2,128,128]{3,2,1,0:T(8,128)(2,1)S(1)} collective-permute-done((bf16[2,2,128,128]{3,2,1,0:T(8,128)(2,1)S(1)}, bf16[2,2,128,128]{3,2,1,0:T(8,128)(2,1)S(1)}, u32[]{:S(2)}, u32[]{:S(2)}) %collective-permute-start.15) | collective-permute-done | bytes 131104 | tf_op jit(solution)/shard_map/ppermute | solution.py:132
  138.6 3.0 %collective-permute-start.16 = (bf16[4,2,128,128]{3,2,1,0:T(8,128)(2,1)S(1)}, bf16[4,2,128,128]{3,2,1,0:T(8,128)(2,1)S(1)}, u32[]{:S(2)}, u32[]{:S(2)}) collective-permute-start(bf16[4,2,128,128]{3,2,1,0:T(8,128)(2,1)S(1)} %pad_maximum_fusion), channel_id=1, source_target_pairs={{0,64},{8,72},{16,80},{24,88},{32,96},{40,104},{48,112},{56,120},{... | collective-permute-start | bytes 786440 | tf_op jit(solution)/shard_map/ppermute | solution.py:132
  141.7 3.3 %collective-permute-start.25 = (bf16[4,2,128,128]{3,2,1,0:T(8,128)(2,1)S(1)}, bf16[4,2,128,128]{3,2,1,0:T(8,128)(2,1)S(1)}, u32[]{:S(2)}, u32[]{:S(2)}) collective-permute-start(bf16[4,2,128,128]{3,2,1,0:T(8,128)(2,1)S(1)} %pad_maximum_fusion.3), channel_id=1, source_target_pairs={{0,48},{8,56},{16,0},{24,8},{32,16},{40,24},{48,32},{56,40},{64,11... | collective-permute-start | bytes 786440 | tf_op jit(solution)/shard_map/ppermute | solution.py:132
  150.2 3.8 %collective-permute-done.23 = bf16[4,2,128,128]{3,2,1,0:T(8,128)(2,1)S(1)} collective-permute-done((bf16[4,2,128,128]{3,2,1,0:T(8,128)(2,1)S(1)}, bf16[4,2,128,128]{3,2,1,0:T(8,128)(2,1)S(1)}, u32[]{:S(2)}, u32[]{:S(2)}) %collective-permute-start.23) | collective-permute-done | bytes 262176 | tf_op jit(solution)/shard_map/ppermute | solution.py:132
  155.0 3.2 %collective-permute-start.27 = (bf16[2,128,128]{2,1,0:T(8,128)(2,1)S(1)}, bf16[2,128,128]{2,1,0:T(8,128)(2,1)S(1)}, u32[]{:S(2)}, u32[]{:S(2)}) collective-permute-start(bf16[2,128,128]{2,1,0:T(8,128)(2,1)S(1)} %get-tuple-element.36), channel_id=1, source_target_pairs={{0,64},{8,72},{16,80},{24,88},{32,96},{40,104},{48,112},{56,120},{... | collective-permute-start | bytes 196616 | tf_op jit(solution)/shard_map/ppermute | solution.py:132
  (94 shorter events, 29.5 us)
Async XLA Ops:
  0.0 18.0 %collective-permute-start = (bf16[256,1024]{1,0:T(8,128)(2,1)}, bf16[256,1024]{1,0:T(8,128)(2,1)S(1)}, u32[]{:S(2)}, u32[]{:S(2)}) collective-permute-start(bf16[256,1024]{1,0:T(8,128)(2,1)} %refs_1_.1), channel_id=1, source_target_pairs={{0,1},{1,2},{2,3},{3,4},{4,5},{5,6},{6,7},{7,0},{8,9},{9,10},{10,1... | collective-permute-start | bytes 1572872 | tf_op jit(solution)/shard_map/ppermute | solution.py:191
  1.9 16.1 %collective-permute-start.7 = (bf16[256,1024]{1,0:T(8,128)(2,1)}, bf16[256,1024]{1,0:T(8,128)(2,1)S(1)}, u32[]{:S(2)}, u32[]{:S(2)}) collective-permute-start(bf16[256,1024]{1,0:T(8,128)(2,1)} %refs_9_.1), channel_id=1, source_target_pairs={{0,7},{1,0},{2,1},{3,2},{4,3},{5,4},{6,5},{7,6},{8,15},{9,8},{10,9... | collective-permute-start | bytes 1572872 | tf_op jit(solution)/shard_map/ppermute | solution.py:192
  18.0 14.3 %collective-permute-start.1 = (bf16[256,1024]{1,0:T(8,128)(2,1)S(1)}, bf16[256,1024]{1,0:T(8,128)(2,1)S(1)}, u32[]{:S(2)}, u32[]{:S(2)}) collective-permute-start(bf16[256,1024]{1,0:T(8,128)(2,1)S(1)} %collective-permute-done.refs_2_), channel_id=1, source_target_pairs={{0,1},{1,2},{2,3},{3,4},{4,5},{5,6},{6,7},{7,0},{8,9},{9,10},{10,1... | collective-permute-start | bytes 1572872 | tf_op jit(solution)/shard_map/ppermute | solution.py:191
  18.0 14.3 %collective-permute-start.8 = (bf16[256,1024]{1,0:T(8,128)(2,1)S(1)}, bf16[256,1024]{1,0:T(8,128)(2,1)S(1)}, u32[]{:S(2)}, u32[]{:S(2)}) collective-permute-start(bf16[256,1024]{1,0:T(8,128)(2,1)S(1)} %collective-permute-done.7.refs_10_), channel_id=1, source_target_pairs={{0,7},{1,0},{2,1},{3,2},{4,3},{5,4},{6,5},{7,6},{8,15},{9,8},{10,9... | collective-permute-start | bytes 1572872 | tf_op jit(solution)/shard_map/ppermute | solution.py:192
  32.3 13.4 %collective-permute-start.2 = (bf16[256,1024]{1,0:T(8,128)(2,1)S(1)}, bf16[256,1024]{1,0:T(8,128)(2,1)S(1)}, u32[]{:S(2)}, u32[]{:S(2)}) collective-permute-start(bf16[256,1024]{1,0:T(8,128)(2,1)S(1)} %collective-permute-done.1.refs_3_), channel_id=1, source_target_pairs={{0,1},{1,2},{2,3},{3,4},{4,5},{5,6},{6,7},{7,0},{8,9},{9,10},{10,1... | collective-permute-start | bytes 1572872 | tf_op jit(solution)/shard_map/ppermute | solution.py:191
  32.3 14.2 %collective-permute-start.9 = (bf16[256,1024]{1,0:T(8,128)(2,1)S(1)}, bf16[256,1024]{1,0:T(8,128)(2,1)S(1)}, u32[]{:S(2)}, u32[]{:S(2)}) collective-permute-start(bf16[256,1024]{1,0:T(8,128)(2,1)S(1)} %collective-permute-done.8.refs_11_), channel_id=1, source_target_pairs={{0,7},{1,0},{2,1},{3,2},{4,3},{5,4},{6,5},{7,6},{8,15},{9,8},{10,9... | collective-permute-start | bytes 1572872 | tf_op jit(solution)/shard_map/ppermute | solution.py:192
  45.7 12.5 %collective-permute-start.3 = (bf16[256,1024]{1,0:T(8,128)(2,1)S(1)}, bf16[256,1024]{1,0:T(8,128)(2,1)S(1)}, u32[]{:S(2)}, u32[]{:S(2)}) collective-permute-start(bf16[256,1024]{1,0:T(8,128)(2,1)S(1)} %collective-permute-done.2.refs_4_), channel_id=1, source_target_pairs={{0,1},{1,2},{2,3},{3,4},{4,5},{5,6},{6,7},{7,0},{8,9},{9,10},{10,1... | collective-permute-start | bytes 1572872 | tf_op jit(solution)/shard_map/ppermute | solution.py:191
  46.5 12.5 %collective-permute-start.10 = (bf16[256,1024]{1,0:T(8,128)(2,1)S(1)}, bf16[256,1024]{1,0:T(8,128)(2,1)S(1)}, u32[]{:S(2)}, u32[]{:S(2)}) collective-permute-start(bf16[256,1024]{1,0:T(8,128)(2,1)S(1)} %collective-permute-done.9.refs_12_), channel_id=1, source_target_pairs={{0,7},{1,0},{2,1},{3,2},{4,3},{5,4},{6,5},{7,6},{8,15},{9,8},{10,9... | collective-permute-start | bytes 1572872 | tf_op jit(solution)/shard_map/ppermute | solution.py:192
  58.2 12.1 %collective-permute-start.4 = (bf16[256,1024]{1,0:T(8,128)(2,1)S(1)}, bf16[256,1024]{1,0:T(8,128)(2,1)S(1)}, u32[]{:S(2)}, u32[]{:S(2)}) collective-permute-start(bf16[256,1024]{1,0:T(8,128)(2,1)S(1)} %collective-permute-done.3.refs_5_), channel_id=1, source_target_pairs={{0,1},{1,2},{2,3},{3,4},{4,5},{5,6},{6,7},{7,0},{8,9},{9,10},{10,1... | collective-permute-start | bytes 1572872 | tf_op jit(solution)/shard_map/ppermute | solution.py:191
  59.0 12.1 %collective-permute-start.11 = (bf16[256,1024]{1,0:T(8,128)(2,1)S(1)}, bf16[256,1024]{1,0:T(8,128)(2,1)S(1)}, u32[]{:S(2)}, u32[]{:S(2)}) collective-permute-start(bf16[256,1024]{1,0:T(8,128)(2,1)S(1)} %collective-permute-done.10.refs_13_), channel_id=1, source_target_pairs={{0,7},{1,0},{2,1},{3,2},{4,3},{5,4},{6,5},{7,6},{8,15},{9,8},{10,9... | collective-permute-start | bytes 1572872 | tf_op jit(solution)/shard_map/ppermute | solution.py:192
  70.3 11.9 %collective-permute-start.5 = (bf16[256,1024]{1,0:T(8,128)(2,1)S(1)}, bf16[256,1024]{1,0:T(8,128)(2,1)}, u32[]{:S(2)}, u32[]{:S(2)}) collective-permute-start(bf16[256,1024]{1,0:T(8,128)(2,1)S(1)} %collective-permute-done.4.refs_6_), channel_id=1, source_target_pairs={{0,1},{1,2},{2,3},{3,4},{4,5},{5,6},{6,7},{7,0},{8,9},{9,10},{10,1... | collective-permute-start | bytes 1572872 | tf_op jit(solution)/shard_map/ppermute | solution.py:191
  71.1 11.6 %collective-permute-start.12 = (bf16[256,1024]{1,0:T(8,128)(2,1)S(1)}, bf16[256,1024]{1,0:T(8,128)(2,1)}, u32[]{:S(2)}, u32[]{:S(2)}) collective-permute-start(bf16[256,1024]{1,0:T(8,128)(2,1)S(1)} %collective-permute-done.11.refs_14_), channel_id=1, source_target_pairs={{0,7},{1,0},{2,1},{3,2},{4,3},{5,4},{6,5},{7,6},{8,15},{9,8},{10,9... | collective-permute-start | bytes 1572872 | tf_op jit(solution)/shard_map/ppermute | solution.py:192
  82.2 14.5 %collective-permute-start.6 = (bf16[256,1024]{1,0:T(8,128)(2,1)}, bf16[256,1024]{1,0:T(8,128)(2,1)}, u32[]{:S(2)}, u32[]{:S(2)}) collective-permute-start(bf16[256,1024]{1,0:T(8,128)(2,1)} %collective-permute-done.5.refs_7_), channel_id=1, source_target_pairs={{0,1},{1,2},{2,3},{3,4},{4,5},{5,6},{6,7},{7,0},{8,9},{9,10},{10,1... | collective-permute-start | bytes 1572872 | tf_op jit(solution)/shard_map/ppermute | solution.py:191
  82.6 14.0 %collective-permute-start.13 = (bf16[256,1024]{1,0:T(8,128)(2,1)}, bf16[256,1024]{1,0:T(8,128)(2,1)}, u32[]{:S(2)}, u32[]{:S(2)}) collective-permute-start(bf16[256,1024]{1,0:T(8,128)(2,1)} %collective-permute-done.12.refs_15_), channel_id=1, source_target_pairs={{0,7},{1,0},{2,1},{3,2},{4,3},{5,4},{6,5},{7,6},{8,15},{9,8},{10,9... | collective-permute-start | bytes 1572872 | tf_op jit(solution)/shard_map/ppermute | solution.py:192
  128.3 13.3 %collective-permute-start.24 = (bf16[2,2,128,128]{3,2,1,0:T(8,128)(2,1)S(1)}, bf16[2,2,128,128]{3,2,1,0:T(8,128)(2,1)S(1)}, u32[]{:S(2)}, u32[]{:S(2)}) collective-permute-start(bf16[2,2,128,128]{3,2,1,0:T(8,128)(2,1)S(1)} %bitcast.79), channel_id=1, source_target_pairs={{0,48},{8,56},{16,0},{24,8},{32,16},{40,24},{48,32},{56,40},{64,11... | collective-permute-start | bytes 393224 | tf_op jit(solution)/shard_map/ppermute | solution.py:132
  131.8 9.7 %collective-permute-start.22 = (bf16[2,2,128,128]{3,2,1,0:T(8,128)(2,1)S(1)}, bf16[2,2,128,128]{3,2,1,0:T(8,128)(2,1)S(1)}, u32[]{:S(2)}, u32[]{:S(2)}) collective-permute-start(bf16[2,2,128,128]{3,2,1,0:T(8,128)(2,1)S(1)} %bitcast.78), channel_id=1, source_target_pairs={{0,16},{8,24},{16,32},{24,40},{32,48},{40,56},{48,0},{56,8},{64,80... | collective-permute-start | bytes 393224 | tf_op jit(solution)/shard_map/ppermute | solution.py:132
  131.8 6.2 %collective-permute-start.17 = (bf16[2,2,128,128]{3,2,1,0:T(8,128)(2,1)S(1)}, bf16[2,2,128,128]{3,2,1,0:T(8,128)(2,1)S(1)}, u32[]{:S(2)}, u32[]{:S(2)}) collective-permute-start(bf16[2,2,128,128]{3,2,1,0:T(8,128)(2,1)S(1)} %bitcast.80), channel_id=1, source_target_pairs={{0,192},{8,200},{16,208},{24,216},{32,224},{40,232},{48,240},{56,2... | collective-permute-start | bytes 393224 | tf_op jit(solution)/shard_map/ppermute | solution.py:132
  138.1 8.2 %collective-permute-start.18 = (bf16[4,2,128,128]{3,2,1,0:T(8,128)(2,1)S(1)}, bf16[4,2,128,128]{3,2,1,0:T(8,128)(2,1)S(1)}, u32[]{:S(2)}, u32[]{:S(2)}) collective-permute-start(bf16[4,2,128,128]{3,2,1,0:T(8,128)(2,1)S(1)} %pad_maximum_fusion.1), channel_id=1, source_target_pairs={{0,192},{8,200},{16,208},{24,216},{32,224},{40,232},{48,240},{56,2... | collective-permute-start | bytes 786440 | tf_op jit(solution)/shard_map/ppermute | solution.py:132
  138.6 7.8 %collective-permute-start.16 = (bf16[4,2,128,128]{3,2,1,0:T(8,128)(2,1)S(1)}, bf16[4,2,128,128]{3,2,1,0:T(8,128)(2,1)S(1)}, u32[]{:S(2)}, u32[]{:S(2)}) collective-permute-start(bf16[4,2,128,128]{3,2,1,0:T(8,128)(2,1)S(1)} %pad_maximum_fusion), channel_id=1, source_target_pairs={{0,64},{8,72},{16,80},{24,88},{32,96},{40,104},{48,112},{56,120},{... | collective-permute-start | bytes 786440 | tf_op jit(solution)/shard_map/ppermute | solution.py:132
  141.7 8.6 %collective-permute-start.25 = (bf16[4,2,128,128]{3,2,1,0:T(8,128)(2,1)S(1)}, bf16[4,2,128,128]{3,2,1,0:T(8,128)(2,1)S(1)}, u32[]{:S(2)}, u32[]{:S(2)}) collective-permute-start(bf16[4,2,128,128]{3,2,1,0:T(8,128)(2,1)S(1)} %pad_maximum_fusion.3), channel_id=1, source_target_pairs={{0,48},{8,56},{16,0},{24,8},{32,16},{40,24},{48,32},{56,40},{64,11... | collective-permute-start | bytes 786440 | tf_op jit(solution)/shard_map/ppermute | solution.py:132
  145.0 9.1 %collective-permute-start.23 = (bf16[4,2,128,128]{3,2,1,0:T(8,128)(2,1)S(1)}, bf16[4,2,128,128]{3,2,1,0:T(8,128)(2,1)S(1)}, u32[]{:S(2)}, u32[]{:S(2)}) collective-permute-start(bf16[4,2,128,128]{3,2,1,0:T(8,128)(2,1)S(1)} %pad_maximum_fusion.2), channel_id=1, source_target_pairs={{0,16},{8,24},{16,32},{24,40},{32,48},{40,56},{48,0},{56,8},{64,80... | collective-permute-start | bytes 786440 | tf_op jit(solution)/shard_map/ppermute | solution.py:132
  146.5 8.5 %collective-permute-start.19 = (bf16[2,128,128]{2,1,0:T(8,128)(2,1)S(1)}, bf16[2,128,128]{2,1,0:T(8,128)(2,1)S(1)}, u32[]{:S(2)}, u32[]{:S(2)}) collective-permute-start(bf16[2,128,128]{2,1,0:T(8,128)(2,1)S(1)} %get-tuple-element.31), channel_id=1, source_target_pairs={{0,32},{8,40},{16,48},{24,56},{32,0},{40,8},{48,16},{56,24},{64,96... | collective-permute-start | bytes 196616 | tf_op jit(solution)/shard_map/ppermute | solution.py:132
  148.2 10.0 %collective-permute-start.21 = (bf16[2,128,128]{2,1,0:T(8,128)(2,1)S(1)}, bf16[2,128,128]{2,1,0:T(8,128)(2,1)S(1)}, u32[]{:S(2)}, u32[]{:S(2)}) collective-permute-start(bf16[2,128,128]{2,1,0:T(8,128)(2,1)S(1)} %get-tuple-element.32), channel_id=1, source_target_pairs={{0,48},{8,56},{16,0},{24,8},{32,16},{40,24},{48,32},{56,40},{64,11... | collective-permute-start | bytes 196616 | tf_op jit(solution)/shard_map/ppermute | solution.py:132
  149.5 8.7 %collective-permute-start.20 = (bf16[2,128,128]{2,1,0:T(8,128)(2,1)S(1)}, bf16[2,128,128]{2,1,0:T(8,128)(2,1)S(1)}, u32[]{:S(2)}, u32[]{:S(2)}) collective-permute-start(bf16[2,128,128]{2,1,0:T(8,128)(2,1)S(1)} %get-tuple-element.33), channel_id=1, source_target_pairs={{0,16},{8,24},{16,32},{24,40},{32,48},{40,56},{48,0},{56,8},{64,80... | collective-permute-start | bytes 196616 | tf_op jit(solution)/shard_map/ppermute | solution.py:132
  (20 other events, 58.5 us)

commit v2 on v1

v2 whole, which is shorter than its diff:
```python
import math

import jax
import jax.numpy as jnp
from jax import lax
from jax.experimental import pallas as pl
from jax.experimental.pallas import tpu as pltpu
from jax.sharding import PartitionSpec as P

BS = 128
NX, NY, NC = 4, 4, 2
CAPO = 4
UNROLL = 4
F32, BF16 = jnp.float32, jnp.bfloat16
ANY = pl.BlockSpec(memory_space=pl.ANY)


def gate_kernel(gate_ref, up_ref, grad_ref, out_ref):
    gate = gate_ref[...].astype(F32)
    up = up_ref[...].astype(F32)
    grad = grad_ref[...].astype(F32)
    sig = jax.nn.sigmoid(gate)
    act = gate * sig
    out_ref[0, 0] = (grad * up * sig * (1.0 + gate * (1.0 - sig))).astype(BF16)
    out_ref[1, 0] = (grad * act).astype(BF16)
    out_ref[2, 0] = (act * up).astype(BF16)


def hidden_blocks(gate_pre, up_pre, hidden_grad):
    rows, width = gate_pre.shape
    blocks = width // BS
    spec = pl.BlockSpec((rows, BS), lambda i: (0, i))
    out = pl.pallas_call(
        gate_kernel,
        grid=(blocks,),
        in_specs=[spec] * 3,
        out_specs=pl.BlockSpec((3, 1, rows, BS), lambda i: (0, i, 0, 0)),
        out_shape=jax.ShapeDtypeStruct((3, blocks, rows, BS), BF16),
        cost_estimate=pl.CostEstimate(flops=0, bytes_accessed=6 * rows * width * 2, transcendentals=0),
        name="gate_blocks",
    )(gate_pre, up_pre, hidden_grad)
    return out.reshape(3 * blocks, rows, BS)


def tile_kernel(first, last, per, n_hid, scale, tab_ref, *refs):
    n_chunk = 4 * (last - first)
    chunks, hids = refs[:n_chunk], refs[n_chunk : n_chunk + 2]
    out_ref, blk, stage, zero, in_sems, out_sems, zero_sem = refs[-7:]
    rows = hids[0].shape[1]
    copies = []
    for i, chunk in enumerate(chunks):
        step, kind, core = i // 4, (i // 2) % 2, i % 2
        for k in range(per):
            at = (step * 2 + kind) * per + k
            copies.append(
                (chunk.at[:, pl.ds(k * BS, BS)], blk.at[at, pl.ds(core * rows, rows)])
            )
    n_feat = n_chunk // 2 * per
    for core in range(2):
        copies.append((hids[core], blk.at[pl.ds(n_feat, n_hid), pl.ds(core * rows, rows)]))
    copies = [pltpu.make_async_copy(a, b, in_sems.at[i]) for i, (a, b) in enumerate(copies)]
    for copy in copies:
        copy.start()

    places = out_ref.shape[0]
    begin, end = tab_ref[places + first], tab_ref[places + last]
    if first == 0:
        zero[...] = jnp.zeros_like(zero)
        empty = tab_ref[places + 8]

        def zero_start(i, carry):
            pltpu.make_async_copy(zero, out_ref.at[tab_ref[i] % 64], zero_sem).start()
            return carry

        def zero_wait(i, carry):
            pltpu.make_async_copy(zero, out_ref.at[tab_ref[i] % 64], zero_sem).wait()
            return carry

        lax.fori_loop(empty, places, zero_start, 0)
    for copy in copies:
        copy.wait()

    def tile(i):
        entry = tab_ref[jnp.minimum(i, end - 1)]
        hid = n_feat + (entry // 64) % 64
        feat = (entry // 4096) % 8
        down = (entry // (4096 * 64)) % 2
        step = (entry // (4096 * 8)) % 8
        feat = ((step - first) * 2 + down) * per + feat
        left = blk[jnp.where(down == 1, hid, feat)]
        right = blk[jnp.where(down == 1, feat, hid)]
        out = lax.dot_general(left, right, (((0,), (0,)), ((), ())), preferred_element_type=F32)
        return out * scale

    def put(n, k):
        i = begin + n * UNROLL + k
        at = (n % 2) * UNROLL + k
        entry = tab_ref[jnp.minimum(i, end - 1)]
        return pltpu.make_async_copy(stage.at[at], out_ref.at[entry % 64], out_sems.at[at])

    rounds = (end - begin + UNROLL - 1) // UNROLL

    def body(n, carry):
        @pl.when(n >= 2)
        def _():
            for k in range(UNROLL):
                put(n - 2, k).wait()

        made = [tile(begin + n * UNROLL + k) for k in range(UNROLL)]
        for k in range(UNROLL):
            stage[(n % 2) * UNROLL + k] = made[k]
        for k in range(UNROLL):

            @pl.when(begin + n * UNROLL + k < end)
            def _():
                put(n, k).start()

        return carry

    lax.fori_loop(0, rounds, body, 0)

    @pl.when(rounds >= 2)
    def _():
        for k in range(UNROLL):
            put(rounds - 2, k).wait()

    for k in range(UNROLL):

        @pl.when((rounds >= 1) & (begin + (rounds - 1) * UNROLL + k < end))
        def _():
            put(rounds - 1, k).wait()

    if first == 0:
        lax.fori_loop(empty, places, zero_wait, 0)


def make_tiles(first, last, table, chunks, hids, before, scale):
    rows, width = chunks[0].shape
    per = width // BS
    n_hid = hids[0].shape[0]
    places = NX * NY * CAPO
    blocks = len(chunks) // 2 * per + n_hid
    operands = (table, *chunks, *hids) + (() if before is None else (before,))

    def body(*refs):
        tile_kernel(first, last, per, n_hid, scale, *refs)

    return pl.pallas_call(
        body,
        in_specs=[pl.BlockSpec(memory_space=pltpu.SMEM)] + [ANY] * (len(operands) - 1),
        out_specs=ANY,
        out_shape=jax.ShapeDtypeStruct((places, BS, BS), F32),
        scratch_shapes=[
            pltpu.VMEM((blocks, 2 * rows, BS), BF16),
            pltpu.VMEM((2 * UNROLL, BS, BS), F32),
            pltpu.VMEM((BS, BS), F32),
            pltpu.SemaphoreType.DMA((len(chunks) * per + 2,)),
            pltpu.SemaphoreType.DMA((2 * UNROLL,)),
            pltpu.SemaphoreType.DMA,
        ],
        input_output_aliases={} if before is None else {len(operands) - 1: 0},
        cost_estimate=pl.CostEstimate(flops=2 * 8 * (last - first) * 512 * BS * BS, bytes_accessed=8 * 2**20, transcendentals=0),
        compiler_params=pltpu.CompilerParams(vmem_limit_bytes=60 * 2**20),
        name=f"tiles_{first}_{last}",
    )(*operands)


def place():
    me = lax.axis_index("tok")
    return me // (NY * NC), (me // NC) % NY, me % NC


def shift_perm(axis, by):
    pairs = []
    for i in range(NX * NY * NC):
        x, y, c = i // (NY * NC), (i // NC) % NY, i % NC
        if axis == "x":
            x = (x + by) % NX
        elif axis == "y":
            y = (y + by) % NY
        else:
            c = (c + by) % NC
        pairs.append((i, (x * NY + y) * NC + c))
    return pairs


def shift(value, axis, by):
    return lax.ppermute(value, "tok", shift_perm(axis, by))


def slot_order():
    x, y, c = place()
    p = jnp.arange(NX * NY * CAPO, dtype=jnp.int32)
    half, d1, d2, j = p // 32, (p // 8) % 4, (p // 2) % 4, p % 2
    to_x = (x + jnp.where(half == 0, d1, d2)) % NX
    to_y = (y + jnp.where(half == 0, d2, d1)) % NY
    return ((to_x * NY + to_y) * NC + c) * CAPO + half * 2 + j


def tile_table(block_hidden, block_feature, block_slot, n_col, per, hid_per):
    col = lax.axis_index("col")
    matrix = jnp.arange(3, dtype=jnp.int32)[:, None]
    source = block_feature // per
    down = (matrix == 2).astype(jnp.int32)
    step = jnp.where(down == 1, source - col, col - source) % n_col
    hid = matrix * hid_per + block_hidden % hid_per
    value = 1 + (((down * 8 + step) * 8 + block_feature % per) * 64 + hid)
    value = jnp.where(block_hidden // hid_per == col, value, 0).reshape(-1)
    hit = slot_order()[:, None] == block_slot.reshape(-1)[None, :]
    code = jnp.sum(jnp.where(hit, value[None, :], 0), axis=1)
    places = code.shape[0]
    p = jnp.arange(places, dtype=jnp.int32)
    entry = jnp.where(code > 0, (code - 1) * 64 + p, p)
    key = jnp.where(code > 0, (entry // (4096 * 8)) % 8, 8) * places + p
    rank = jnp.sum((key[None, :] < key[:, None]).astype(jnp.int32), axis=1)
    ordered = jnp.sum(jnp.where(rank[None, :] == p[:, None], entry[None, :], 0), axis=1)
    bounds = jnp.arange(16, dtype=jnp.int32) * places
    starts = jnp.sum((key[None, :] < bounds[:, None]).astype(jnp.int32), axis=1)
    return jnp.concatenate([ordered, starts])


def first_stage(total, axis):
    cut = total.shape[1] // 2
    far = total[2].astype(BF16)
    up_far = shift(far[:cut], axis, 1)
    down_far = shift(far[cut:], axis, -1)
    near_up = jnp.concatenate([total[1, :cut] + up_far.astype(F32), total[1, cut:]]).astype(BF16)
    near_down = jnp.concatenate([total[3, :cut], total[3, cut:] + down_far.astype(F32)]).astype(BF16)
    from_down = shift(near_up, axis, 1)
    from_up = shift(near_down, axis, -1)
    return total[0] + from_down.astype(F32) + from_up.astype(F32)


def second_stage(total, axis):
    sent = total.astype(BF16)
    got = [shift(sent[k], axis, k) for k in (2, 1, 3)]
    out = total[0]
    for g in got:
        out = out + g.astype(F32)
    return out


def on_device(
    features, out_grad, gate_pre, up_pre, hidden_grad, block_hidden, block_feature, block_slot
):
    tok_rows = features.shape[0]
    n_col = lax.axis_size("col")
    scale = 1.0 / math.sqrt(tok_rows * lax.axis_size("tok"))
    forward = [(i, (i + 1) % n_col) for i in range(n_col)]
    back = [(i, (i - 1) % n_col) for i in range(n_col)]
    table = tile_table(
        block_hidden, block_feature, block_slot, n_col, features.shape[1] // BS, gate_pre.shape[1] // BS
    )
    xs, ys = [features], [out_grad]
    pairs = []
    total = None
    for step in range(n_col):
        x, y = xs[-1], ys[-1]
        if step == 1:
            x, gates = lax.optimization_barrier((x, (gate_pre, up_pre, hidden_grad)))
            hid = hidden_blocks(*gates)
        if step == 2:
            x, y, hid, table = lax.optimization_barrier((x, y, hid, table))
            hids = (hid, shift(hid, "core", 1))
        if step == 4:
            x, y, hids = lax.optimization_barrier((x, y, hids))
        if step == 5:
            total = make_tiles(0, 4, table, sum(pairs[:4], []), hids, total, scale)
            x, y, total = lax.optimization_barrier((x, y, total))
        if step == n_col - 1:
            total = make_tiles(4, 7, table, sum(pairs[4:], []), hids, total, scale)
            x, y, total = lax.optimization_barrier((x, y, total))
        else:
            xs.append(lax.ppermute(x, "col", forward))
            ys.append(lax.ppermute(y, "col", back))
        pairs.append([x, shift(x, "core", 1), y, shift(y, "core", 1)])
    total = make_tiles(7, 8, table, pairs[7], hids, total, scale)
    total = total.reshape(2, 4, 4, 2, BS, BS)
    half_x = first_stage(total[0], "x")
    half_y = first_stage(total[1], "y")
    out_x = second_stage(half_x, "y")
    out_y = second_stage(half_y, "x")
    return jnp.concatenate([out_x, out_y])[None]


def solution(mesh):
    in_specs = (P("tok", "col"),) * 5 + (P(), P(), P())
    return jax.shard_map(
        on_device,
        mesh=mesh,
        in_specs=in_specs,
        out_specs=P("col", "tok", None, None),
        check_vma=False,
    )
```

time: 163 us -> 159 us (0.975)
  waiting for transfers between devices: 71 us -> 60.4 us
  Pallas kernels: 24.8 us -> 34 us
  local copies, waits for them, and re-layouts: 14.1 us -> 10.2 us
  starting transfers between devices: 45.6 us -> 49.2 us
  other arithmetic: 5.69 us -> 4.02 us
    pallas_call x1 -> x3, Pallas kernels: 15.7 us -> 24.9 us  [make_tiles(): pl.pallas_call(body, in_specs=[pl.BlockSpec(memory_space=pltpu.SMEM)] + [...]
    ppermute x14, waiting for transfers between devices: 55 us -> 45.8 us  [the longest x7 45.8 us: on_device(): xs.append(lax.ppermute(x, 'col', forward))]
    unnamed x30 -> x54, local copies, waits for them, and re-layouts: 12.8 us -> 6.51 us
    ppermute x15 -> x31, starting transfers between devices: 19.8 us -> 24.3 us  [shift(): return lax.ppermute(value, 'tok', shift_perm(axis, by))]
    another operation x5, other arithmetic: 3.62 us -> 0.82 us
    slice x1, local copies, waits for them, and re-layouts: 0.27 us -> 2.64 us  [on_device(): half_x = first_stage(total[0], 'x')]
    ppermute x15 -> x31, waiting for transfers between devices: 16 us -> 14.6 us  [shift(): return lax.ppermute(value, 'tok', shift_perm(axis, by))]
  transfers between devices with their start and end apart: 29 -> 45, of which waited for: 14 -> 15; matrix products, arithmetic and copies ran while one was open for 2% -> 2% of each run, Pallas kernels for 6% -> 18%
where the time goes in v2:
time: 159 us; the launch traced here: 158 us
  waiting for transfers between devices  60.4 us (38%)
  starting transfers between devices  49.2 us (31%)
  Pallas kernels  34 us (21%)
  local copies, waits for them, and re-layouts  10.2 us (6%)
  other arithmetic  4.02 us (3%)
    ppermute x7, waiting for transfers between devices, on_device(): xs.append(lax.ppermute(x, 'col', forward))  45.8 us
    pallas_call x3, Pallas kernels, make_tiles(): pl.pallas_call(body, in_specs=[pl.BlockSpec(memory_space=pltpu.SMEM)] + [...  24.9 us
    ppermute x31, starting transfers between devices, shift(): return lax.ppermute(value, 'tok', shift_perm(axis, by))  24.3 us
    ppermute x7, starting transfers between devices, on_device(): ys.append(lax.ppermute(y, 'col', back))  22.9 us
    ppermute x31, waiting for transfers between devices, shift(): return lax.ppermute(value, 'tok', shift_perm(axis, by))  14.6 us
    pallas_call x1, Pallas kernels, hidden_blocks(): pl.pallas_call(gate_kernel, grid=(blocks,), in_specs=[spec] * 3, out_spec...  9.03 us
    unnamed x54, local copies, waits for them, and re-layouts  6.51 us
  transfers between devices with their start and end apart: 45, of which 15 were waited for; matrix products, arithmetic and copies ran while one was open for 2% of the time, Pallas kernels for 18%

profile of v2, /device:TPU:6, one launch (start us, length us, event | category | flops | bytes accessed | tf_op | source)
XLA Modules:
  0.0 158.3 jit_solution(2856690047410921368)
XLA Ops:
  0.0 1.9 %collective-permute-start = (bf16[256,1024]{1,0:T(8,128)(2,1)}, bf16[256,1024]{1,0:T(8,128)(2,1)}, u32[]{:S(2)}, u32[]{:S(2)}) collective-permute-start(bf16[256,1024]{1,0:T(8,128)(2,1)} %refs_1_.1), channel_id=1, source_target_pairs={{0,1},{1,2},{2,3},{3,4},{4,5},{5,6},{6,7},{7,0},{8,9},{9,10},{10,1... | collective-permute-start | bytes 1572872 | tf_op jit(solution)/shard_map/ppermute | solution.py:274
  1.9 3.9 %collective-permute-start.2 = (bf16[256,1024]{1,0:T(8,128)(2,1)}, bf16[256,1024]{1,0:T(8,128)(2,1)S(1)}, u32[]{:S(2)}, u32[]{:S(2)}) collective-permute-start(bf16[256,1024]{1,0:T(8,128)(2,1)} %refs_3_.1), channel_id=1, source_target_pairs={{0,7},{1,0},{2,1},{3,2},{4,3},{5,4},{6,5},{7,6},{8,15},{9,8},{10,9... | collective-permute-start | bytes 1572872 | tf_op jit(solution)/shard_map/ppermute | solution.py:275
  7.8 10.3 %collective-permute-done.refs_5_ = bf16[256,1024]{1,0:T(8,128)(2,1)} collective-permute-done((bf16[256,1024]{1,0:T(8,128)(2,1)}, bf16[256,1024]{1,0:T(8,128)(2,1)}, u32[]{:S(2)}, u32[]{:S(2)}) %collective-permute-start) | collective-permute-done | bytes 524320 | tf_op jit(solution)/shard_map/ppermute | solution.py:274
  18.1 3.2 %collective-permute-start.3 = (bf16[256,1024]{1,0:T(8,128)(2,1)S(1)}, bf16[256,1024]{1,0:T(8,128)(2,1)S(1)}, u32[]{:S(2)}, u32[]{:S(2)}) collective-permute-start(bf16[256,1024]{1,0:T(8,128)(2,1)S(1)} %collective-permute-done.2.refs_7_), channel_id=1, source_target_pairs={{0,7},{1,0},{2,1},{3,2},{4,3},{5,4},{6,5},{7,6},{8,15},{9,8},{10,9... | collective-permute-start | bytes 1572872 | tf_op jit(solution)/shard_map/ppermute | solution.py:275
  22.4 9.0 %gate_blocks.1 = bf16[3,14,256,128]{3,2,1,0:T(8,128)(2,1)} custom-call(bf16[256,1792]{1,0:T(8,128)(2,1)} %gate_ref, bf16[256,1792]{1,0:T(8,128)(2,1)} %up_ref, bf16[256,1792]{1,0:T(8,128)(2,1)} %grad_ref), custom_call_target="tpu_custom_call" | custom-call | bytes 5505024 | tf_op jit(solution)/shard_map/gate_blocks/pallas_call | solution.py:33
  34.7 3.2 %collective-permute-start.6 = (bf16[256,1024]{1,0:T(8,128)(2,1)}, bf16[256,1024]{1,0:T(8,128)(2,1)S(1)}, u32[]{:S(2)}, u32[]{:S(2)}) collective-permute-start(bf16[256,1024]{1,0:T(8,128)(2,1)} %copy-done.17), channel_id=1, source_target_pairs={{0,7},{1,0},{2,1},{3,2},{4,3},{5,4},{6,5},{7,6},{8,15},{9,8},{10,9... | collective-permute-start | bytes 1572872 | tf_op jit(solution)/shard_map/ppermute | solution.py:275
  38.0 2.5 %collective-permute-done.11.refs_2_ = bf16[256,1024]{1,0:T(8,128)(2,1)S(1)} collective-permute-done((bf16[256,1024]{1,0:T(8,128)(2,1)S(1)}, bf16[256,1024]{1,0:T(8,128)(2,1)S(1)}, u32[]{:S(2)}, u32[]{:S(2)}) %collective-permute-start.11) | collective-permute-done | bytes 524320 | tf_op jit(solution)/shard_map/ppermute | solution.py:188
  40.8 9.2 %collective-permute-done.4.refs_13_ = bf16[256,1024]{1,0:T(8,128)(2,1)S(1)} collective-permute-done((bf16[256,1024]{1,0:T(8,128)(2,1)}, bf16[256,1024]{1,0:T(8,128)(2,1)S(1)}, u32[]{:S(2)}, u32[]{:S(2)}) %collective-permute-start.4) | collective-permute-done | bytes 524320 | tf_op jit(solution)/shard_map/ppermute | solution.py:274
  50.0 3.2 %collective-permute-start.7 = (bf16[256,1024]{1,0:T(8,128)(2,1)S(1)}, bf16[256,1024]{1,0:T(8,128)(2,1)S(1)}, u32[]{:S(2)}, u32[]{:S(2)}) collective-permute-start(bf16[256,1024]{1,0:T(8,128)(2,1)S(1)} %collective-permute-done.6.refs_15_), channel_id=1, source_target_pairs={{0,7},{1,0},{2,1},{3,2},{4,3},{5,4},{6,5},{7,6},{8,15},{9,8},{10,9... | collective-permute-start | bytes 1572872 | tf_op jit(solution)/shard_map/ppermute | solution.py:275
  53.8 10.4 %collective-permute-done.5.refs_1_ = bf16[256,1024]{1,0:T(8,128)(2,1)S(1)} collective-permute-done((bf16[256,1024]{1,0:T(8,128)(2,1)S(1)}, bf16[256,1024]{1,0:T(8,128)(2,1)S(1)}, u32[]{:S(2)}, u32[]{:S(2)}) %collective-permute-start.5) | collective-permute-done | bytes 524320 | tf_op jit(solution)/shard_map/ppermute | solution.py:274
  64.8 2.9 %collective-permute-start.10 = (bf16[256,1024]{1,0:T(8,128)(2,1)S(1)}, bf16[256,1024]{1,0:T(8,128)(2,1)}, u32[]{:S(2)}, u32[]{:S(2)}) collective-permute-start(bf16[256,1024]{1,0:T(8,128)(2,1)S(1)} %collective-permute-done.7.refs_3_), channel_id=1, source_target_pairs={{0,7},{1,0},{2,1},{3,2},{4,3},{5,4},{6,5},{7,6},{8,15},{9,8},{10,9... | collective-permute-start | bytes 1572872 | tf_op jit(solution)/shard_map/ppermute | solution.py:275
  69.5 11.0 %tiles_0_4.1.refs_15_ = f32[64,128,128]{2,1,0:T(8,128)} custom-call(s32[80]{0:T(128)} %pad_add_fusion.refs_0_, bf16[256,1024]{1,0:T(8,128)(2,1)} %refs_1_.1, bf16[256,1024]{1,0:T(8,128)(2,1)} %copy-done.18, bf16[256,1024]{1,0:T(8,128)(2,1)} %refs_3_.1, bf16[256,1024]{1,0:T(8,128)(2,1)} %copy-done.21, bf16[256,1024]{1,0:T(8,128)(2,1)} %collective-permute-done.refs_5_, ...), custom_call_target="tpu_custom_call" | custom-call | flops 536870912 | bytes 8388608 | tf_op jit(solution)/shard_map/tiles_0_4/pallas_call | solution.py:148
  80.5 2.4 %collective-permute-done.9.refs_5_ = bf16[256,1024]{1,0:T(8,128)(2,1)} collective-permute-done((bf16[256,1024]{1,0:T(8,128)(2,1)S(1)}, bf16[256,1024]{1,0:T(8,128)(2,1)}, u32[]{:S(2)}, u32[]{:S(2)}) %collective-permute-start.9) | collective-permute-done | bytes 524320 | tf_op jit(solution)/shard_map/ppermute | solution.py:274
  82.8 3.2 %collective-permute-start.21 = (bf16[256,1024]{1,0:T(8,128)(2,1)}, bf16[256,1024]{1,0:T(8,128)(2,1)S(1)}, u32[]{:S(2)}, u32[]{:S(2)}) collective-permute-start(bf16[256,1024]{1,0:T(8,128)(2,1)} %collective-permute-done.10.refs_7_), channel_id=1, source_target_pairs={{0,7},{1,0},{2,1},{3,2},{4,3},{5,4},{6,5},{7,6},{8,15},{9,8},{10,9... | collective-permute-start | bytes 1572872 | tf_op jit(solution)/shard_map/ppermute | solution.py:275
  86.6 10.6 %collective-permute-done.19.refs_9_ = bf16[256,1024]{1,0:T(8,128)(2,1)S(1)} collective-permute-done((bf16[256,1024]{1,0:T(8,128)(2,1)}, bf16[256,1024]{1,0:T(8,128)(2,1)S(1)}, u32[]{:S(2)}, u32[]{:S(2)}) %collective-permute-start.19) | collective-permute-done | bytes 524320 | tf_op jit(solution)/shard_map/ppermute | solution.py:274
  97.8 3.2 %collective-permute-start.22 = (bf16[256,1024]{1,0:T(8,128)(2,1)S(1)}, bf16[256,1024]{1,0:T(8,128)(2,1)S(1)}, u32[]{:S(2)}, u32[]{:S(2)}) collective-permute-start(bf16[256,1024]{1,0:T(8,128)(2,1)S(1)} %collective-permute-done.21.refs_11_), channel_id=1, source_target_pairs={{0,7},{1,0},{2,1},{3,2},{4,3},{5,4},{6,5},{7,6},{8,15},{9,8},{10,9... | collective-permute-start | bytes 1572872 | tf_op jit(solution)/shard_map/ppermute | solution.py:275
  102.6 8.5 %tiles_4_7.1.refs_7_ = f32[64,128,128]{2,1,0:T(8,128)} custom-call(s32[80]{0:T(128)} %pad_add_fusion.refs_0_, bf16[256,1024]{1,0:T(8,128)(2,1)} %copy-done.2, bf16[256,1024]{1,0:T(8,128)(2,1)} %collective-permute-done.23.refs_2_, bf16[256,1024]{1,0:T(8,128)(2,1)} %copy-done.3, bf16[256,1024]{1,0:T(8,128)(2,1)} %copy-done.6, ...), custom_call_target="tpu_custom_call", output_to_operand_aliasing={{}: (15, {})} | custom-call | flops 402653184 | bytes 8388608 | tf_op jit(solution)/shard_map/tiles_4_7/pallas_call | solution.py:148
  116.5 5.5 %tiles_7_8.1 = f32[64,128,128]{2,1,0:T(8,128)} custom-call(s32[80]{0:T(128)} %pad_add_fusion.refs_0_, bf16[256,1024]{1,0:T(8,128)(2,1)} %copy-done.7, bf16[256,1024]{1,0:T(8,128)(2,1)} %copy-done.12, bf16[256,1024]{1,0:T(8,128)(2,1)} %copy-done.9, bf16[256,1024]{1,0:T(8,128)(2,1)} %copy-done.13, ...), custom_call_target="tpu_custom_call", output_to_operand_aliasing={{}: (7, {})} | custom-call | flops 134217728 | bytes 8388608 | tf_op jit(solution)/shard_map/tiles_7_8/pallas_call | solution.py:148
  122.0 2.6 %fusion.41 = (f32[32,128,128]{2,1,0:T(8,128)S(1)}, f32[32,128,128]{2,1,0:T(8,128)S(1)}) fusion(f32[64,128,128]{2,1,0:T(8,128)} %tiles_7_8.1), kind=kLoop, calls=%fused_computation.122 | loop fusion | bytes 8388608 | tf_op jit(solution)/shard_map/slice | solution.py:279
  142.5 3.2 %collective-permute-start.35 = (bf16[2,128,128]{2,1,0:T(8,128)(2,1)S(1)}, bf16[2,128,128]{2,1,0:T(8,128)(2,1)S(1)}, u32[]{:S(2)}, u32[]{:S(2)}) collective-permute-start(bf16[2,128,128]{2,1,0:T(8,128)(2,1)S(1)} %get-tuple-element.61), channel_id=1, source_target_pairs={{0,32},{8,40},{16,48},{24,56},{32,0},{40,8},{48,16},{56,24},{64,96... | collective-permute-start | bytes 196616 | tf_op jit(solution)/shard_map/ppermute | solution.py:188
  146.5 2.5 %collective-permute-start.37 = (bf16[2,128,128]{2,1,0:T(8,128)(2,1)S(1)}, bf16[2,128,128]{2,1,0:T(8,128)(2,1)S(1)}, u32[]{:S(2)}, u32[]{:S(2)}) collective-permute-start(bf16[2,128,128]{2,1,0:T(8,128)(2,1)S(1)} %get-tuple-element.62), channel_id=1, source_target_pairs={{0,48},{8,56},{16,0},{24,8},{32,16},{40,24},{48,32},{56,40},{64,11... | collective-permute-start | bytes 196616 | tf_op jit(solution)/shard_map/ppermute | solution.py:188
  149.8 2.2 %collective-permute-start.43 = (bf16[2,128,128]{2,1,0:T(8,128)(2,1)S(1)}, bf16[2,128,128]{2,1,0:T(8,128)(2,1)S(1)}, u32[]{:S(2)}, u32[]{:S(2)}) collective-permute-start(bf16[2,128,128]{2,1,0:T(8,128)(2,1)S(1)} %get-tuple-element.66), channel_id=1, source_target_pairs={{0,64},{8,72},{16,80},{24,88},{32,96},{40,104},{48,112},{56,120},{... | collective-permute-start | bytes 196616 | tf_op jit(solution)/shard_map/ppermute | solution.py:188
  152.2 2.8 %collective-permute-done.42 = bf16[2,128,128]{2,1,0:T(8,128)(2,1)S(1)} collective-permute-done((bf16[2,128,128]{2,1,0:T(8,128)(2,1)S(1)}, bf16[2,128,128]{2,1,0:T(8,128)(2,1)S(1)}, u32[]{:S(2)}, u32[]{:S(2)}) %collective-permute-start.42) | collective-permute-done | bytes 65568 | tf_op jit(solution)/shard_map/ppermute | solution.py:188
  155.0 2.6 %collective-permute-done.44 = bf16[2,128,128]{2,1,0:T(8,128)(2,1)S(1)} collective-permute-done((bf16[2,128,128]{2,1,0:T(8,128)(2,1)S(1)}, bf16[2,128,128]{2,1,0:T(8,128)(2,1)S(1)}, u32[]{:S(2)}, u32[]{:S(2)}) %collective-permute-start.44) | collective-permute-done | bytes 65568 | tf_op jit(solution)/shard_map/ppermute | solution.py:188
  (158 shorter events, 37.6 us)
Async XLA Ops:
  0.0 18.1 %collective-permute-start = (bf16[256,1024]{1,0:T(8,128)(2,1)}, bf16[256,1024]{1,0:T(8,128)(2,1)}, u32[]{:S(2)}, u32[]{:S(2)}) collective-permute-start(bf16[256,1024]{1,0:T(8,128)(2,1)} %refs_1_.1), channel_id=1, source_target_pairs={{0,1},{1,2},{2,3},{3,4},{4,5},{5,6},{6,7},{7,0},{8,9},{9,10},{10,1... | collective-permute-start | bytes 1572872 | tf_op jit(solution)/shard_map/ppermute | solution.py:274
  1.9 16.2 %collective-permute-start.2 = (bf16[256,1024]{1,0:T(8,128)(2,1)}, bf16[256,1024]{1,0:T(8,128)(2,1)S(1)}, u32[]{:S(2)}, u32[]{:S(2)}) collective-permute-start(bf16[256,1024]{1,0:T(8,128)(2,1)} %refs_3_.1), channel_id=1, source_target_pairs={{0,7},{1,0},{2,1},{3,2},{4,3},{5,4},{6,5},{7,6},{8,15},{9,8},{10,9... | collective-permute-start | bytes 1572872 | tf_op jit(solution)/shard_map/ppermute | solution.py:275
  18.1 14.5 %collective-permute-start.1 = (bf16[256,1024]{1,0:T(8,128)(2,1)}, bf16[256,1024]{1,0:T(8,128)(2,1)S(1)}, u32[]{:S(2)}, u32[]{:S(2)}) collective-permute-start(bf16[256,1024]{1,0:T(8,128)(2,1)} %collective-permute-done.refs_5_), channel_id=1, source_target_pairs={{0,1},{1,2},{2,3},{3,4},{4,5},{5,6},{6,7},{7,0},{8,9},{9,10},{10,1... | collective-permute-start | bytes 1572872 | tf_op jit(solution)/shard_map/ppermute | solution.py:274
  18.1 14.5 %collective-permute-start.3 = (bf16[256,1024]{1,0:T(8,128)(2,1)S(1)}, bf16[256,1024]{1,0:T(8,128)(2,1)S(1)}, u32[]{:S(2)}, u32[]{:S(2)}) collective-permute-start(bf16[256,1024]{1,0:T(8,128)(2,1)S(1)} %collective-permute-done.2.refs_7_), channel_id=1, source_target_pairs={{0,7},{1,0},{2,1},{3,2},{4,3},{5,4},{6,5},{7,6},{8,15},{9,8},{10,9... | collective-permute-start | bytes 1572872 | tf_op jit(solution)/shard_map/ppermute | solution.py:275
  34.2 30.5 %collective-permute-start.8 = (bf16[42,256,128]{2,1,0:T(8,128)(2,1)}, bf16[42,256,128]{2,1,0:T(8,128)(2,1)S(1)}, u32[]{:S(2)}, u32[]{:S(2)}) collective-permute-start(bf16[42,256,128]{2,1,0:T(8,128)(2,1)} %bitcast.71), channel_id=1, source_target_pairs={{0,8},{8,0},{16,24},{24,16},{32,40},{40,32},{48,56},{56,48},{64,72... | collective-permute-start | bytes 8257544 | tf_op jit(solution)/shard_map/ppermute | solution.py:188
  34.7 15.3 %collective-permute-start.4 = (bf16[256,1024]{1,0:T(8,128)(2,1)}, bf16[256,1024]{1,0:T(8,128)(2,1)S(1)}, u32[]{:S(2)}, u32[]{:S(2)}) collective-permute-start(bf16[256,1024]{1,0:T(8,128)(2,1)} %copy-done.16), channel_id=1, source_target_pairs={{0,1},{1,2},{2,3},{3,4},{4,5},{5,6},{6,7},{7,0},{8,9},{9,10},{10,1... | collective-permute-start | bytes 1572872 | tf_op jit(solution)/shard_map/ppermute | solution.py:274
  34.7 15.3 %collective-permute-start.6 = (bf16[256,1024]{1,0:T(8,128)(2,1)}, bf16[256,1024]{1,0:T(8,128)(2,1)S(1)}, u32[]{:S(2)}, u32[]{:S(2)}) collective-permute-start(bf16[256,1024]{1,0:T(8,128)(2,1)} %copy-done.17), channel_id=1, source_target_pairs={{0,7},{1,0},{2,1},{3,2},{4,3},{5,4},{6,5},{7,6},{8,15},{9,8},{10,9... | collective-permute-start | bytes 1572872 | tf_op jit(solution)/shard_map/ppermute | solution.py:275
  38.0 15.3 %collective-permute-start.12 = (bf16[256,1024]{1,0:T(8,128)(2,1)}, bf16[256,1024]{1,0:T(8,128)(2,1)S(1)}, u32[]{:S(2)}, u32[]{:S(2)}) collective-permute-start(bf16[256,1024]{1,0:T(8,128)(2,1)} %refs_3_.1), channel_id=1, source_target_pairs={{0,8},{8,0},{16,24},{24,16},{32,40},{40,32},{48,56},{56,48},{64,72... | collective-permute-start | bytes 1572872 | tf_op jit(solution)/shard_map/ppermute | solution.py:188
  40.5 12.8 %collective-permute-start.13 = (bf16[256,1024]{1,0:T(8,128)(2,1)}, bf16[256,1024]{1,0:T(8,128)(2,1)S(1)}, u32[]{:S(2)}, u32[]{:S(2)}) collective-permute-start(bf16[256,1024]{1,0:T(8,128)(2,1)} %collective-permute-done.refs_5_), channel_id=1, source_target_pairs={{0,8},{8,0},{16,24},{24,16},{32,40},{40,32},{48,56},{56,48},{64,72... | collective-permute-start | bytes 1572872 | tf_op jit(solution)/shard_map/ppermute | solution.py:188
  50.0 14.2 %collective-permute-start.5 = (bf16[256,1024]{1,0:T(8,128)(2,1)S(1)}, bf16[256,1024]{1,0:T(8,128)(2,1)S(1)}, u32[]{:S(2)}, u32[]{:S(2)}) collective-permute-start(bf16[256,1024]{1,0:T(8,128)(2,1)S(1)} %collective-permute-done.4.refs_13_), channel_id=1, source_target_pairs={{0,1},{1,2},{2,3},{3,4},{4,5},{5,6},{6,7},{7,0},{8,9},{9,10},{10,1... | collective-permute-start | bytes 1572872 | tf_op jit(solution)/shard_map/ppermute | solution.py:274
  50.0 14.2 %collective-permute-start.7 = (bf16[256,1024]{1,0:T(8,128)(2,1)S(1)}, bf16[256,1024]{1,0:T(8,128)(2,1)S(1)}, u32[]{:S(2)}, u32[]{:S(2)}) collective-permute-start(bf16[256,1024]{1,0:T(8,128)(2,1)S(1)} %collective-permute-done.6.refs_15_), channel_id=1, source_target_pairs={{0,7},{1,0},{2,1},{3,2},{4,3},{5,4},{6,5},{7,6},{8,15},{9,8},{10,9... | collective-permute-start | bytes 1572872 | tf_op jit(solution)/shard_map/ppermute | solution.py:275
  53.3 14.4 %collective-permute-start.15 = (bf16[256,1024]{1,0:T(8,128)(2,1)}, bf16[256,1024]{1,0:T(8,128)(2,1)S(1)}, u32[]{:S(2)}, u32[]{:S(2)}) collective-permute-start(bf16[256,1024]{1,0:T(8,128)(2,1)} %copy-done.16), channel_id=1, source_target_pairs={{0,8},{8,0},{16,24},{24,16},{32,40},{40,32},{48,56},{56,48},{64,72... | collective-permute-start | bytes 1572872 | tf_op jit(solution)/shard_map/ppermute | solution.py:188
  64.8 15.6 %collective-permute-start.10 = (bf16[256,1024]{1,0:T(8,128)(2,1)S(1)}, bf16[256,1024]{1,0:T(8,128)(2,1)}, u32[]{:S(2)}, u32[]{:S(2)}) collective-permute-start(bf16[256,1024]{1,0:T(8,128)(2,1)S(1)} %collective-permute-done.7.refs_3_), channel_id=1, source_target_pairs={{0,7},{1,0},{2,1},{3,2},{4,3},{5,4},{6,5},{7,6},{8,15},{9,8},{10,9... | collective-permute-start | bytes 1572872 | tf_op jit(solution)/shard_map/ppermute | solution.py:275
  67.7 15.1 %collective-permute-start.9 = (bf16[256,1024]{1,0:T(8,128)(2,1)S(1)}, bf16[256,1024]{1,0:T(8,128)(2,1)}, u32[]{:S(2)}, u32[]{:S(2)}) collective-permute-start(bf16[256,1024]{1,0:T(8,128)(2,1)S(1)} %collective-permute-done.5.refs_1_), channel_id=1, source_target_pairs={{0,1},{1,2},{2,3},{3,4},{4,5},{5,6},{6,7},{7,0},{8,9},{9,10},{10,1... | collective-permute-start | bytes 1572872 | tf_op jit(solution)/shard_map/ppermute | solution.py:274
  67.7 18.8 %collective-permute-start.23 = (bf16[256,1024]{1,0:T(8,128)(2,1)S(1)}, bf16[256,1024]{1,0:T(8,128)(2,1)}, u32[]{:S(2)}, u32[]{:S(2)}) collective-permute-start(bf16[256,1024]{1,0:T(8,128)(2,1)S(1)} %collective-permute-done.5.refs_1_), channel_id=1, source_target_pairs={{0,8},{8,0},{16,24},{24,16},{32,40},{40,32},{48,56},{56,48},{64,72... | collective-permute-start | bytes 1572872 | tf_op jit(solution)/shard_map/ppermute | solution.py:188
  82.8 14.4 %collective-permute-start.19 = (bf16[256,1024]{1,0:T(8,128)(2,1)}, bf16[256,1024]{1,0:T(8,128)(2,1)S(1)}, u32[]{:S(2)}, u32[]{:S(2)}) collective-permute-start(bf16[256,1024]{1,0:T(8,128)(2,1)} %collective-permute-done.9.refs_5_), channel_id=1, source_target_pairs={{0,1},{1,2},{2,3},{3,4},{4,5},{5,6},{6,7},{7,0},{8,9},{9,10},{10,1... | collective-permute-start | bytes 1572872 | tf_op jit(solution)/shard_map/ppermute | solution.py:274
  82.8 14.4 %collective-permute-start.21 = (bf16[256,1024]{1,0:T(8,128)(2,1)}, bf16[256,1024]{1,0:T(8,128)(2,1)S(1)}, u32[]{:S(2)}, u32[]{:S(2)}) collective-permute-start(bf16[256,1024]{1,0:T(8,128)(2,1)} %collective-permute-done.10.refs_7_), channel_id=1, source_target_pairs={{0,7},{1,0},{2,1},{3,2},{4,3},{5,4},{6,5},{7,6},{8,15},{9,8},{10,9... | collective-permute-start | bytes 1572872 | tf_op jit(solution)/shard_map/ppermute | solution.py:275
  86.1 11.7 %collective-permute-start.24 = (bf16[256,1024]{1,0:T(8,128)(2,1)S(1)}, bf16[256,1024]{1,0:T(8,128)(2,1)S(1)}, u32[]{:S(2)}, u32[]{:S(2)}) collective-permute-start(bf16[256,1024]{1,0:T(8,128)(2,1)S(1)} %collective-permute-done.7.refs_3_), channel_id=1, source_target_pairs={{0,8},{8,0},{16,24},{24,16},{32,40},{40,32},{48,56},{56,48},{64,72... | collective-permute-start | bytes 1572872 | tf_op jit(solution)/shard_map/ppermute | solution.py:188
  86.1 11.7 %collective-permute-start.25 = (bf16[256,1024]{1,0:T(8,128)(2,1)}, bf16[256,1024]{1,0:T(8,128)(2,1)S(1)}, u32[]{:S(2)}, u32[]{:S(2)}) collective-permute-start(bf16[256,1024]{1,0:T(8,128)(2,1)} %collective-permute-done.9.refs_5_), channel_id=1, source_target_pairs={{0,8},{8,0},{16,24},{24,16},{32,40},{40,32},{48,56},{56,48},{64,72... | collective-permute-start | bytes 1572872 | tf_op jit(solution)/shard_map/ppermute | solution.py:188
  86.6 14.4 %collective-permute-start.26 = (bf16[256,1024]{1,0:T(8,128)(2,1)}, bf16[256,1024]{1,0:T(8,128)(2,1)S(1)}, u32[]{:S(2)}, u32[]{:S(2)}) collective-permute-start(bf16[256,1024]{1,0:T(8,128)(2,1)} %collective-permute-done.10.refs_7_), channel_id=1, source_target_pairs={{0,8},{8,0},{16,24},{24,16},{32,40},{40,32},{48,56},{56,48},{64,72... | collective-permute-start | bytes 1572872 | tf_op jit(solution)/shard_map/ppermute | solution.py:188
  97.7 15.1 %collective-permute-start.20 = (bf16[256,1024]{1,0:T(8,128)(2,1)S(1)}, bf16[256,1024]{1,0:T(8,128)(2,1)S(1)}, u32[]{:S(2)}, u32[]{:S(2)}) collective-permute-start(bf16[256,1024]{1,0:T(8,128)(2,1)S(1)} %collective-permute-done.19.refs_9_), channel_id=1, source_target_pairs={{0,1},{1,2},{2,3},{3,4},{4,5},{5,6},{6,7},{7,0},{8,9},{9,10},{10,1... | collective-permute-start | bytes 1572872 | tf_op jit(solution)/shard_map/ppermute | solution.py:274
  97.8 15.1 %collective-permute-start.22 = (bf16[256,1024]{1,0:T(8,128)(2,1)S(1)}, bf16[256,1024]{1,0:T(8,128)(2,1)S(1)}, u32[]{:S(2)}, u32[]{:S(2)}) collective-permute-start(bf16[256,1024]{1,0:T(8,128)(2,1)S(1)} %collective-permute-done.21.refs_11_), channel_id=1, source_target_pairs={{0,7},{1,0},{2,1},{3,2},{4,3},{5,4},{6,5},{7,6},{8,15},{9,8},{10,9... | collective-permute-start | bytes 1572872 | tf_op jit(solution)/shard_map/ppermute | solution.py:275
  135.7 13.3 %collective-permute-start.39 = (bf16[4,2,128,128]{3,2,1,0:T(8,128)(2,1)S(1)}, bf16[4,2,128,128]{3,2,1,0:T(8,128)(2,1)S(1)}, u32[]{:S(2)}, u32[]{:S(2)}) collective-permute-start(bf16[4,2,128,128]{3,2,1,0:T(8,128)(2,1)S(1)} %pad_maximum_fusion.2), channel_id=1, source_target_pairs={{0,16},{8,24},{16,32},{24,40},{32,48},{40,56},{48,0},{56,8},{64,80... | collective-permute-start | bytes 786440 | tf_op jit(solution)/shard_map/ppermute | solution.py:188
  137.4 11.6 %collective-permute-start.41 = (bf16[4,2,128,128]{3,2,1,0:T(8,128)(2,1)S(1)}, bf16[4,2,128,128]{3,2,1,0:T(8,128)(2,1)S(1)}, u32[]{:S(2)}, u32[]{:S(2)}) collective-permute-start(bf16[4,2,128,128]{3,2,1,0:T(8,128)(2,1)S(1)} %pad_maximum_fusion.3), channel_id=1, source_target_pairs={{0,48},{8,56},{16,0},{24,8},{32,16},{40,24},{48,32},{56,40},{64,11... | collective-permute-start | bytes 786440 | tf_op jit(solution)/shard_map/ppermute | solution.py:188
  (48 other events, 322.5 us)

commit v3 on v1

v3 whole, which is shorter than its diff:
```python
import math

import jax
import jax.numpy as jnp
from jax import lax
from jax.experimental import pallas as pl
from jax.experimental.pallas import tpu as pltpu
from jax.sharding import PartitionSpec as P

BS = 128
NX, NY, NC = 4, 4, 2
CAPO = 4
UNROLL = 4
PLACES = NX * NY * NC * CAPO
GROUPS = ((0, 16), (16, 48), (64, 16), (80, 48))
F32, BF16 = jnp.float32, jnp.bfloat16
ANY = pl.BlockSpec(memory_space=pl.ANY)


def gate_kernel(gate_ref, up_ref, grad_ref, out_ref):
    for k in range(out_ref.shape[1]):
        at = (slice(None), pl.ds(k * BS, BS))
        gate = gate_ref[at].astype(F32)
        up = up_ref[at].astype(F32)
        grad = grad_ref[at].astype(F32)
        sig = jax.nn.sigmoid(gate)
        act = gate * sig
        out_ref[0, k] = (grad * up * sig * (1.0 + gate * (1.0 - sig))).astype(BF16)
        out_ref[1, k] = (grad * act).astype(BF16)
        out_ref[2, k] = (act * up).astype(BF16)


def hidden_blocks(gate_pre, up_pre, hidden_grad):
    rows, width = gate_pre.shape
    blocks = width // BS
    each = blocks // 2
    spec = pl.BlockSpec((rows, each * BS), lambda i: (0, i))
    out = pl.pallas_call(
        gate_kernel,
        grid=(blocks // each,),
        in_specs=[spec] * 3,
        out_specs=pl.BlockSpec((3, each, rows, BS), lambda i: (0, i, 0, 0)),
        out_shape=jax.ShapeDtypeStruct((3, blocks, rows, BS), BF16),
        cost_estimate=pl.CostEstimate(flops=0, bytes_accessed=12 * rows * width * 2, transcendentals=0),
        compiler_params=pltpu.CompilerParams(vmem_limit_bytes=16 * 2**20),
        name="gate_blocks",
    )(gate_pre, up_pre, hidden_grad)
    return out.reshape(3 * blocks, rows, BS)


def tile_kernel(first, last, per, n_hid, scale, tab_ref, *refs):
    n_chunk = 2 * (last - first)
    chunks, hid_ref = refs[:n_chunk], refs[n_chunk]
    outs, (blk, stage, stage16, in_sems, out_sems) = refs[-9:-5], refs[-5:]
    copies = []
    for i, chunk in enumerate(chunks):
        for k in range(per):
            copies.append((chunk.at[:, pl.ds(k * BS, BS)], blk.at[i * per + k]))
    n_feat = n_chunk * per
    copies.append((hid_ref, blk.at[pl.ds(n_feat, n_hid)]))
    copies = [pltpu.make_async_copy(a, b, in_sems.at[i]) for i, (a, b) in enumerate(copies)]
    for copy in copies:
        copy.start()

    for copy in copies:
        copy.wait()

    for g, (base, size) in enumerate(GROUPS):
        begin, end = tab_ref[PLACES + g * 16 + first], tab_ref[PLACES + g * 16 + last]
        held = stage16 if outs[g].dtype == BF16 else stage

        def tile(i):
            entry = tab_ref[jnp.minimum(i, end - 1)] // PLACES
            hid = n_feat + entry % 64
            feat = (entry // 64) % 8
            step = (entry // 512) % 8
            down = entry // 4096
            feat = ((step - first) * 2 + down) * per + feat
            left = blk[jnp.where(down == 1, hid, feat)]
            right = blk[jnp.where(down == 1, feat, hid)]
            out = lax.dot_general(
                left, right, (((0,), (0,)), ((), ())), preferred_element_type=F32
            )
            return (out * scale).astype(held.dtype)

        def put(n, k):
            i = begin + n * UNROLL + k
            at = (n % 2) * UNROLL + k
            entry = tab_ref[jnp.minimum(i, end - 1)]
            return pltpu.make_async_copy(
                held.at[at], outs[g].at[entry % PLACES - base], out_sems.at[at]
            )

        rounds = (end - begin + UNROLL - 1) // UNROLL

        def body(n, carry):
            @pl.when(n >= 2)
            def _():
                for k in range(UNROLL):
                    put(n - 2, k).wait()

            made = [tile(begin + n * UNROLL + k) for k in range(UNROLL)]
            for k in range(UNROLL):
                held[(n % 2) * UNROLL + k] = made[k]
            for k in range(UNROLL):

                @pl.when(begin + n * UNROLL + k < end)
                def _():
                    put(n, k).start()

            return carry

        lax.fori_loop(0, rounds, body, 0)

        @pl.when(rounds >= 2)
        def _():
            for k in range(UNROLL):
                put(rounds - 2, k).wait()

        for k in range(UNROLL):

            @pl.when((rounds >= 1) & (begin + (rounds - 1) * UNROLL + k < end))
            def _():
                put(rounds - 1, k).wait()


def make_tiles(first, last, table, chunks, hid, before, scale):
    rows, width = chunks[0].shape
    per = width // BS
    n_hid = hid.shape[0]
    blocks = len(chunks) * per + n_hid
    operands = (table, *chunks, hid, *before)
    at = len(operands) - len(before)

    def body(*refs):
        tile_kernel(first, last, per, n_hid, scale, *refs)

    return pl.pallas_call(
        body,
        in_specs=[pl.BlockSpec(memory_space=pltpu.SMEM)] + [ANY] * (len(operands) - 1),
        out_specs=[ANY] * len(GROUPS),
        out_shape=[jax.ShapeDtypeStruct(b.shape, b.dtype) for b in before],
        scratch_shapes=[
            pltpu.VMEM((blocks, rows, BS), BF16),
            pltpu.VMEM((2 * UNROLL, BS, BS), F32),
            pltpu.VMEM((2 * UNROLL, BS, BS), BF16),
            pltpu.SemaphoreType.DMA((len(chunks) * per + 1,)),
            pltpu.SemaphoreType.DMA((2 * UNROLL,)),
        ],
        input_output_aliases={at + g: g for g in range(len(before))},
        cost_estimate=pl.CostEstimate(flops=0, bytes_accessed=10 * 2**20, transcendentals=0),
        compiler_params=pltpu.CompilerParams(vmem_limit_bytes=20 * 2**20),
        name=f"tiles_{first}_{last}",
    )(*operands)


def place():
    me = lax.axis_index("tok")
    return me // (NY * NC), (me // NC) % NY, me % NC


def shift(value, kind, by):
    pairs = []
    for i in range(NX * NY * NC):
        x, y, c = i // (NY * NC), (i // NC) % NY, i % NC
        if kind == "core":
            c = 1 - c
        elif kind == "first":
            x, y = ((x + by) % NX, y) if c == 0 else (x, (y + by) % NY)
        else:
            x, y = (x, y ^ by) if c == 0 else (x ^ by, y)
        pairs.append((i, (x * NY + y) * NC + c))
    return lax.ppermute(value, "tok", pairs)


def slot_order():
    x, y, c = place()
    p = jnp.arange(PLACES, dtype=jnp.int32)
    q = p % 64
    near = (q - 16) // 16
    d1 = jnp.where(q < 16, 2, jnp.where(near == 2, 3, near))
    d2 = (q // CAPO) % 4
    to_c = jnp.where(p < 64, 1 - c, c)
    to_x = jnp.where(to_c == 0, (x + d1) % NX, x ^ d2)
    to_y = jnp.where(to_c == 0, y ^ d2, (y + d1) % NY)
    return ((to_x * NY + to_y) * NC + to_c) * CAPO + p % CAPO


def tile_table(block_hidden, block_feature, block_slot, n_col, per, hid_per):
    col = lax.axis_index("col")
    matrix = jnp.arange(3, dtype=jnp.int32)[:, None]
    source = block_feature // per
    down = (matrix == 2).astype(jnp.int32)
    step = jnp.where(down == 1, source - col, col - source) % n_col
    hid = matrix * hid_per + block_hidden % hid_per
    value = 1 + (((down * 8 + step) * 8 + block_feature % per) * 64 + hid)
    value = jnp.where(block_hidden // hid_per == col, value, 0).reshape(-1)
    hit = slot_order()[:, None] == block_slot.reshape(-1)[None, :]
    code = jnp.sum(jnp.where(hit, value[None, :], 0), axis=1)
    p = jnp.arange(PLACES, dtype=jnp.int32)
    group = (p >= 16).astype(jnp.int32) + (p >= 64) + (p >= 80)
    entry = jnp.where(code > 0, (code - 1) * PLACES + p, p)
    came = jnp.where(code > 0, ((code - 1) // 512) % 8, 8)
    key = (group * 16 + came) * PLACES + p
    rank = jnp.sum((key[None, :] < key[:, None]).astype(jnp.int32), axis=1)
    ordered = jnp.sum(jnp.where(rank[None, :] == p[:, None], entry[None, :], 0), axis=1)
    bounds = jnp.arange(16 * len(GROUPS), dtype=jnp.int32) * PLACES
    starts = jnp.sum((key[None, :] < bounds[:, None]).astype(jnp.int32), axis=1)
    return jnp.concatenate([ordered, starts])


def reduce_tiles(send_far, send_rest, own_far, own_rest):
    got_far = shift(send_far, "core", 1)
    send_rest, got_far = lax.optimization_barrier((send_rest, got_far))
    got_rest = shift(send_rest, "core", 1)
    far = (own_far + got_far.astype(F32)).astype(BF16)
    from_down = shift(far[:8], "first", 1)
    from_up = shift(far[8:], "first", -1)
    here, up, down = (own_rest + got_rest.astype(F32)).reshape(3, 16, BS, BS)
    own_up = shift(up[8:].astype(BF16), "first", 1)
    own_down = shift(down[:8].astype(BF16), "first", -1)
    low = shift((up[:8] + from_down.astype(F32)).astype(BF16), "first", 1)
    high = shift((down[8:] + from_up.astype(F32)).astype(BF16), "first", -1)
    low = here[:8] + low.astype(F32) + own_down.astype(F32)
    high = here[8:] + high.astype(F32) + own_up.astype(F32)
    total = (*low.reshape(2, CAPO, BS, BS), *high.reshape(2, CAPO, BS, BS))
    out = total[0]
    for k in (2, 1, 3):
        out = out + shift(total[k].astype(BF16), "second", k).astype(F32)
    return out


def on_device(
    features, out_grad, gate_pre, up_pre, hidden_grad, block_hidden, block_feature, block_slot
):
    tok_rows = features.shape[0]
    n_col = lax.axis_size("col")
    scale = 1.0 / math.sqrt(tok_rows * lax.axis_size("tok"))
    forward = [(i, (i + 1) % n_col) for i in range(n_col)]
    back = [(i, (i - 1) % n_col) for i in range(n_col)]
    table = tile_table(
        block_hidden, block_feature, block_slot, n_col, features.shape[1] // BS, gate_pre.shape[1] // BS
    )
    tie = lax.optimization_barrier
    calls = {3: (0, 2), 4: (2, 3), 6: (3, 5), 7: (5, 7)}
    x, y = features, out_grad
    tiles = tuple(
        jnp.zeros((size, BS, BS), BF16 if g < 2 else F32) for g, (base, size) in enumerate(GROUPS)
    )
    chunks = []
    for step in range(n_col):
        if step == 1:
            x, tiles, gates = tie((x, tiles, (gate_pre, up_pre, hidden_grad)))
            hid = hidden_blocks(*gates)
        if step == 2:
            x, y, hid, table = tie((x, y, hid, table))
        if step in calls:
            first, last = calls[step]
            tiles = make_tiles(first, last, table, chunks[2 * first : 2 * last], hid, tiles, scale)
            x, y, tiles = tie((x, y, tiles))
        chunks += [x, y]
        if step < n_col - 1:
            x = lax.ppermute(x, "col", forward)
            y = lax.ppermute(y, "col", back)
    tiles = make_tiles(n_col - 1, n_col, table, chunks[-2:], hid, tiles, scale)
    return reduce_tiles(*tiles)[None]


def solution(mesh):
    in_specs = (P("tok", "col"),) * 5 + (P(), P(), P())
    return jax.shard_map(
        on_device,
        mesh=mesh,
        in_specs=in_specs,
        out_specs=P("col", "tok", None, None),
        check_vma=False,
    )
```

time: 163 us -> 135 us (0.83)
  the two profiles are of different devices: /device:TPU:6 before, /device:TPU:32 now
where the time goes in v3:
time: 135 us; the launch traced here: 132 us
  waiting for transfers between devices  69.9 us (52%)
  starting transfers between devices  32 us (24%)
  Pallas kernels  21.2 us (16%)
  local copies, waits for them, and re-layouts  5.42 us (4%)
  other arithmetic  3.43 us (3%)
    ppermute x7, waiting for transfers between devices, on_device(): x = lax.ppermute(x, 'col', forward)  36.2 us
    pallas_call x5, Pallas kernels, make_tiles(): pl.pallas_call(body, in_specs=[pl.BlockSpec(memory_space=pltpu.SMEM)] + [...  19.6 us
    ppermute x11, waiting for transfers between devices, shift(): return lax.ppermute(value, 'tok', pairs)  19.4 us
    ppermute x7, starting transfers between devices, on_device(): x = lax.ppermute(x, 'col', forward)  14.9 us
    ppermute x7, waiting for transfers between devices, on_device(): y = lax.ppermute(y, 'col', back)  14.3 us
    ppermute x11, starting transfers between devices, shift(): return lax.ppermute(value, 'tok', pairs)  14.2 us
    unnamed x10, local copies, waits for them, and re-layouts  3.54 us
    ppermute x7, starting transfers between devices, on_device(): y = lax.ppermute(y, 'col', back)  2.99 us
  transfers between devices with their start and end apart: 25, of which 18 were waited for; matrix products, arithmetic and copies ran while one was open for 3% of the time, Pallas kernels for 14%

profile of v3, /device:TPU:32, one launch (start us, length us, event | category | flops | bytes accessed | tf_op | source)
XLA Modules:
  0.0 132.3 jit_solution(4258578509778696155)
XLA Ops:
  4.0 9.9 %collective-permute-done.refs_3_ = bf16[256,1024]{1,0:T(8,128)(2,1)S(1)} collective-permute-done((bf16[256,1024]{1,0:T(8,128)(2,1)}, bf16[256,1024]{1,0:T(8,128)(2,1)S(1)}, u32[]{:S(2)}, u32[]{:S(2)}) %collective-permute-start) | collective-permute-done | bytes 524320 | tf_op jit(solution)/shard_map/ppermute | solution.py:263
  23.7 6.1 %collective-permute-done.3.refs_2_ = bf16[256,1024]{1,0:T(8,128)(2,1)S(1)} collective-permute-done((bf16[256,1024]{1,0:T(8,128)(2,1)S(1)}, bf16[256,1024]{1,0:T(8,128)(2,1)S(1)}, u32[]{:S(2)}, u32[]{:S(2)}) %collective-permute-start.3) | collective-permute-done | bytes 524320 | tf_op jit(solution)/shard_map/ppermute | solution.py:264
  29.9 3.0 %collective-permute-start.4 = (bf16[256,1024]{1,0:T(8,128)(2,1)S(1)}, bf16[256,1024]{1,0:T(8,128)(2,1)S(1)}, u32[]{:S(2)}, u32[]{:S(2)}) collective-permute-start(bf16[256,1024]{1,0:T(8,128)(2,1)S(1)} %collective-permute-done.1.refs_1_), channel_id=1, source_target_pairs={{0,1},{1,2},{2,3},{3,4},{4,5},{5,6},{6,7},{7,0},{8,9},{9,10},{10,1... | collective-permute-start | bytes 1572872 | tf_op jit(solution)/shard_map/ppermute | solution.py:263
  33.9 5.3 %tiles_0_2.1 = (bf16[16,128,128]{2,1,0:T(8,128)(2,1)S(1)}, bf16[48,128,128]{2,1,0:T(8,128)(2,1)S(1)}, f32[16,128,128]{2,1,0:T(8,128)S(1)}, f32[48,128,128]{2,1,0:T(8,128)S(1)}) custom-call(s32[192]{0:T(256)S(1)} %pad_add_fusion.refs_0_, bf16[256,1024]{1,0:T(8,128)(2,1)S(1)} %copy-done.3, ...), custom_call_target="tpu_custom_call", output_to_operand_aliasing={{0}: (6, {}), {1}: (7, {}), {2}: (8, {}), {3}: (9, {})} | custom-call | bytes 10485760 | tf_op jit(solution)/shard_map/tiles_0_2/pallas_call | solution.py:138
  39.2 3.6 %collective-permute-done.4.refs_1_ = bf16[256,1024]{1,0:T(8,128)(2,1)S(1)} collective-permute-done((bf16[256,1024]{1,0:T(8,128)(2,1)S(1)}, bf16[256,1024]{1,0:T(8,128)(2,1)S(1)}, u32[]{:S(2)}, u32[]{:S(2)}) %collective-permute-start.4) | collective-permute-done | bytes 524320 | tf_op jit(solution)/shard_map/ppermute | solution.py:263
  42.9 2.6 %collective-permute-done.5.refs_2_ = bf16[256,1024]{1,0:T(8,128)(2,1)S(1)} collective-permute-done((bf16[256,1024]{1,0:T(8,128)(2,1)S(1)}, bf16[256,1024]{1,0:T(8,128)(2,1)S(1)}, u32[]{:S(2)}, u32[]{:S(2)}) %collective-permute-start.5) | collective-permute-done | bytes 524320 | tf_op jit(solution)/shard_map/ppermute | solution.py:264
  47.5 3.7 %tiles_2_3.1 = (bf16[16,128,128]{2,1,0:T(8,128)(2,1)S(1)}, bf16[48,128,128]{2,1,0:T(8,128)(2,1)S(1)}, f32[16,128,128]{2,1,0:T(8,128)S(1)}, f32[48,128,128]{2,1,0:T(8,128)S(1)}) custom-call(s32[192]{0:T(256)S(1)} %pad_add_fusion.refs_0_, ...), custom_call_target="tpu_custom_call", output_to_operand_aliasing={{0}: (4, {}), {1}: (5, {}), {2}: (6, {}), {3}: (7, {})} | custom-call | bytes 10485760 | tf_op jit(solution)/shard_map/tiles_2_3/pallas_call | solution.py:138
  51.1 5.3 %collective-permute-done.6.refs_3_ = bf16[256,1024]{1,0:T(8,128)(2,1)S(1)} collective-permute-done((bf16[256,1024]{1,0:T(8,128)(2,1)S(1)}, bf16[256,1024]{1,0:T(8,128)(2,1)S(1)}, u32[]{:S(2)}, u32[]{:S(2)}) %collective-permute-start.6) | collective-permute-done | bytes 524320 | tf_op jit(solution)/shard_map/ppermute | solution.py:263
  59.5 9.3 %collective-permute-done.8.refs_1_ = bf16[256,1024]{1,0:T(8,128)(2,1)S(1)} collective-permute-done((bf16[256,1024]{1,0:T(8,128)(2,1)S(1)}, bf16[256,1024]{1,0:T(8,128)(2,1)S(1)}, u32[]{:S(2)}, u32[]{:S(2)}) %collective-permute-start.8) | collective-permute-done | bytes 524320 | tf_op jit(solution)/shard_map/ppermute | solution.py:263
  68.9 2.5 %collective-permute-start.9 = (bf16[256,1024]{1,0:T(8,128)(2,1)S(1)}, bf16[256,1024]{1,0:T(8,128)(2,1)S(1)}, u32[]{:S(2)}, u32[]{:S(2)}) collective-permute-start(bf16[256,1024]{1,0:T(8,128)(2,1)S(1)} %collective-permute-done.8.refs_1_), channel_id=1, source_target_pairs={{0,1},{1,2},{2,3},{3,4},{4,5},{5,6},{6,7},{7,0},{8,9},{9,10},{10,1... | collective-permute-start | bytes 1572872 | tf_op jit(solution)/shard_map/ppermute | solution.py:263
  71.3 3.5 %tiles_3_5.1 = (bf16[16,128,128]{2,1,0:T(8,128)(2,1)S(1)}, bf16[48,128,128]{2,1,0:T(8,128)(2,1)S(1)}, f32[16,128,128]{2,1,0:T(8,128)S(1)}, f32[48,128,128]{2,1,0:T(8,128)S(1)}) custom-call(s32[192]{0:T(256)S(1)} %pad_add_fusion.refs_0_, ...), custom_call_target="tpu_custom_call", output_to_operand_aliasing={{0}: (6, {}), {1}: (7, {}), {2}: (8, {}), {3}: (9, {})} | custom-call | bytes 10485760 | tf_op jit(solution)/shard_map/tiles_3_5/pallas_call | solution.py:138
  74.9 5.1 %collective-permute-done.9.refs_3_ = bf16[256,1024]{1,0:T(8,128)(2,1)S(1)} collective-permute-done((bf16[256,1024]{1,0:T(8,128)(2,1)S(1)}, bf16[256,1024]{1,0:T(8,128)(2,1)S(1)}, u32[]{:S(2)}, u32[]{:S(2)}) %collective-permute-start.9) | collective-permute-done | bytes 524320 | tf_op jit(solution)/shard_map/ppermute | solution.py:263
  80.0 2.5 %collective-permute-done.11.refs_4_ = bf16[256,1024]{1,0:T(8,128)(2,1)S(1)} collective-permute-done((bf16[256,1024]{1,0:T(8,128)(2,1)S(1)}, bf16[256,1024]{1,0:T(8,128)(2,1)S(1)}, u32[]{:S(2)}, u32[]{:S(2)}) %collective-permute-start.11) | collective-permute-done | bytes 524320 | tf_op jit(solution)/shard_map/ppermute | solution.py:264
  84.5 4.3 %tiles_5_7.1 = (bf16[16,128,128]{2,1,0:T(8,128)(2,1)S(1)}, bf16[48,128,128]{2,1,0:T(8,128)(2,1)S(1)}, f32[16,128,128]{2,1,0:T(8,128)S(1)}, f32[48,128,128]{2,1,0:T(8,128)S(1)}) custom-call(s32[192]{0:T(256)S(1)} %pad_add_fusion.refs_0_, ...), custom_call_target="tpu_custom_call", output_to_operand_aliasing={{0}: (6, {}), {1}: (7, {}), {2}: (8, {}), {3}: (9, {})} | custom-call | bytes 10485760 | tf_op jit(solution)/shard_map/tiles_5_7/pallas_call | solution.py:138
  88.8 2.9 %collective-permute-done.12.refs_1_ = bf16[256,1024]{1,0:T(8,128)(2,1)S(1)} collective-permute-done((bf16[256,1024]{1,0:T(8,128)(2,1)S(1)}, bf16[256,1024]{1,0:T(8,128)(2,1)S(1)}, u32[]{:S(2)}, u32[]{:S(2)}) %collective-permute-start.12) | collective-permute-done | bytes 524320 | tf_op jit(solution)/shard_map/ppermute | solution.py:263
  93.7 2.9 %tiles_7_8.1 = (bf16[16,128,128]{2,1,0:T(8,128)(2,1)S(1)}, bf16[48,128,128]{2,1,0:T(8,128)(2,1)S(1)}, f32[16,128,128]{2,1,0:T(8,128)S(1)}, f32[48,128,128]{2,1,0:T(8,128)S(1)}) custom-call(s32[192]{0:T(256)S(1)} %pad_add_fusion.refs_0_, ...), custom_call_target="tpu_custom_call", output_to_operand_aliasing={{0}: (4, {}), {1}: (5, {}), {2}: (6, {}), {3}: (7, {})} | custom-call | bytes 10485760 | tf_op jit(solution)/shard_map/tiles_7_8/pallas_call | solution.py:138
  98.9 2.5 %collective-permute-start.19 = (bf16[8,128,128]{2,1,0:T(8,128)(2,1)S(1)}, bf16[8,128,128]{2,1,0:T(8,128)(2,1)S(1)}, u32[]{:S(2)}, u32[]{:S(2)}) collective-permute-start(bf16[8,128,128]{2,1,0:T(8,128)(2,1)S(1)} %get-tuple-element.127), channel_id=1, source_target_pairs={{0,192},{8,56},{16,208},{24,8},{32,224},{40,24},{48,240},{56,40},{... | collective-permute-start | bytes 786440 | tf_op jit(solution)/shard_map/ppermute | solution.py:173
  102.7 2.6 %collective-permute-done.19 = bf16[8,128,128]{2,1,0:T(8,128)(2,1)S(1)} collective-permute-done((bf16[8,128,128]{2,1,0:T(8,128)(2,1)S(1)}, bf16[8,128,128]{2,1,0:T(8,128)(2,1)S(1)}, u32[]{:S(2)}, u32[]{:S(2)}) %collective-permute-start.19) | collective-permute-done | bytes 262176 | tf_op jit(solution)/shard_map/ppermute | solution.py:173
  105.4 3.7 %collective-permute-start.20 = (bf16[8,128,128]{2,1,0:T(8,128)(2,1)S(1)}, bf16[8,128,128]{2,1,0:T(8,128)(2,1)S(1)}, u32[]{:S(2)}, u32[]{:S(2)}) collective-permute-start(bf16[8,128,128]{2,1,0:T(8,128)(2,1)S(1)} %fusion), channel_id=1, source_target_pairs={{0,192},{8,56},{16,208},{24,8},{32,224},{40,24},{48,240},{56,40},{... | collective-permute-start | bytes 786440 | tf_op jit(solution)/shard_map/ppermute | solution.py:173
  109.1 3.2 %collective-permute-start.18 = (bf16[8,128,128]{2,1,0:T(8,128)(2,1)S(1)}, bf16[8,128,128]{2,1,0:T(8,128)(2,1)S(1)}, u32[]{:S(2)}, u32[]{:S(2)}) collective-permute-start(bf16[8,128,128]{2,1,0:T(8,128)(2,1)S(1)} %get-tuple-element.126), channel_id=1, source_target_pairs={{0,192},{8,56},{16,208},{24,8},{32,224},{40,24},{48,240},{56,40},{... | collective-permute-start | bytes 786440 | tf_op jit(solution)/shard_map/ppermute | solution.py:173
  113.0 3.7 %collective-permute-done.21 = bf16[8,128,128]{2,1,0:T(8,128)(2,1)S(1)} collective-permute-done((bf16[8,128,128]{2,1,0:T(8,128)(2,1)S(1)}, bf16[8,128,128]{2,1,0:T(8,128)(2,1)S(1)}, u32[]{:S(2)}, u32[]{:S(2)}) %collective-permute-start.21) | collective-permute-done | bytes 262176 | tf_op jit(solution)/shard_map/ppermute | solution.py:173
  117.0 3.3 %collective-permute-start.22 = (bf16[4,128,128]{2,1,0:T(8,128)(2,1)S(1)}, bf16[4,128,128]{2,1,0:T(8,128)(2,1)S(1)}, u32[]{:S(2)}, u32[]{:S(2)}) collective-permute-start(bf16[4,128,128]{2,1,0:T(8,128)(2,1)S(1)} %get-tuple-element.129), channel_id=1, source_target_pairs={{0,32},{8,136},{16,48},{24,152},{32,0},{40,168},{48,16},{56,184},{... | collective-permute-start | bytes 393224 | tf_op jit(solution)/shard_map/ppermute | solution.py:173
  121.3 5.0 %collective-permute-done.17 = bf16[8,128,128]{2,1,0:T(8,128)(2,1)S(1)} collective-permute-done((bf16[8,128,128]{2,1,0:T(8,128)(2,1)S(1)}, bf16[8,128,128]{2,1,0:T(8,128)(2,1)S(1)}, u32[]{:S(2)}, u32[]{:S(2)}) %collective-permute-start.17) | collective-permute-done | bytes 262176 | tf_op jit(solution)/shard_map/ppermute | solution.py:173
  126.6 4.9 %collective-permute-done.23 = bf16[4,128,128]{2,1,0:T(8,128)(2,1)S(1)} collective-permute-done((bf16[4,128,128]{2,1,0:T(8,128)(2,1)S(1)}, bf16[4,128,128]{2,1,0:T(8,128)(2,1)S(1)}, u32[]{:S(2)}, u32[]{:S(2)}) %collective-permute-start.23) | collective-permute-done | bytes 131104 | tf_op jit(solution)/shard_map/ppermute | solution.py:173
  (69 shorter events, 30.5 us)
Async XLA Ops:
  0.0 13.9 %collective-permute-start = (bf16[256,1024]{1,0:T(8,128)(2,1)}, bf16[256,1024]{1,0:T(8,128)(2,1)S(1)}, u32[]{:S(2)}, u32[]{:S(2)}) collective-permute-start(bf16[256,1024]{1,0:T(8,128)(2,1)} %refs_1_.1), channel_id=1, source_target_pairs={{0,1},{1,2},{2,3},{3,4},{4,5},{5,6},{6,7},{7,0},{8,9},{9,10},{10,1... | collective-permute-start | bytes 1572872 | tf_op jit(solution)/shard_map/ppermute | solution.py:263
  1.9 13.9 %collective-permute-start.2 = (bf16[256,1024]{1,0:T(8,128)(2,1)}, bf16[256,1024]{1,0:T(8,128)(2,1)S(1)}, u32[]{:S(2)}, u32[]{:S(2)}) collective-permute-start(bf16[256,1024]{1,0:T(8,128)(2,1)} %refs_2_.1), channel_id=1, source_target_pairs={{0,7},{1,0},{2,1},{3,2},{4,3},{5,4},{6,5},{7,6},{8,15},{9,8},{10,9... | collective-permute-start | bytes 1572872 | tf_op jit(solution)/shard_map/ppermute | solution.py:264
  13.9 16.0 %collective-permute-start.1 = (bf16[256,1024]{1,0:T(8,128)(2,1)S(1)}, bf16[256,1024]{1,0:T(8,128)(2,1)S(1)}, u32[]{:S(2)}, u32[]{:S(2)}) collective-permute-start(bf16[256,1024]{1,0:T(8,128)(2,1)S(1)} %collective-permute-done.refs_3_), channel_id=1, source_target_pairs={{0,1},{1,2},{2,3},{3,4},{4,5},{5,6},{6,7},{7,0},{8,9},{9,10},{10,1... | collective-permute-start | bytes 1572872 | tf_op jit(solution)/shard_map/ppermute | solution.py:263
  15.8 14.1 %collective-permute-start.3 = (bf16[256,1024]{1,0:T(8,128)(2,1)S(1)}, bf16[256,1024]{1,0:T(8,128)(2,1)S(1)}, u32[]{:S(2)}, u32[]{:S(2)}) collective-permute-start(bf16[256,1024]{1,0:T(8,128)(2,1)S(1)} %collective-permute-done.2.refs_4_), channel_id=1, source_target_pairs={{0,7},{1,0},{2,1},{3,2},{4,3},{5,4},{6,5},{7,6},{8,15},{9,8},{10,9... | collective-permute-start | bytes 1572872 | tf_op jit(solution)/shard_map/ppermute | solution.py:264
  29.9 13.0 %collective-permute-start.4 = (bf16[256,1024]{1,0:T(8,128)(2,1)S(1)}, bf16[256,1024]{1,0:T(8,128)(2,1)S(1)}, u32[]{:S(2)}, u32[]{:S(2)}) collective-permute-start(bf16[256,1024]{1,0:T(8,128)(2,1)S(1)} %collective-permute-done.1.refs_1_), channel_id=1, source_target_pairs={{0,1},{1,2},{2,3},{3,4},{4,5},{5,6},{6,7},{7,0},{8,9},{9,10},{10,1... | collective-permute-start | bytes 1572872 | tf_op jit(solution)/shard_map/ppermute | solution.py:263
  32.9 12.5 %collective-permute-start.5 = (bf16[256,1024]{1,0:T(8,128)(2,1)S(1)}, bf16[256,1024]{1,0:T(8,128)(2,1)S(1)}, u32[]{:S(2)}, u32[]{:S(2)}) collective-permute-start(bf16[256,1024]{1,0:T(8,128)(2,1)S(1)} %collective-permute-done.3.refs_2_), channel_id=1, source_target_pairs={{0,7},{1,0},{2,1},{3,2},{4,3},{5,4},{6,5},{7,6},{8,15},{9,8},{10,9... | collective-permute-start | bytes 1572872 | tf_op jit(solution)/shard_map/ppermute | solution.py:264
  45.4 11.0 %collective-permute-start.6 = (bf16[256,1024]{1,0:T(8,128)(2,1)S(1)}, bf16[256,1024]{1,0:T(8,128)(2,1)S(1)}, u32[]{:S(2)}, u32[]{:S(2)}) collective-permute-start(bf16[256,1024]{1,0:T(8,128)(2,1)S(1)} %collective-permute-done.4.refs_1_), channel_id=1, source_target_pairs={{0,1},{1,2},{2,3},{3,4},{4,5},{5,6},{6,7},{7,0},{8,9},{9,10},{10,1... | collective-permute-start | bytes 1572872 | tf_op jit(solution)/shard_map/ppermute | solution.py:263
  47.2 10.3 %collective-permute-start.7 = (bf16[256,1024]{1,0:T(8,128)(2,1)S(1)}, bf16[256,1024]{1,0:T(8,128)(2,1)S(1)}, u32[]{:S(2)}, u32[]{:S(2)}) collective-permute-start(bf16[256,1024]{1,0:T(8,128)(2,1)S(1)} %collective-permute-done.5.refs_2_), channel_id=1, source_target_pairs={{0,7},{1,0},{2,1},{3,2},{4,3},{5,4},{6,5},{7,6},{8,15},{9,8},{10,9... | collective-permute-start | bytes 1572872 | tf_op jit(solution)/shard_map/ppermute | solution.py:264
  57.5 11.4 %collective-permute-start.8 = (bf16[256,1024]{1,0:T(8,128)(2,1)S(1)}, bf16[256,1024]{1,0:T(8,128)(2,1)S(1)}, u32[]{:S(2)}, u32[]{:S(2)}) collective-permute-start(bf16[256,1024]{1,0:T(8,128)(2,1)S(1)} %collective-permute-done.6.refs_3_), channel_id=1, source_target_pairs={{0,1},{1,2},{2,3},{3,4},{4,5},{5,6},{6,7},{7,0},{8,9},{9,10},{10,1... | collective-permute-start | bytes 1572872 | tf_op jit(solution)/shard_map/ppermute | solution.py:263
  59.2 12.1 %collective-permute-start.10 = (bf16[256,1024]{1,0:T(8,128)(2,1)S(1)}, bf16[256,1024]{1,0:T(8,128)(2,1)S(1)}, u32[]{:S(2)}, u32[]{:S(2)}) collective-permute-start(bf16[256,1024]{1,0:T(8,128)(2,1)S(1)} %collective-permute-done.7.refs_4_), channel_id=1, source_target_pairs={{0,7},{1,0},{2,1},{3,2},{4,3},{5,4},{6,5},{7,6},{8,15},{9,8},{10,9... | collective-permute-start | bytes 1572872 | tf_op jit(solution)/shard_map/ppermute | solution.py:264
  68.9 11.1 %collective-permute-start.9 = (bf16[256,1024]{1,0:T(8,128)(2,1)S(1)}, bf16[256,1024]{1,0:T(8,128)(2,1)S(1)}, u32[]{:S(2)}, u32[]{:S(2)}) collective-permute-start(bf16[256,1024]{1,0:T(8,128)(2,1)S(1)} %collective-permute-done.8.refs_1_), channel_id=1, source_target_pairs={{0,1},{1,2},{2,3},{3,4},{4,5},{5,6},{6,7},{7,0},{8,9},{9,10},{10,1... | collective-permute-start | bytes 1572872 | tf_op jit(solution)/shard_map/ppermute | solution.py:263
  71.3 11.1 %collective-permute-start.11 = (bf16[256,1024]{1,0:T(8,128)(2,1)S(1)}, bf16[256,1024]{1,0:T(8,128)(2,1)S(1)}, u32[]{:S(2)}, u32[]{:S(2)}) collective-permute-start(bf16[256,1024]{1,0:T(8,128)(2,1)S(1)} %collective-permute-done.10.refs_2_), channel_id=1, source_target_pairs={{0,7},{1,0},{2,1},{3,2},{4,3},{5,4},{6,5},{7,6},{8,15},{9,8},{10,9... | collective-permute-start | bytes 1572872 | tf_op jit(solution)/shard_map/ppermute | solution.py:264
  82.4 9.2 %collective-permute-start.12 = (bf16[256,1024]{1,0:T(8,128)(2,1)S(1)}, bf16[256,1024]{1,0:T(8,128)(2,1)S(1)}, u32[]{:S(2)}, u32[]{:S(2)}) collective-permute-start(bf16[256,1024]{1,0:T(8,128)(2,1)S(1)} %collective-permute-done.9.refs_3_), channel_id=1, source_target_pairs={{0,1},{1,2},{2,3},{3,4},{4,5},{5,6},{6,7},{7,0},{8,9},{9,10},{10,1... | collective-permute-start | bytes 1572872 | tf_op jit(solution)/shard_map/ppermute | solution.py:263
  84.5 9.2 %collective-permute-start.13 = (bf16[256,1024]{1,0:T(8,128)(2,1)S(1)}, bf16[256,1024]{1,0:T(8,128)(2,1)S(1)}, u32[]{:S(2)}, u32[]{:S(2)}) collective-permute-start(bf16[256,1024]{1,0:T(8,128)(2,1)S(1)} %collective-permute-done.11.refs_4_), channel_id=1, source_target_pairs={{0,7},{1,0},{2,1},{3,2},{4,3},{5,4},{6,5},{7,6},{8,15},{9,8},{10,9... | collective-permute-start | bytes 1572872 | tf_op jit(solution)/shard_map/ppermute | solution.py:264
  98.6 3.4 %collective-permute-start.15 = (bf16[48,128,128]{2,1,0:T(8,128)(2,1)S(1)}, bf16[48,128,128]{2,1,0:T(8,128)(2,1)S(1)}, u32[]{:S(2)}, u32[]{:S(2)}) collective-permute-start(bf16[48,128,128]{2,1,0:T(8,128)(2,1)S(1)} %get-tuple-element.118), channel_id=1, source_target_pairs={{0,8},{8,0},{16,24},{24,16},{32,40},{40,32},{48,56},{56,48},{64,72... | collective-permute-start | bytes 4718600 | tf_op jit(solution)/shard_map/ppermute | solution.py:173
  98.9 6.4 %collective-permute-start.19 = (bf16[8,128,128]{2,1,0:T(8,128)(2,1)S(1)}, bf16[8,128,128]{2,1,0:T(8,128)(2,1)S(1)}, u32[]{:S(2)}, u32[]{:S(2)}) collective-permute-start(bf16[8,128,128]{2,1,0:T(8,128)(2,1)S(1)} %get-tuple-element.127), channel_id=1, source_target_pairs={{0,192},{8,56},{16,208},{24,8},{32,224},{40,24},{48,240},{56,40},{... | collective-permute-start | bytes 786440 | tf_op jit(solution)/shard_map/ppermute | solution.py:173
  101.4 11.0 %collective-permute-start.16 = (bf16[8,128,128]{2,1,0:T(8,128)(2,1)S(1)}, bf16[8,128,128]{2,1,0:T(8,128)(2,1)S(1)}, u32[]{:S(2)}, u32[]{:S(2)}) collective-permute-start(bf16[8,128,128]{2,1,0:T(8,128)(2,1)S(1)} %get-tuple-element.128), channel_id=1, source_target_pairs={{0,64},{8,24},{16,80},{24,40},{32,96},{40,56},{48,112},{56,8},{64,... | collective-permute-start | bytes 786440 | tf_op jit(solution)/shard_map/ppermute | solution.py:173
  105.4 7.6 %collective-permute-start.20 = (bf16[8,128,128]{2,1,0:T(8,128)(2,1)S(1)}, bf16[8,128,128]{2,1,0:T(8,128)(2,1)S(1)}, u32[]{:S(2)}, u32[]{:S(2)}) collective-permute-start(bf16[8,128,128]{2,1,0:T(8,128)(2,1)S(1)} %fusion), channel_id=1, source_target_pairs={{0,192},{8,56},{16,208},{24,8},{32,224},{40,24},{48,240},{56,40},{... | collective-permute-start | bytes 786440 | tf_op jit(solution)/shard_map/ppermute | solution.py:173
  109.1 7.6 %collective-permute-start.21 = (bf16[8,128,128]{2,1,0:T(8,128)(2,1)S(1)}, bf16[8,128,128]{2,1,0:T(8,128)(2,1)S(1)}, u32[]{:S(2)}, u32[]{:S(2)}) collective-permute-start(bf16[8,128,128]{2,1,0:T(8,128)(2,1)S(1)} %get-tuple-element.125), channel_id=1, source_target_pairs={{0,64},{8,24},{16,80},{24,40},{32,96},{40,56},{48,112},{56,8},{64,... | collective-permute-start | bytes 786440 | tf_op jit(solution)/shard_map/ppermute | solution.py:173
  109.1 12.2 %collective-permute-start.18 = (bf16[8,128,128]{2,1,0:T(8,128)(2,1)S(1)}, bf16[8,128,128]{2,1,0:T(8,128)(2,1)S(1)}, u32[]{:S(2)}, u32[]{:S(2)}) collective-permute-start(bf16[8,128,128]{2,1,0:T(8,128)(2,1)S(1)} %get-tuple-element.126), channel_id=1, source_target_pairs={{0,192},{8,56},{16,208},{24,8},{32,224},{40,24},{48,240},{56,40},{... | collective-permute-start | bytes 786440 | tf_op jit(solution)/shard_map/ppermute | solution.py:173
  116.9 9.5 %collective-permute-start.17 = (bf16[8,128,128]{2,1,0:T(8,128)(2,1)S(1)}, bf16[8,128,128]{2,1,0:T(8,128)(2,1)S(1)}, u32[]{:S(2)}, u32[]{:S(2)}) collective-permute-start(bf16[8,128,128]{2,1,0:T(8,128)(2,1)S(1)} %get-tuple-element.124), channel_id=1, source_target_pairs={{0,64},{8,24},{16,80},{24,40},{32,96},{40,56},{48,112},{56,8},{64,... | collective-permute-start | bytes 786440 | tf_op jit(solution)/shard_map/ppermute | solution.py:173
  117.0 9.6 %collective-permute-start.22 = (bf16[4,128,128]{2,1,0:T(8,128)(2,1)S(1)}, bf16[4,128,128]{2,1,0:T(8,128)(2,1)S(1)}, u32[]{:S(2)}, u32[]{:S(2)}) collective-permute-start(bf16[4,128,128]{2,1,0:T(8,128)(2,1)S(1)} %get-tuple-element.129), channel_id=1, source_target_pairs={{0,32},{8,136},{16,48},{24,152},{32,0},{40,168},{48,16},{56,184},{... | collective-permute-start | bytes 393224 | tf_op jit(solution)/shard_map/ppermute | solution.py:173
  120.3 6.3 %collective-permute-start.24 = (bf16[4,128,128]{2,1,0:T(8,128)(2,1)S(1)}, bf16[4,128,128]{2,1,0:T(8,128)(2,1)S(1)}, u32[]{:S(2)}, u32[]{:S(2)}) collective-permute-start(bf16[4,128,128]{2,1,0:T(8,128)(2,1)S(1)} %get-tuple-element.130), channel_id=1, source_target_pairs={{0,48},{8,200},{16,32},{24,216},{32,16},{40,232},{48,0},{56,248},{... | collective-permute-start | bytes 393224 | tf_op jit(solution)/shard_map/ppermute | solution.py:173
  126.5 5.1 %collective-permute-start.23 = (bf16[4,128,128]{2,1,0:T(8,128)(2,1)S(1)}, bf16[4,128,128]{2,1,0:T(8,128)(2,1)S(1)}, u32[]{:S(2)}, u32[]{:S(2)}) collective-permute-start(bf16[4,128,128]{2,1,0:T(8,128)(2,1)S(1)} %unstack.38), channel_id=1, source_target_pairs={{0,16},{8,72},{16,0},{24,88},{32,48},{40,104},{48,32},{56,120},{64... | collective-permute-start | bytes 393224 | tf_op jit(solution)/shard_map/ppermute | solution.py:173
  (6 other events, 13.5 us)

commit v4 on v3

v4 whole, which is shorter than its diff:
```python
import math

import jax
import jax.numpy as jnp
from jax import lax
from jax.experimental import pallas as pl
from jax.experimental.pallas import tpu as pltpu
from jax.sharding import PartitionSpec as P

BS = 128
NX, NY, NC = 4, 4, 2
CAPO = 4
UNROLL = 4
PLACES = NX * NY * NC * CAPO
GROUPS = ((0, 16), (16, 48), (64, 16), (80, 48))
F32, BF16 = jnp.float32, jnp.bfloat16
ANY = pl.BlockSpec(memory_space=pl.ANY)


def gate_kernel(gate_ref, up_ref, grad_ref, out_ref):
    for k in range(out_ref.shape[1]):
        at = (slice(None), pl.ds(k * BS, BS))
        gate = gate_ref[at].astype(F32)
        up = up_ref[at].astype(F32)
        grad = grad_ref[at].astype(F32)
        sig = jax.nn.sigmoid(gate)
        act = gate * sig
        out_ref[0, k] = (grad * up * sig * (1.0 + gate * (1.0 - sig))).astype(BF16)
        out_ref[1, k] = (grad * act).astype(BF16)
        out_ref[2, k] = (act * up).astype(BF16)


def hidden_blocks(gate_pre, up_pre, hidden_grad):
    rows, width = gate_pre.shape
    blocks = width // BS
    each = blocks // 2
    spec = pl.BlockSpec((rows, each * BS), lambda i: (0, i))
    out = pl.pallas_call(
        gate_kernel,
        grid=(blocks // each,),
        in_specs=[spec] * 3,
        out_specs=pl.BlockSpec((3, each, rows, BS), lambda i: (0, i, 0, 0)),
        out_shape=jax.ShapeDtypeStruct((3, blocks, rows, BS), BF16),
        cost_estimate=pl.CostEstimate(flops=0, bytes_accessed=12 * rows * width * 2, transcendentals=0),
        compiler_params=pltpu.CompilerParams(vmem_limit_bytes=16 * 2**20),
        name="gate_blocks",
    )(gate_pre, up_pre, hidden_grad)
    return out.reshape(3 * blocks, rows, BS)


def tile_kernel(segment, scale, tab_ref, chunk_ref, hid_ref, *refs):
    outs, (stage, stage16, sems) = refs[-7:-3], refs[-3:]
    begin, end = tab_ref[PLACES + segment], tab_ref[PLACES + segment + 1]
    rounds = (end - begin + UNROLL - 1) // UNROLL

    def tile(i):
        entry = tab_ref[jnp.minimum(i, end - 1)] // PLACES
        feat = chunk_ref[:, pl.ds(pl.multiple_of((entry // 64) % 8 * BS, BS), BS)]
        hid = hid_ref[entry % 64]
        left, right = (hid, feat) if segment % 2 else (feat, hid)
        out = lax.dot_general(left, right, (((0,), (0,)), ((), ())), preferred_element_type=F32)
        return out * scale

    def each_copy(n, k, act):
        i = begin + n * UNROLL + k
        at = (n % 2) * UNROLL + k
        p = tab_ref[jnp.minimum(i, end - 1)] % PLACES
        for g, (base, size) in enumerate(GROUPS):

            @pl.when((i < end) & (p >= base) & (p < base + size))
            def _():
                held = stage16 if outs[g].dtype == BF16 else stage
                act(pltpu.make_async_copy(held.at[at], outs[g].at[p - base], sems.at[at]))

    def start(copy):
        copy.start()

    def wait(copy):
        copy.wait()

    def body(n, carry):
        @pl.when(n >= 2)
        def _():
            for k in range(UNROLL):
                each_copy(n - 2, k, wait)

        made = [tile(begin + n * UNROLL + k) for k in range(UNROLL)]
        for k in range(UNROLL):
            stage[(n % 2) * UNROLL + k] = made[k]
            stage16[(n % 2) * UNROLL + k] = made[k].astype(BF16)
        for k in range(UNROLL):
            each_copy(n, k, start)
        return carry

    lax.fori_loop(0, rounds, body, 0)
    for back in (2, 1):

        @pl.when(rounds >= back)
        def _():
            for k in range(UNROLL):
                each_copy(rounds - back, k, wait)


def make_tiles(segment, table, chunk, hid, tiles, scale):
    def body(*refs):
        tile_kernel(segment, scale, *refs)

    return pl.pallas_call(
        body,
        in_specs=[
            pl.BlockSpec(memory_space=pltpu.SMEM),
            pl.BlockSpec(memory_space=pltpu.VMEM),
            pl.BlockSpec(memory_space=pltpu.VMEM),
            *[ANY] * len(tiles),
        ],
        out_specs=[ANY] * len(tiles),
        out_shape=[jax.ShapeDtypeStruct(t.shape, t.dtype) for t in tiles],
        scratch_shapes=[
            pltpu.VMEM((2 * UNROLL, BS, BS), F32),
            pltpu.VMEM((2 * UNROLL, BS, BS), BF16),
            pltpu.SemaphoreType.DMA((2 * UNROLL,)),
        ],
        input_output_aliases={3 + g: g for g in range(len(tiles))},
        cost_estimate=pl.CostEstimate(flops=0, bytes_accessed=4 * 2**20, transcendentals=0),
        compiler_params=pltpu.CompilerParams(vmem_limit_bytes=12 * 2**20),
        name=f"tiles_{segment}",
    )(table, chunk, hid, *tiles)


def place():
    me = lax.axis_index("tok")
    return me // (NY * NC), (me // NC) % NY, me % NC


def shift(value, kind, by):
    pairs = []
    for i in range(NX * NY * NC):
        x, y, c = i // (NY * NC), (i // NC) % NY, i % NC
        if kind == "core":
            c = 1 - c
        elif kind == "first":
            x, y = ((x + by) % NX, y) if c == 0 else (x, (y + by) % NY)
        else:
            x, y = (x, y ^ by) if c == 0 else (x ^ by, y)
        pairs.append((i, (x * NY + y) * NC + c))
    return lax.ppermute(value, "tok", pairs)


def slot_order():
    x, y, c = place()
    p = jnp.arange(PLACES, dtype=jnp.int32)
    q = p % 64
    near = (q - 16) // 16
    d1 = jnp.where(q < 16, 2, jnp.where(near == 2, 3, near))
    d2 = (q // CAPO) % 4
    to_c = jnp.where(p < 64, 1 - c, c)
    to_x = jnp.where(to_c == 0, (x + d1) % NX, x ^ d2)
    to_y = jnp.where(to_c == 0, y ^ d2, (y + d1) % NY)
    return ((to_x * NY + to_y) * NC + to_c) * CAPO + p % CAPO


def tile_table(block_hidden, block_feature, block_slot, n_col, per, hid_per):
    col = lax.axis_index("col")
    matrix = jnp.arange(3, dtype=jnp.int32)[:, None]
    down = (matrix == 2).astype(jnp.int32)
    ahead = jnp.where(place()[2] == 0, 1, -1)
    step = (ahead * (col - block_feature // per)) % n_col
    hid = matrix * hid_per + block_hidden % hid_per
    value = 1 + (((step * 2 + down) * 8 + block_feature % per) * 64 + hid)
    value = jnp.where(block_hidden // hid_per == col, value, 0).reshape(-1)
    hit = slot_order()[:, None] == block_slot.reshape(-1)[None, :]
    code = jnp.sum(jnp.where(hit, value[None, :], 0), axis=1)
    p = jnp.arange(PLACES, dtype=jnp.int32)
    entry = jnp.where(code > 0, (code - 1) * PLACES + p, p)
    key = jnp.where(code > 0, (code - 1) // 512, 2 * n_col) * PLACES + p
    rank = jnp.sum((key[None, :] < key[:, None]).astype(jnp.int32), axis=1)
    ordered = jnp.sum(jnp.where(rank[None, :] == p[:, None], entry[None, :], 0), axis=1)
    bounds = jnp.arange(24, dtype=jnp.int32) * PLACES
    starts = jnp.sum((key[None, :] < bounds[:, None]).astype(jnp.int32), axis=1)
    return jnp.concatenate([ordered, starts])


def reduce_tiles(send_far, send_rest, own_far, own_rest):
    got_far = shift(send_far, "core", 1)
    send_rest, got_far = lax.optimization_barrier((send_rest, got_far))
    got_rest = shift(send_rest, "core", 1)
    far = (own_far + got_far.astype(F32)).astype(BF16)
    from_down = shift(far[:8], "first", 1)
    from_up = shift(far[8:], "first", -1)
    here, up, down = (own_rest + got_rest.astype(F32)).reshape(3, 16, BS, BS)
    own_up = shift(up[8:].astype(BF16), "first", 1)
    own_down = shift(down[:8].astype(BF16), "first", -1)
    low = shift((up[:8] + from_down.astype(F32)).astype(BF16), "first", 1)
    high = shift((down[8:] + from_up.astype(F32)).astype(BF16), "first", -1)
    low = here[:8] + low.astype(F32) + own_down.astype(F32)
    high = here[8:] + high.astype(F32) + own_up.astype(F32)
    total = (*low.reshape(2, CAPO, BS, BS), *high.reshape(2, CAPO, BS, BS))
    out = total[0]
    for k in (2, 1, 3):
        out = out + shift(total[k].astype(BF16), "second", k).astype(F32)
    return out


def on_device(
    features, out_grad, gate_pre, up_pre, hidden_grad, block_hidden, block_feature, block_slot
):
    tok_rows = features.shape[0]
    n_col = lax.axis_size("col")
    scale = 1.0 / math.sqrt(tok_rows * lax.axis_size("tok"))
    ring = [
        (t * n_col + z, t * n_col + (z + (1 if t % NC == 0 else -1)) % n_col)
        for t in range(NX * NY * NC)
        for z in range(n_col)
    ]
    table = tile_table(
        block_hidden, block_feature, block_slot, n_col, features.shape[1] // BS, gate_pre.shape[1] // BS
    )
    hid = hidden_blocks(gate_pre, up_pre, hidden_grad)
    tiles = tuple(
        jnp.zeros((size, BS, BS), BF16 if g < 2 else F32) for g, (base, size) in enumerate(GROUPS)
    )
    tie = lax.optimization_barrier
    chunks = [features, out_grad]
    made = 0
    for segment in range(2, 2 * n_col):
        value = chunks[segment - 2]
        if segment == 4:
            value, table, hid, tiles = tie((value, table, hid, tiles))
        if segment > 4:
            tiles = make_tiles(made, table, chunks[made], hid, tiles, scale)
            made += 1
            value, tiles = tie((value, tiles))
        chunks.append(lax.ppermute(value, ("tok", "col"), ring))
    for segment in range(made, 2 * n_col):
        tiles = make_tiles(segment, table, chunks[segment], hid, tiles, scale)
    return reduce_tiles(*tiles)[None]


def solution(mesh):
    in_specs = (P("tok", "col"),) * 5 + (P(), P(), P())
    return jax.shard_map(
        on_device,
        mesh=mesh,
        in_specs=in_specs,
        out_specs=P("col", "tok", None, None),
        check_vma=False,
    )
```

time: 135 us -> 124 us (0.919)
  the two profiles are of different devices: /device:TPU:32 before, /device:TPU:24 now
where the time goes in v4:
time: 124 us
  waiting for transfers between devices  72 us (58%)
  Pallas kernels  23.4 us (19%)
  starting transfers between devices  19 us (15%)
  local copies, waits for them, and re-layouts  5.44 us (4%)
  other arithmetic  3.44 us (3%)
    ppermute x14, waiting for transfers between devices, on_device(): chunks.append(lax.ppermute(value, ('tok', 'col'), ring))  52.2 us
    pallas_call x16, Pallas kernels, make_tiles(): pl.pallas_call(body, in_specs=[pl.BlockSpec(memory_space=pltpu.SMEM), pl....  21.8 us
    ppermute x11, waiting for transfers between devices, shift(): return lax.ppermute(value, 'tok', pairs)  19.8 us
    ppermute x11, starting transfers between devices, shift(): return lax.ppermute(value, 'tok', pairs)  14 us
    ppermute x14, starting transfers between devices, on_device(): chunks.append(lax.ppermute(value, ('tok', 'col'), ring))  4.94 us
    unnamed x10, local copies, waits for them, and re-layouts  3.54 us
  transfers between devices with their start and end apart: 25, of which 21 were waited for; matrix products, arithmetic and copies ran while one was open for 4% of the time, Pallas kernels for 18%

profile of v4, /device:TPU:24, one launch (start us, length us, event | category | flops | bytes accessed | tf_op | source)
XLA Modules:
  0.0 123.6 jit_solution(3144713322160109671)
XLA Ops:
  15.8 3.1 %collective-permute-done.1.refs_1_ = bf16[256,1024]{1,0:T(8,128)(2,1)S(1)} collective-permute-done((bf16[256,1024]{1,0:T(8,128)(2,1)}, bf16[256,1024]{1,0:T(8,128)(2,1)S(1)}, u32[]{:S(2)}, u32[]{:S(2)}) %collective-permute-start.1) | collective-permute-done | bytes 524320 | tf_op jit(solution)/shard_map/ppermute | solution.py:233
  20.5 4.0 %collective-permute-done.3.refs_1_ = bf16[256,1024]{1,0:T(8,128)(2,1)S(1)} collective-permute-done((bf16[256,1024]{1,0:T(8,128)(2,1)S(1)}, bf16[256,1024]{1,0:T(8,128)(2,1)S(1)}, u32[]{:S(2)}, u32[]{:S(2)}) %collective-permute-start.3) | collective-permute-done | bytes 524320 | tf_op jit(solution)/shard_map/ppermute | solution.py:233
  25.8 4.3 %collective-permute-done.2.refs_1_ = bf16[256,1024]{1,0:T(8,128)(2,1)S(1)} collective-permute-done((bf16[256,1024]{1,0:T(8,128)(2,1)S(1)}, bf16[256,1024]{1,0:T(8,128)(2,1)S(1)}, u32[]{:S(2)}, u32[]{:S(2)}) %collective-permute-start.2) | collective-permute-done | bytes 524320 | tf_op jit(solution)/shard_map/ppermute | solution.py:233
  31.4 4.3 %collective-permute-done.5.refs_1_ = bf16[256,1024]{1,0:T(8,128)(2,1)S(1)} collective-permute-done((bf16[256,1024]{1,0:T(8,128)(2,1)S(1)}, bf16[256,1024]{1,0:T(8,128)(2,1)S(1)}, u32[]{:S(2)}, u32[]{:S(2)}) %collective-permute-start.5) | collective-permute-done | bytes 524320 | tf_op jit(solution)/shard_map/ppermute | solution.py:233
  35.7 2.0 %tiles_4.1 = (bf16[16,128,128]{2,1,0:T(8,128)(2,1)S(1)}, bf16[48,128,128]{2,1,0:T(8,128)(2,1)S(1)}, f32[16,128,128]{2,1,0:T(8,128)S(1)}, f32[48,128,128]{2,1,0:T(8,128)S(1)}) custom-call(s32[152]{0:T(256)S(1)} %pad_add_fusion.refs_0_, ...), custom_call_target="tpu_custom_call", output_to_operand_aliasing={{0}: (3, {}), {1}: (4, {}), {2}: (5, {}), {3}: (6, {})} | custom-call | bytes 4194304 | tf_op jit(solution)/shard_map/tiles_4/pallas_call | solution.py:108
  37.7 3.6 %collective-permute-done.4.refs_1_ = bf16[256,1024]{1,0:T(8,128)(2,1)S(1)} collective-permute-done((bf16[256,1024]{1,0:T(8,128)(2,1)S(1)}, bf16[256,1024]{1,0:T(8,128)(2,1)S(1)}, u32[]{:S(2)}, u32[]{:S(2)}) %collective-permute-start.4) | collective-permute-done | bytes 524320 | tf_op jit(solution)/shard_map/ppermute | solution.py:233
  43.0 4.0 %collective-permute-done.7.refs_1_ = bf16[256,1024]{1,0:T(8,128)(2,1)S(1)} collective-permute-done((bf16[256,1024]{1,0:T(8,128)(2,1)S(1)}, bf16[256,1024]{1,0:T(8,128)(2,1)S(1)}, u32[]{:S(2)}, u32[]{:S(2)}) %collective-permute-start.7) | collective-permute-done | bytes 524320 | tf_op jit(solution)/shard_map/ppermute | solution.py:233
  48.3 4.3 %collective-permute-done.6.refs_1_ = bf16[256,1024]{1,0:T(8,128)(2,1)S(1)} collective-permute-done((bf16[256,1024]{1,0:T(8,128)(2,1)S(1)}, bf16[256,1024]{1,0:T(8,128)(2,1)S(1)}, u32[]{:S(2)}, u32[]{:S(2)}) %collective-permute-start.6) | collective-permute-done | bytes 524320 | tf_op jit(solution)/shard_map/ppermute | solution.py:233
  53.2 5.0 %collective-permute-done.9.refs_1_ = bf16[256,1024]{1,0:T(8,128)(2,1)S(1)} collective-permute-done((bf16[256,1024]{1,0:T(8,128)(2,1)S(1)}, bf16[256,1024]{1,0:T(8,128)(2,1)S(1)}, u32[]{:S(2)}, u32[]{:S(2)}) %collective-permute-start.9) | collective-permute-done | bytes 524320 | tf_op jit(solution)/shard_map/ppermute | solution.py:233
  58.2 2.0 %tiles_8.1 = (bf16[16,128,128]{2,1,0:T(8,128)(2,1)S(1)}, bf16[48,128,128]{2,1,0:T(8,128)(2,1)S(1)}, f32[16,128,128]{2,1,0:T(8,128)S(1)}, f32[48,128,128]{2,1,0:T(8,128)S(1)}) custom-call(s32[152]{0:T(256)S(1)} %pad_add_fusion.refs_0_, ...), custom_call_target="tpu_custom_call", output_to_operand_aliasing={{0}: (3, {}), {1}: (4, {}), {2}: (5, {}), {3}: (6, {})} | custom-call | bytes 4194304 | tf_op jit(solution)/shard_map/tiles_8/pallas_call | solution.py:108
  60.2 3.6 %collective-permute-done.8.refs_1_ = bf16[256,1024]{1,0:T(8,128)(2,1)S(1)} collective-permute-done((bf16[256,1024]{1,0:T(8,128)(2,1)S(1)}, bf16[256,1024]{1,0:T(8,128)(2,1)S(1)}, u32[]{:S(2)}, u32[]{:S(2)}) %collective-permute-start.8) | collective-permute-done | bytes 524320 | tf_op jit(solution)/shard_map/ppermute | solution.py:233
  65.1 4.3 %collective-permute-done.11.refs_1_ = bf16[256,1024]{1,0:T(8,128)(2,1)S(1)} collective-permute-done((bf16[256,1024]{1,0:T(8,128)(2,1)S(1)}, bf16[256,1024]{1,0:T(8,128)(2,1)S(1)}, u32[]{:S(2)}, u32[]{:S(2)}) %collective-permute-start.11) | collective-permute-done | bytes 524320 | tf_op jit(solution)/shard_map/ppermute | solution.py:233
  70.8 4.2 %collective-permute-done.10.refs_1_ = bf16[256,1024]{1,0:T(8,128)(2,1)S(1)} collective-permute-done((bf16[256,1024]{1,0:T(8,128)(2,1)S(1)}, bf16[256,1024]{1,0:T(8,128)(2,1)S(1)}, u32[]{:S(2)}, u32[]{:S(2)}) %collective-permute-start.10) | collective-permute-done | bytes 524320 | tf_op jit(solution)/shard_map/ppermute | solution.py:233
  78.3 2.4 %collective-permute-done.13.refs_1_ = bf16[256,1024]{1,0:T(8,128)(2,1)S(1)} collective-permute-done((bf16[256,1024]{1,0:T(8,128)(2,1)S(1)}, bf16[256,1024]{1,0:T(8,128)(2,1)S(1)}, u32[]{:S(2)}, u32[]{:S(2)}) %collective-permute-start.13) | collective-permute-done | bytes 524320 | tf_op jit(solution)/shard_map/ppermute | solution.py:233
  80.6 2.1 %tiles_14.1 = (bf16[16,128,128]{2,1,0:T(8,128)(2,1)S(1)}, bf16[48,128,128]{2,1,0:T(8,128)(2,1)S(1)}, f32[16,128,128]{2,1,0:T(8,128)S(1)}, f32[48,128,128]{2,1,0:T(8,128)S(1)}) custom-call(s32[152]{0:T(256)S(1)} %pad_add_fusion.refs_0_, ...), custom_call_target="tpu_custom_call", output_to_operand_aliasing={{0}: (3, {}), {1}: (4, {}), {2}: (5, {}), {3}: (6, {})} | custom-call | bytes 4194304 | tf_op jit(solution)/shard_map/tiles_14/pallas_call | solution.py:108
  82.8 3.5 %collective-permute-done.12.refs_1_ = bf16[256,1024]{1,0:T(8,128)(2,1)S(1)} collective-permute-done((bf16[256,1024]{1,0:T(8,128)(2,1)S(1)}, bf16[256,1024]{1,0:T(8,128)(2,1)S(1)}, u32[]{:S(2)}, u32[]{:S(2)}) %collective-permute-start.12) | collective-permute-done | bytes 524320 | tf_op jit(solution)/shard_map/ppermute | solution.py:233
  90.1 2.8 %collective-permute-start.19 = (bf16[8,128,128]{2,1,0:T(8,128)(2,1)S(1)}, bf16[8,128,128]{2,1,0:T(8,128)(2,1)S(1)}, u32[]{:S(2)}, u32[]{:S(2)}) collective-permute-start(bf16[8,128,128]{2,1,0:T(8,128)(2,1)S(1)} %get-tuple-element.267), channel_id=1, source_target_pairs={{0,192},{8,56},{16,208},{24,8},{32,224},{40,24},{48,240},{56,40},{... | collective-permute-start | bytes 786440 | tf_op jit(solution)/shard_map/ppermute | solution.py:146
  94.0 2.9 %collective-permute-done.19 = bf16[8,128,128]{2,1,0:T(8,128)(2,1)S(1)} collective-permute-done((bf16[8,128,128]{2,1,0:T(8,128)(2,1)S(1)}, bf16[8,128,128]{2,1,0:T(8,128)(2,1)S(1)}, u32[]{:S(2)}, u32[]{:S(2)}) %collective-permute-start.19) | collective-permute-done | bytes 262176 | tf_op jit(solution)/shard_map/ppermute | solution.py:146
  96.9 3.8 %collective-permute-start.20 = (bf16[8,128,128]{2,1,0:T(8,128)(2,1)S(1)}, bf16[8,128,128]{2,1,0:T(8,128)(2,1)S(1)}, u32[]{:S(2)}, u32[]{:S(2)}) collective-permute-start(bf16[8,128,128]{2,1,0:T(8,128)(2,1)S(1)} %fusion), channel_id=1, source_target_pairs={{0,192},{8,56},{16,208},{24,8},{32,224},{40,24},{48,240},{56,40},{... | collective-permute-start | bytes 786440 | tf_op jit(solution)/shard_map/ppermute | solution.py:146
  100.8 3.2 %collective-permute-start.18 = (bf16[8,128,128]{2,1,0:T(8,128)(2,1)S(1)}, bf16[8,128,128]{2,1,0:T(8,128)(2,1)S(1)}, u32[]{:S(2)}, u32[]{:S(2)}) collective-permute-start(bf16[8,128,128]{2,1,0:T(8,128)(2,1)S(1)} %get-tuple-element.266), channel_id=1, source_target_pairs={{0,192},{8,56},{16,208},{24,8},{32,224},{40,24},{48,240},{56,40},{... | collective-permute-start | bytes 786440 | tf_op jit(solution)/shard_map/ppermute | solution.py:146
  104.6 3.8 %collective-permute-done.21 = bf16[8,128,128]{2,1,0:T(8,128)(2,1)S(1)} collective-permute-done((bf16[8,128,128]{2,1,0:T(8,128)(2,1)S(1)}, bf16[8,128,128]{2,1,0:T(8,128)(2,1)S(1)}, u32[]{:S(2)}, u32[]{:S(2)}) %collective-permute-start.21) | collective-permute-done | bytes 262176 | tf_op jit(solution)/shard_map/ppermute | solution.py:146
  110.0 2.2 %collective-permute-start.24 = (bf16[4,128,128]{2,1,0:T(8,128)(2,1)S(1)}, bf16[4,128,128]{2,1,0:T(8,128)(2,1)S(1)}, u32[]{:S(2)}, u32[]{:S(2)}) collective-permute-start(bf16[4,128,128]{2,1,0:T(8,128)(2,1)S(1)} %get-tuple-element.270), channel_id=1, source_target_pairs={{0,48},{8,200},{16,32},{24,216},{32,16},{40,232},{48,0},{56,248},{... | collective-permute-start | bytes 393224 | tf_op jit(solution)/shard_map/ppermute | solution.py:146
  112.2 5.5 %collective-permute-done.17 = bf16[8,128,128]{2,1,0:T(8,128)(2,1)S(1)} collective-permute-done((bf16[8,128,128]{2,1,0:T(8,128)(2,1)S(1)}, bf16[8,128,128]{2,1,0:T(8,128)(2,1)S(1)}, u32[]{:S(2)}, u32[]{:S(2)}) %collective-permute-start.17) | collective-permute-done | bytes 262176 | tf_op jit(solution)/shard_map/ppermute | solution.py:146
  117.9 4.9 %collective-permute-done.23 = bf16[4,128,128]{2,1,0:T(8,128)(2,1)S(1)} collective-permute-done((bf16[4,128,128]{2,1,0:T(8,128)(2,1)S(1)}, bf16[4,128,128]{2,1,0:T(8,128)(2,1)S(1)}, u32[]{:S(2)}, u32[]{:S(2)}) %collective-permute-start.23) | collective-permute-done | bytes 131104 | tf_op jit(solution)/shard_map/ppermute | solution.py:146
  (80 shorter events, 37.7 us)
Async XLA Ops:
  0.0 13.2 %collective-permute-start = (bf16[256,1024]{1,0:T(8,128)(2,1)}, bf16[256,1024]{1,0:T(8,128)(2,1)S(1)}, u32[]{:S(2)}, u32[]{:S(2)}) collective-permute-start(bf16[256,1024]{1,0:T(8,128)(2,1)} %refs_1_.2), channel_id=1, source_target_pairs={{0,1},{1,2},{2,3},{3,4},{4,5},{5,6},{6,7},{7,0},{8,15},{9,8},{10,9... | collective-permute-start | bytes 1572872 | tf_op jit(solution)/shard_map/ppermute | solution.py:233
  1.9 16.9 %collective-permute-start.1 = (bf16[256,1024]{1,0:T(8,128)(2,1)}, bf16[256,1024]{1,0:T(8,128)(2,1)S(1)}, u32[]{:S(2)}, u32[]{:S(2)}) collective-permute-start(bf16[256,1024]{1,0:T(8,128)(2,1)} %refs_1_.3), channel_id=1, source_target_pairs={{0,1},{1,2},{2,3},{3,4},{4,5},{5,6},{6,7},{7,0},{8,15},{9,8},{10,9... | collective-permute-start | bytes 1572872 | tf_op jit(solution)/shard_map/ppermute | solution.py:233
  13.2 11.2 %collective-permute-start.3 = (bf16[256,1024]{1,0:T(8,128)(2,1)S(1)}, bf16[256,1024]{1,0:T(8,128)(2,1)S(1)}, u32[]{:S(2)}, u32[]{:S(2)}) collective-permute-start(bf16[256,1024]{1,0:T(8,128)(2,1)S(1)} %collective-permute-done.refs_1_), channel_id=1, source_target_pairs={{0,1},{1,2},{2,3},{3,4},{4,5},{5,6},{6,7},{7,0},{8,15},{9,8},{10,9... | collective-permute-start | bytes 1572872 | tf_op jit(solution)/shard_map/ppermute | solution.py:233
  18.8 11.2 %collective-permute-start.2 = (bf16[256,1024]{1,0:T(8,128)(2,1)S(1)}, bf16[256,1024]{1,0:T(8,128)(2,1)S(1)}, u32[]{:S(2)}, u32[]{:S(2)}) collective-permute-start(bf16[256,1024]{1,0:T(8,128)(2,1)S(1)} %collective-permute-done.1.refs_1_), channel_id=1, source_target_pairs={{0,1},{1,2},{2,3},{3,4},{4,5},{5,6},{6,7},{7,0},{8,15},{9,8},{10,9... | collective-permute-start | bytes 1572872 | tf_op jit(solution)/shard_map/ppermute | solution.py:233
  24.5 11.2 %collective-permute-start.5 = (bf16[256,1024]{1,0:T(8,128)(2,1)S(1)}, bf16[256,1024]{1,0:T(8,128)(2,1)S(1)}, u32[]{:S(2)}, u32[]{:S(2)}) collective-permute-start(bf16[256,1024]{1,0:T(8,128)(2,1)S(1)} %collective-permute-done.3.refs_1_), channel_id=1, source_target_pairs={{0,1},{1,2},{2,3},{3,4},{4,5},{5,6},{6,7},{7,0},{8,15},{9,8},{10,9... | collective-permute-start | bytes 1572872 | tf_op jit(solution)/shard_map/ppermute | solution.py:233
  30.1 11.2 %collective-permute-start.4 = (bf16[256,1024]{1,0:T(8,128)(2,1)S(1)}, bf16[256,1024]{1,0:T(8,128)(2,1)S(1)}, u32[]{:S(2)}, u32[]{:S(2)}) collective-permute-start(bf16[256,1024]{1,0:T(8,128)(2,1)S(1)} %collective-permute-done.2.refs_1_), channel_id=1, source_target_pairs={{0,1},{1,2},{2,3},{3,4},{4,5},{5,6},{6,7},{7,0},{8,15},{9,8},{10,9... | collective-permute-start | bytes 1572872 | tf_op jit(solution)/shard_map/ppermute | solution.py:233
  35.7 11.2 %collective-permute-start.7 = (bf16[256,1024]{1,0:T(8,128)(2,1)S(1)}, bf16[256,1024]{1,0:T(8,128)(2,1)S(1)}, u32[]{:S(2)}, u32[]{:S(2)}) collective-permute-start(bf16[256,1024]{1,0:T(8,128)(2,1)S(1)} %collective-permute-done.5.refs_1_), channel_id=1, source_target_pairs={{0,1},{1,2},{2,3},{3,4},{4,5},{5,6},{6,7},{7,0},{8,15},{9,8},{10,9... | collective-permute-start | bytes 1572872 | tf_op jit(solution)/shard_map/ppermute | solution.py:233
  41.3 11.2 %collective-permute-start.6 = (bf16[256,1024]{1,0:T(8,128)(2,1)S(1)}, bf16[256,1024]{1,0:T(8,128)(2,1)S(1)}, u32[]{:S(2)}, u32[]{:S(2)}) collective-permute-start(bf16[256,1024]{1,0:T(8,128)(2,1)S(1)} %collective-permute-done.4.refs_1_), channel_id=1, source_target_pairs={{0,1},{1,2},{2,3},{3,4},{4,5},{5,6},{6,7},{7,0},{8,15},{9,8},{10,9... | collective-permute-start | bytes 1572872 | tf_op jit(solution)/shard_map/ppermute | solution.py:233
  46.9 11.2 %collective-permute-start.9 = (bf16[256,1024]{1,0:T(8,128)(2,1)S(1)}, bf16[256,1024]{1,0:T(8,128)(2,1)S(1)}, u32[]{:S(2)}, u32[]{:S(2)}) collective-permute-start(bf16[256,1024]{1,0:T(8,128)(2,1)S(1)} %collective-permute-done.7.refs_1_), channel_id=1, source_target_pairs={{0,1},{1,2},{2,3},{3,4},{4,5},{5,6},{6,7},{7,0},{8,15},{9,8},{10,9... | collective-permute-start | bytes 1572872 | tf_op jit(solution)/shard_map/ppermute | solution.py:233
  52.5 11.2 %collective-permute-start.8 = (bf16[256,1024]{1,0:T(8,128)(2,1)S(1)}, bf16[256,1024]{1,0:T(8,128)(2,1)S(1)}, u32[]{:S(2)}, u32[]{:S(2)}) collective-permute-start(bf16[256,1024]{1,0:T(8,128)(2,1)S(1)} %collective-permute-done.6.refs_1_), channel_id=1, source_target_pairs={{0,1},{1,2},{2,3},{3,4},{4,5},{5,6},{6,7},{7,0},{8,15},{9,8},{10,9... | collective-permute-start | bytes 1572872 | tf_op jit(solution)/shard_map/ppermute | solution.py:233
  58.2 11.2 %collective-permute-start.11 = (bf16[256,1024]{1,0:T(8,128)(2,1)S(1)}, bf16[256,1024]{1,0:T(8,128)(2,1)S(1)}, u32[]{:S(2)}, u32[]{:S(2)}) collective-permute-start(bf16[256,1024]{1,0:T(8,128)(2,1)S(1)} %collective-permute-done.9.refs_1_), channel_id=1, source_target_pairs={{0,1},{1,2},{2,3},{3,4},{4,5},{5,6},{6,7},{7,0},{8,15},{9,8},{10,9... | collective-permute-start | bytes 1572872 | tf_op jit(solution)/shard_map/ppermute | solution.py:233
  63.8 11.2 %collective-permute-start.10 = (bf16[256,1024]{1,0:T(8,128)(2,1)S(1)}, bf16[256,1024]{1,0:T(8,128)(2,1)S(1)}, u32[]{:S(2)}, u32[]{:S(2)}) collective-permute-start(bf16[256,1024]{1,0:T(8,128)(2,1)S(1)} %collective-permute-done.8.refs_1_), channel_id=1, source_target_pairs={{0,1},{1,2},{2,3},{3,4},{4,5},{5,6},{6,7},{7,0},{8,15},{9,8},{10,9... | collective-permute-start | bytes 1572872 | tf_op jit(solution)/shard_map/ppermute | solution.py:233
  69.4 11.2 %collective-permute-start.13 = (bf16[256,1024]{1,0:T(8,128)(2,1)S(1)}, bf16[256,1024]{1,0:T(8,128)(2,1)S(1)}, u32[]{:S(2)}, u32[]{:S(2)}) collective-permute-start(bf16[256,1024]{1,0:T(8,128)(2,1)S(1)} %collective-permute-done.11.refs_1_), channel_id=1, source_target_pairs={{0,1},{1,2},{2,3},{3,4},{4,5},{5,6},{6,7},{7,0},{8,15},{9,8},{10,9... | collective-permute-start | bytes 1572872 | tf_op jit(solution)/shard_map/ppermute | solution.py:233
  75.0 11.2 %collective-permute-start.12 = (bf16[256,1024]{1,0:T(8,128)(2,1)S(1)}, bf16[256,1024]{1,0:T(8,128)(2,1)S(1)}, u32[]{:S(2)}, u32[]{:S(2)}) collective-permute-start(bf16[256,1024]{1,0:T(8,128)(2,1)S(1)} %collective-permute-done.10.refs_1_), channel_id=1, source_target_pairs={{0,1},{1,2},{2,3},{3,4},{4,5},{5,6},{6,7},{7,0},{8,15},{9,8},{10,9... | collective-permute-start | bytes 1572872 | tf_op jit(solution)/shard_map/ppermute | solution.py:233
  89.8 3.4 %collective-permute-start.15 = (bf16[48,128,128]{2,1,0:T(8,128)(2,1)S(1)}, bf16[48,128,128]{2,1,0:T(8,128)(2,1)S(1)}, u32[]{:S(2)}, u32[]{:S(2)}) collective-permute-start(bf16[48,128,128]{2,1,0:T(8,128)(2,1)S(1)} %get-tuple-element.258), channel_id=1, source_target_pairs={{0,8},{8,0},{16,24},{24,16},{32,40},{40,32},{48,56},{56,48},{64,72... | collective-permute-start | bytes 4718600 | tf_op jit(solution)/shard_map/ppermute | solution.py:146
  90.1 6.7 %collective-permute-start.19 = (bf16[8,128,128]{2,1,0:T(8,128)(2,1)S(1)}, bf16[8,128,128]{2,1,0:T(8,128)(2,1)S(1)}, u32[]{:S(2)}, u32[]{:S(2)}) collective-permute-start(bf16[8,128,128]{2,1,0:T(8,128)(2,1)S(1)} %get-tuple-element.267), channel_id=1, source_target_pairs={{0,192},{8,56},{16,208},{24,8},{32,224},{40,24},{48,240},{56,40},{... | collective-permute-start | bytes 786440 | tf_op jit(solution)/shard_map/ppermute | solution.py:146
  93.0 11.1 %collective-permute-start.16 = (bf16[8,128,128]{2,1,0:T(8,128)(2,1)S(1)}, bf16[8,128,128]{2,1,0:T(8,128)(2,1)S(1)}, u32[]{:S(2)}, u32[]{:S(2)}) collective-permute-start(bf16[8,128,128]{2,1,0:T(8,128)(2,1)S(1)} %get-tuple-element.268), channel_id=1, source_target_pairs={{0,64},{8,24},{16,80},{24,40},{32,96},{40,56},{48,112},{56,8},{64,... | collective-permute-start | bytes 786440 | tf_op jit(solution)/shard_map/ppermute | solution.py:146
  96.9 7.7 %collective-permute-start.20 = (bf16[8,128,128]{2,1,0:T(8,128)(2,1)S(1)}, bf16[8,128,128]{2,1,0:T(8,128)(2,1)S(1)}, u32[]{:S(2)}, u32[]{:S(2)}) collective-permute-start(bf16[8,128,128]{2,1,0:T(8,128)(2,1)S(1)} %fusion), channel_id=1, source_target_pairs={{0,192},{8,56},{16,208},{24,8},{32,224},{40,24},{48,240},{56,40},{... | collective-permute-start | bytes 786440 | tf_op jit(solution)/shard_map/ppermute | solution.py:146
  100.8 7.7 %collective-permute-start.21 = (bf16[8,128,128]{2,1,0:T(8,128)(2,1)S(1)}, bf16[8,128,128]{2,1,0:T(8,128)(2,1)S(1)}, u32[]{:S(2)}, u32[]{:S(2)}) collective-permute-start(bf16[8,128,128]{2,1,0:T(8,128)(2,1)S(1)} %get-tuple-element.265), channel_id=1, source_target_pairs={{0,64},{8,24},{16,80},{24,40},{32,96},{40,56},{48,112},{56,8},{64,... | collective-permute-start | bytes 786440 | tf_op jit(solution)/shard_map/ppermute | solution.py:146
  100.8 11.4 %collective-permute-start.18 = (bf16[8,128,128]{2,1,0:T(8,128)(2,1)S(1)}, bf16[8,128,128]{2,1,0:T(8,128)(2,1)S(1)}, u32[]{:S(2)}, u32[]{:S(2)}) collective-permute-start(bf16[8,128,128]{2,1,0:T(8,128)(2,1)S(1)} %get-tuple-element.266), channel_id=1, source_target_pairs={{0,192},{8,56},{16,208},{24,8},{32,224},{40,24},{48,240},{56,40},{... | collective-permute-start | bytes 786440 | tf_op jit(solution)/shard_map/ppermute | solution.py:146
  108.6 9.1 %collective-permute-start.17 = (bf16[8,128,128]{2,1,0:T(8,128)(2,1)S(1)}, bf16[8,128,128]{2,1,0:T(8,128)(2,1)S(1)}, u32[]{:S(2)}, u32[]{:S(2)}) collective-permute-start(bf16[8,128,128]{2,1,0:T(8,128)(2,1)S(1)} %get-tuple-element.264), channel_id=1, source_target_pairs={{0,64},{8,24},{16,80},{24,40},{32,96},{40,56},{48,112},{56,8},{64,... | collective-permute-start | bytes 786440 | tf_op jit(solution)/shard_map/ppermute | solution.py:146
  108.7 9.2 %collective-permute-start.22 = (bf16[4,128,128]{2,1,0:T(8,128)(2,1)S(1)}, bf16[4,128,128]{2,1,0:T(8,128)(2,1)S(1)}, u32[]{:S(2)}, u32[]{:S(2)}) collective-permute-start(bf16[4,128,128]{2,1,0:T(8,128)(2,1)S(1)} %get-tuple-element.269), channel_id=1, source_target_pairs={{0,32},{8,136},{16,48},{24,152},{32,0},{40,168},{48,16},{56,184},{... | collective-permute-start | bytes 393224 | tf_op jit(solution)/shard_map/ppermute | solution.py:146
  110.0 7.9 %collective-permute-start.24 = (bf16[4,128,128]{2,1,0:T(8,128)(2,1)S(1)}, bf16[4,128,128]{2,1,0:T(8,128)(2,1)S(1)}, u32[]{:S(2)}, u32[]{:S(2)}) collective-permute-start(bf16[4,128,128]{2,1,0:T(8,128)(2,1)S(1)} %get-tuple-element.270), channel_id=1, source_target_pairs={{0,48},{8,200},{16,32},{24,216},{32,16},{40,232},{48,0},{56,248},{... | collective-permute-start | bytes 393224 | tf_op jit(solution)/shard_map/ppermute | solution.py:146
  117.8 5.1 %collective-permute-start.23 = (bf16[4,128,128]{2,1,0:T(8,128)(2,1)S(1)}, bf16[4,128,128]{2,1,0:T(8,128)(2,1)S(1)}, u32[]{:S(2)}, u32[]{:S(2)}) collective-permute-start(bf16[4,128,128]{2,1,0:T(8,128)(2,1)S(1)} %unstack.38), channel_id=1, source_target_pairs={{0,16},{8,72},{16,0},{24,88},{32,48},{40,104},{48,32},{56,120},{64... | collective-permute-start | bytes 393224 | tf_op jit(solution)/shard_map/ppermute | solution.py:146
  (6 other events, 12.3 us)

commit v5 on v4

--- a/solution.py
+++ b/solution.py
@@ -12,7 +12,7 @@
 CAPO = 4
 UNROLL = 4
 PLACES = NX * NY * NC * CAPO
-GROUPS = ((0, 16), (16, 48), (64, 16), (80, 48))
+GROUPS = ((0, 32), (32, 32), (64, 32), (96, 32))
 F32, BF16 = jnp.float32, jnp.bfloat16
 ANY = pl.BlockSpec(memory_space=pl.ANY)
 
@@ -149,10 +149,10 @@
 def slot_order():
     x, y, c = place()
     p = jnp.arange(PLACES, dtype=jnp.int32)
-    q = p % 64
-    near = (q - 16) // 16
-    d1 = jnp.where(q < 16, 2, jnp.where(near == 2, 3, near))
-    d2 = (q // CAPO) % 4
+    b = (p // 8) % 8
+    d1 = jnp.where((b == 1) | (b == 4), 1, jnp.where((b == 0) | (b == 2), 2, jnp.where(b < 6, 3, 0)))
+    upper = (b == 1) | (b == 2) | (b == 5) | (b == 7)
+    d2 = (p // CAPO) % 2 + 2 * upper.astype(jnp.int32)
     to_c = jnp.where(p < 64, 1 - c, c)
     to_x = jnp.where(to_c == 0, (x + d1) % NX, x ^ d2)
     to_y = jnp.where(to_c == 0, y ^ d2, (y + d1) % NY)
@@ -180,24 +180,33 @@
     return jnp.concatenate([ordered, starts])
 
 
-def reduce_tiles(send_far, send_rest, own_far, own_rest):
-    got_far = shift(send_far, "core", 1)
-    send_rest, got_far = lax.optimization_barrier((send_rest, got_far))
+def reduce_tiles(send_now, send_rest, own_now, own_rest):
+    tie = lax.optimization_barrier
+    got_now = shift(send_now, "core", 1)
+    send_rest, got_now = tie((send_rest, got_now))
     got_rest = shift(send_rest, "core", 1)
-    far = (own_far + got_far.astype(F32)).astype(BF16)
-    from_down = shift(far[:8], "first", 1)
-    from_up = shift(far[8:], "first", -1)
-    here, up, down = (own_rest + got_rest.astype(F32)).reshape(3, 16, BS, BS)
-    own_up = shift(up[8:].astype(BF16), "first", 1)
-    own_down = shift(down[:8].astype(BF16), "first", -1)
-    low = shift((up[:8] + from_down.astype(F32)).astype(BF16), "first", 1)
-    high = shift((down[8:] + from_up.astype(F32)).astype(BF16), "first", -1)
-    low = here[:8] + low.astype(F32) + own_down.astype(F32)
-    high = here[8:] + high.astype(F32) + own_up.astype(F32)
+    now = (own_now + got_now.astype(F32)).astype(BF16)
+    up, down = tie((now[:16], now[16:]))
+    up = shift(up, "first", 1)
+    down = shift(down, "first", -1)
+    rest = own_rest + got_rest.astype(F32)
+    rest, up, down = tie((rest, up, down))
+    low, high = tie(
+        (
+            (rest[:8] + up[:8].astype(F32)).astype(BF16),
+            (rest[8:16] + down[:8].astype(F32)).astype(BF16),
+        )
+    )
+    low = shift(low, "first", 1)
+    high = shift(high, "first", -1)
+    low, high = tie((low, high))
+    low = rest[16:24] + low.astype(F32) + down[8:].astype(F32)
+    high = rest[24:] + high.astype(F32) + up[8:].astype(F32)
     total = (*low.reshape(2, CAPO, BS, BS), *high.reshape(2, CAPO, BS, BS))
-    out = total[0]
-    for k in (2, 1, 3):
-        out = out + shift(total[k].astype(BF16), "second", k).astype(F32)
+    out, *sent = tie((total[0], *(total[k].astype(BF16) for k in (2, 1, 3))))
+    got = tie(tuple(shift(value, "second", k) for value, k in zip(sent, (2, 1, 3))))
+    for value in got:
+        out = out + value.astype(F32)
     return out
 
 

time: 124 us -> 121 us (0.976)
  the two profiles are of different devices: /device:TPU:24 before, /device:TPU:6 now
where the time goes in v5:
time: 121 us
  waiting for transfers between devices  72.8 us (60%)
  Pallas kernels  25.6 us (21%)
  starting transfers between devices  13.4 us (11%)
  local copies, waits for them, and re-layouts  5.9 us (5%)
  other arithmetic  3.18 us (3%)
    ppermute x14, waiting for transfers between devices, on_device(): chunks.append(lax.ppermute(value, ('tok', 'col'), ring))  50 us
    pallas_call x16, Pallas kernels, make_tiles(): pl.pallas_call(body, in_specs=[pl.BlockSpec(memory_space=pltpu.SMEM), pl....  24 us
    ppermute x9, waiting for transfers between devices, shift(): return lax.ppermute(value, 'tok', pairs)  22.8 us
    ppermute x9, starting transfers between devices, shift(): return lax.ppermute(value, 'tok', pairs)  8.78 us
    ppermute x14, starting transfers between devices, on_device(): chunks.append(lax.ppermute(value, ('tok', 'col'), ring))  4.59 us
    unnamed x12, local copies, waits for them, and re-layouts  4.43 us
  transfers between devices with their start and end apart: 23, of which 22 were waited for; matrix products, arithmetic and copies ran while one was open for 3% of the time, Pallas kernels for 20%

profile of v5, /device:TPU:6, one launch (start us, length us, event | category | flops | bytes accessed | tf_op | source)
XLA Modules:
  0.0 121.1 jit_solution(14659550361832217280)
XLA Ops:
  0.0 1.9 %collective-permute-start = (bf16[256,1024]{1,0:T(8,128)(2,1)}, bf16[256,1024]{1,0:T(8,128)(2,1)S(1)}, u32[]{:S(2)}, u32[]{:S(2)}) collective-permute-start(bf16[256,1024]{1,0:T(8,128)(2,1)} %refs_1_.2), channel_id=1, source_target_pairs={{0,1},{1,2},{2,3},{3,4},{4,5},{5,6},{6,7},{7,0},{8,15},{9,8},{10,9... | collective-permute-start | bytes 1572872 | tf_op jit(solution)/shard_map/ppermute | solution.py:242
  1.9 1.9 %collective-permute-start.1 = (bf16[256,1024]{1,0:T(8,128)(2,1)}, bf16[256,1024]{1,0:T(8,128)(2,1)S(1)}, u32[]{:S(2)}, u32[]{:S(2)}) collective-permute-start(bf16[256,1024]{1,0:T(8,128)(2,1)} %refs_1_.3), channel_id=1, source_target_pairs={{0,1},{1,2},{2,3},{3,4},{4,5},{5,6},{6,7},{7,0},{8,15},{9,8},{10,9... | collective-permute-start | bytes 1572872 | tf_op jit(solution)/shard_map/ppermute | solution.py:242
  11.3 1.9 %collective-permute-done.refs_1_ = bf16[256,1024]{1,0:T(8,128)(2,1)S(1)} collective-permute-done((bf16[256,1024]{1,0:T(8,128)(2,1)}, bf16[256,1024]{1,0:T(8,128)(2,1)S(1)}, u32[]{:S(2)}, u32[]{:S(2)}) %collective-permute-start) | collective-permute-done | bytes 524320 | tf_op jit(solution)/shard_map/ppermute | solution.py:242
  16.0 2.8 %collective-permute-done.1.refs_1_ = bf16[256,1024]{1,0:T(8,128)(2,1)S(1)} collective-permute-done((bf16[256,1024]{1,0:T(8,128)(2,1)}, bf16[256,1024]{1,0:T(8,128)(2,1)S(1)}, u32[]{:S(2)}, u32[]{:S(2)}) %collective-permute-start.1) | collective-permute-done | bytes 524320 | tf_op jit(solution)/shard_map/ppermute | solution.py:242
  20.7 3.8 %collective-permute-done.3.refs_1_ = bf16[256,1024]{1,0:T(8,128)(2,1)S(1)} collective-permute-done((bf16[256,1024]{1,0:T(8,128)(2,1)S(1)}, bf16[256,1024]{1,0:T(8,128)(2,1)S(1)}, u32[]{:S(2)}, u32[]{:S(2)}) %collective-permute-start.3) | collective-permute-done | bytes 524320 | tf_op jit(solution)/shard_map/ppermute | solution.py:242
  25.9 4.3 %collective-permute-done.2.refs_1_ = bf16[256,1024]{1,0:T(8,128)(2,1)S(1)} collective-permute-done((bf16[256,1024]{1,0:T(8,128)(2,1)S(1)}, bf16[256,1024]{1,0:T(8,128)(2,1)S(1)}, u32[]{:S(2)}, u32[]{:S(2)}) %collective-permute-start.2) | collective-permute-done | bytes 524320 | tf_op jit(solution)/shard_map/ppermute | solution.py:242
  31.5 4.2 %collective-permute-done.5.refs_1_ = bf16[256,1024]{1,0:T(8,128)(2,1)S(1)} collective-permute-done((bf16[256,1024]{1,0:T(8,128)(2,1)S(1)}, bf16[256,1024]{1,0:T(8,128)(2,1)S(1)}, u32[]{:S(2)}, u32[]{:S(2)}) %collective-permute-start.5) | collective-permute-done | bytes 524320 | tf_op jit(solution)/shard_map/ppermute | solution.py:242
  35.8 2.1 %tiles_4.1 = (bf16[32,128,128]{2,1,0:T(8,128)(2,1)S(1)}, bf16[32,128,128]{2,1,0:T(8,128)(2,1)S(1)}, f32[32,128,128]{2,1,0:T(8,128)S(1)}, f32[32,128,128]{2,1,0:T(8,128)S(1)}) custom-call(s32[152]{0:T(256)S(1)} %pad_add_fusion.refs_0_, ...), custom_call_target="tpu_custom_call", output_to_operand_aliasing={{0}: (3, {}), {1}: (4, {}), {2}: (5, {}), {3}: (6, {})} | custom-call | bytes 4194304 | tf_op jit(solution)/shard_map/tiles_4/pallas_call | solution.py:108
  37.9 3.5 %collective-permute-done.4.refs_1_ = bf16[256,1024]{1,0:T(8,128)(2,1)S(1)} collective-permute-done((bf16[256,1024]{1,0:T(8,128)(2,1)S(1)}, bf16[256,1024]{1,0:T(8,128)(2,1)S(1)}, u32[]{:S(2)}, u32[]{:S(2)}) %collective-permute-start.4) | collective-permute-done | bytes 524320 | tf_op jit(solution)/shard_map/ppermute | solution.py:242
  42.8 4.2 %collective-permute-done.7.refs_1_ = bf16[256,1024]{1,0:T(8,128)(2,1)S(1)} collective-permute-done((bf16[256,1024]{1,0:T(8,128)(2,1)S(1)}, bf16[256,1024]{1,0:T(8,128)(2,1)S(1)}, u32[]{:S(2)}, u32[]{:S(2)}) %collective-permute-start.7) | collective-permute-done | bytes 524320 | tf_op jit(solution)/shard_map/ppermute | solution.py:242
  48.3 4.3 %collective-permute-done.6.refs_1_ = bf16[256,1024]{1,0:T(8,128)(2,1)S(1)} collective-permute-done((bf16[256,1024]{1,0:T(8,128)(2,1)S(1)}, bf16[256,1024]{1,0:T(8,128)(2,1)S(1)}, u32[]{:S(2)}, u32[]{:S(2)}) %collective-permute-start.6) | collective-permute-done | bytes 524320 | tf_op jit(solution)/shard_map/ppermute | solution.py:242
  53.8 4.4 %collective-permute-done.9.refs_1_ = bf16[256,1024]{1,0:T(8,128)(2,1)S(1)} collective-permute-done((bf16[256,1024]{1,0:T(8,128)(2,1)S(1)}, bf16[256,1024]{1,0:T(8,128)(2,1)S(1)}, u32[]{:S(2)}, u32[]{:S(2)}) %collective-permute-start.9) | collective-permute-done | bytes 524320 | tf_op jit(solution)/shard_map/ppermute | solution.py:242
  58.2 2.0 %tiles_8.1 = (bf16[32,128,128]{2,1,0:T(8,128)(2,1)S(1)}, bf16[32,128,128]{2,1,0:T(8,128)(2,1)S(1)}, f32[32,128,128]{2,1,0:T(8,128)S(1)}, f32[32,128,128]{2,1,0:T(8,128)S(1)}) custom-call(s32[152]{0:T(256)S(1)} %pad_add_fusion.refs_0_, ...), custom_call_target="tpu_custom_call", output_to_operand_aliasing={{0}: (3, {}), {1}: (4, {}), {2}: (5, {}), {3}: (6, {})} | custom-call | bytes 4194304 | tf_op jit(solution)/shard_map/tiles_8/pallas_call | solution.py:108
  60.2 3.6 %collective-permute-done.8.refs_1_ = bf16[256,1024]{1,0:T(8,128)(2,1)S(1)} collective-permute-done((bf16[256,1024]{1,0:T(8,128)(2,1)S(1)}, bf16[256,1024]{1,0:T(8,128)(2,1)S(1)}, u32[]{:S(2)}, u32[]{:S(2)}) %collective-permute-start.8) | collective-permute-done | bytes 524320 | tf_op jit(solution)/shard_map/ppermute | solution.py:242
  65.2 4.3 %collective-permute-done.11.refs_1_ = bf16[256,1024]{1,0:T(8,128)(2,1)S(1)} collective-permute-done((bf16[256,1024]{1,0:T(8,128)(2,1)S(1)}, bf16[256,1024]{1,0:T(8,128)(2,1)S(1)}, u32[]{:S(2)}, u32[]{:S(2)}) %collective-permute-start.11) | collective-permute-done | bytes 524320 | tf_op jit(solution)/shard_map/ppermute | solution.py:242
  69.5 2.2 %tiles_10.1 = (bf16[32,128,128]{2,1,0:T(8,128)(2,1)S(1)}, bf16[32,128,128]{2,1,0:T(8,128)(2,1)S(1)}, f32[32,128,128]{2,1,0:T(8,128)S(1)}, f32[32,128,128]{2,1,0:T(8,128)S(1)}) custom-call(s32[152]{0:T(256)S(1)} %pad_add_fusion.refs_0_, ...), custom_call_target="tpu_custom_call", output_to_operand_aliasing={{0}: (3, {}), {1}: (4, {}), {2}: (5, {}), {3}: (6, {})} | custom-call | bytes 4194304 | tf_op jit(solution)/shard_map/tiles_10/pallas_call | solution.py:108
  71.6 3.4 %collective-permute-done.10.refs_1_ = bf16[256,1024]{1,0:T(8,128)(2,1)S(1)} collective-permute-done((bf16[256,1024]{1,0:T(8,128)(2,1)S(1)}, bf16[256,1024]{1,0:T(8,128)(2,1)S(1)}, u32[]{:S(2)}, u32[]{:S(2)}) %collective-permute-start.10) | collective-permute-done | bytes 524320 | tf_op jit(solution)/shard_map/ppermute | solution.py:242
  80.7 2.1 %tiles_14.1 = (bf16[32,128,128]{2,1,0:T(8,128)(2,1)S(1)}, bf16[32,128,128]{2,1,0:T(8,128)(2,1)S(1)}, f32[32,128,128]{2,1,0:T(8,128)S(1)}, f32[32,128,128]{2,1,0:T(8,128)S(1)}) custom-call(s32[152]{0:T(256)S(1)} %pad_add_fusion.refs_0_, ...), custom_call_target="tpu_custom_call", output_to_operand_aliasing={{0}: (3, {}), {1}: (4, {}), {2}: (5, {}), {3}: (6, {})} | custom-call | bytes 4194304 | tf_op jit(solution)/shard_map/tiles_14/pallas_call | solution.py:108
  82.8 3.5 %collective-permute-done.12.refs_1_ = bf16[256,1024]{1,0:T(8,128)(2,1)S(1)} collective-permute-done((bf16[256,1024]{1,0:T(8,128)(2,1)S(1)}, bf16[256,1024]{1,0:T(8,128)(2,1)S(1)}, u32[]{:S(2)}, u32[]{:S(2)}) %collective-permute-start.12) | collective-permute-done | bytes 524320 | tf_op jit(solution)/shard_map/ppermute | solution.py:242
  87.7 2.6 %collective-permute-done.14 = bf16[32,128,128]{2,1,0:T(8,128)(2,1)S(1)} collective-permute-done((bf16[32,128,128]{2,1,0:T(8,128)(2,1)S(1)}, bf16[32,128,128]{2,1,0:T(8,128)(2,1)S(1)}, u32[]{:S(2)}, u32[]{:S(2)}) %collective-permute-start.14) | collective-permute-done | bytes 1048608 | tf_op jit(solution)/shard_map/ppermute | solution.py:146
  93.3 6.9 %collective-permute-done.16 = bf16[16,128,128]{2,1,0:T(8,128)(2,1)S(1)} collective-permute-done((bf16[16,128,128]{2,1,0:T(8,128)(2,1)S(1)}, bf16[16,128,128]{2,1,0:T(8,128)(2,1)S(1)}, u32[]{:S(2)}, u32[]{:S(2)}) %collective-permute-start.16) | collective-permute-done | bytes 524320 | tf_op jit(solution)/shard_map/ppermute | solution.py:146
  104.1 4.3 %collective-permute-done.18 = bf16[8,128,128]{2,1,0:T(8,128)(2,1)S(1)} collective-permute-done((bf16[8,128,128]{2,1,0:T(8,128)(2,1)S(1)}, bf16[8,128,128]{2,1,0:T(8,128)(2,1)S(1)}, u32[]{:S(2)}, u32[]{:S(2)}) %collective-permute-start.18) | collective-permute-done | bytes 262176 | tf_op jit(solution)/shard_map/ppermute | solution.py:146
  110.2 3.3 %collective-permute-start.20 = (bf16[4,128,128]{2,1,0:T(8,128)(2,1)S(1)}, bf16[4,128,128]{2,1,0:T(8,128)(2,1)S(1)}, u32[]{:S(2)}, u32[]{:S(2)}) collective-permute-start(bf16[4,128,128]{2,1,0:T(8,128)(2,1)S(1)} %get-tuple-element.287), channel_id=1, source_target_pairs={{0,32},{8,136},{16,48},{24,152},{32,0},{40,168},{48,16},{56,184},{... | collective-permute-start | bytes 393224 | tf_op jit(solution)/shard_map/ppermute | solution.py:146
  114.6 2.2 %collective-permute-done.20 = bf16[4,128,128]{2,1,0:T(8,128)(2,1)S(1)} collective-permute-done((bf16[4,128,128]{2,1,0:T(8,128)(2,1)S(1)}, bf16[4,128,128]{2,1,0:T(8,128)(2,1)S(1)}, u32[]{:S(2)}, u32[]{:S(2)}) %collective-permute-start.20) | collective-permute-done | bytes 131104 | tf_op jit(solution)/shard_map/ppermute | solution.py:146
  (75 shorter events, 41.0 us)
Async XLA Ops:
  0.0 13.2 %collective-permute-start = (bf16[256,1024]{1,0:T(8,128)(2,1)}, bf16[256,1024]{1,0:T(8,128)(2,1)S(1)}, u32[]{:S(2)}, u32[]{:S(2)}) collective-permute-start(bf16[256,1024]{1,0:T(8,128)(2,1)} %refs_1_.2), channel_id=1, source_target_pairs={{0,1},{1,2},{2,3},{3,4},{4,5},{5,6},{6,7},{7,0},{8,15},{9,8},{10,9... | collective-permute-start | bytes 1572872 | tf_op jit(solution)/shard_map/ppermute | solution.py:242
  1.9 16.9 %collective-permute-start.1 = (bf16[256,1024]{1,0:T(8,128)(2,1)}, bf16[256,1024]{1,0:T(8,128)(2,1)S(1)}, u32[]{:S(2)}, u32[]{:S(2)}) collective-permute-start(bf16[256,1024]{1,0:T(8,128)(2,1)} %refs_1_.3), channel_id=1, source_target_pairs={{0,1},{1,2},{2,3},{3,4},{4,5},{5,6},{6,7},{7,0},{8,15},{9,8},{10,9... | collective-permute-start | bytes 1572872 | tf_op jit(solution)/shard_map/ppermute | solution.py:242
  14.0 5.4 %copy-start.4 = (bf16[256,1024]{1,0:T(8,128)(2,1)S(1)}, bf16[256,1024]{1,0:T(8,128)(2,1)}, u32[]{:S(2)}) copy-start(bf16[256,1024]{1,0:T(8,128)(2,1)} %refs_1_.3) | copy-start | bytes 1572868
  14.1 10.5 %collective-permute-start.3 = (bf16[256,1024]{1,0:T(8,128)(2,1)S(1)}, bf16[256,1024]{1,0:T(8,128)(2,1)S(1)}, u32[]{:S(2)}, u32[]{:S(2)}) collective-permute-start(bf16[256,1024]{1,0:T(8,128)(2,1)S(1)} %collective-permute-done.refs_1_), channel_id=1, source_target_pairs={{0,1},{1,2},{2,3},{3,4},{4,5},{5,6},{6,7},{7,0},{8,15},{9,8},{10,9... | collective-permute-start | bytes 1572872 | tf_op jit(solution)/shard_map/ppermute | solution.py:242
  18.8 11.3 %collective-permute-start.2 = (bf16[256,1024]{1,0:T(8,128)(2,1)S(1)}, bf16[256,1024]{1,0:T(8,128)(2,1)S(1)}, u32[]{:S(2)}, u32[]{:S(2)}) collective-permute-start(bf16[256,1024]{1,0:T(8,128)(2,1)S(1)} %collective-permute-done.1.refs_1_), channel_id=1, source_target_pairs={{0,1},{1,2},{2,3},{3,4},{4,5},{5,6},{6,7},{7,0},{8,15},{9,8},{10,9... | collective-permute-start | bytes 1572872 | tf_op jit(solution)/shard_map/ppermute | solution.py:242
  24.5 11.2 %collective-permute-start.5 = (bf16[256,1024]{1,0:T(8,128)(2,1)S(1)}, bf16[256,1024]{1,0:T(8,128)(2,1)S(1)}, u32[]{:S(2)}, u32[]{:S(2)}) collective-permute-start(bf16[256,1024]{1,0:T(8,128)(2,1)S(1)} %collective-permute-done.3.refs_1_), channel_id=1, source_target_pairs={{0,1},{1,2},{2,3},{3,4},{4,5},{5,6},{6,7},{7,0},{8,15},{9,8},{10,9... | collective-permute-start | bytes 1572872 | tf_op jit(solution)/shard_map/ppermute | solution.py:242
  30.1 11.2 %collective-permute-start.4 = (bf16[256,1024]{1,0:T(8,128)(2,1)S(1)}, bf16[256,1024]{1,0:T(8,128)(2,1)S(1)}, u32[]{:S(2)}, u32[]{:S(2)}) collective-permute-start(bf16[256,1024]{1,0:T(8,128)(2,1)S(1)} %collective-permute-done.2.refs_1_), channel_id=1, source_target_pairs={{0,1},{1,2},{2,3},{3,4},{4,5},{5,6},{6,7},{7,0},{8,15},{9,8},{10,9... | collective-permute-start | bytes 1572872 | tf_op jit(solution)/shard_map/ppermute | solution.py:242
  35.8 11.2 %collective-permute-start.7 = (bf16[256,1024]{1,0:T(8,128)(2,1)S(1)}, bf16[256,1024]{1,0:T(8,128)(2,1)S(1)}, u32[]{:S(2)}, u32[]{:S(2)}) collective-permute-start(bf16[256,1024]{1,0:T(8,128)(2,1)S(1)} %collective-permute-done.5.refs_1_), channel_id=1, source_target_pairs={{0,1},{1,2},{2,3},{3,4},{4,5},{5,6},{6,7},{7,0},{8,15},{9,8},{10,9... | collective-permute-start | bytes 1572872 | tf_op jit(solution)/shard_map/ppermute | solution.py:242
  41.4 11.2 %collective-permute-start.6 = (bf16[256,1024]{1,0:T(8,128)(2,1)S(1)}, bf16[256,1024]{1,0:T(8,128)(2,1)S(1)}, u32[]{:S(2)}, u32[]{:S(2)}) collective-permute-start(bf16[256,1024]{1,0:T(8,128)(2,1)S(1)} %collective-permute-done.4.refs_1_), channel_id=1, source_target_pairs={{0,1},{1,2},{2,3},{3,4},{4,5},{5,6},{6,7},{7,0},{8,15},{9,8},{10,9... | collective-permute-start | bytes 1572872 | tf_op jit(solution)/shard_map/ppermute | solution.py:242
  47.0 11.2 %collective-permute-start.9 = (bf16[256,1024]{1,0:T(8,128)(2,1)S(1)}, bf16[256,1024]{1,0:T(8,128)(2,1)S(1)}, u32[]{:S(2)}, u32[]{:S(2)}) collective-permute-start(bf16[256,1024]{1,0:T(8,128)(2,1)S(1)} %collective-permute-done.7.refs_1_), channel_id=1, source_target_pairs={{0,1},{1,2},{2,3},{3,4},{4,5},{5,6},{6,7},{7,0},{8,15},{9,8},{10,9... | collective-permute-start | bytes 1572872 | tf_op jit(solution)/shard_map/ppermute | solution.py:242
  52.6 11.2 %collective-permute-start.8 = (bf16[256,1024]{1,0:T(8,128)(2,1)S(1)}, bf16[256,1024]{1,0:T(8,128)(2,1)S(1)}, u32[]{:S(2)}, u32[]{:S(2)}) collective-permute-start(bf16[256,1024]{1,0:T(8,128)(2,1)S(1)} %collective-permute-done.6.refs_1_), channel_id=1, source_target_pairs={{0,1},{1,2},{2,3},{3,4},{4,5},{5,6},{6,7},{7,0},{8,15},{9,8},{10,9... | collective-permute-start | bytes 1572872 | tf_op jit(solution)/shard_map/ppermute | solution.py:242
  58.2 11.2 %collective-permute-start.11 = (bf16[256,1024]{1,0:T(8,128)(2,1)S(1)}, bf16[256,1024]{1,0:T(8,128)(2,1)S(1)}, u32[]{:S(2)}, u32[]{:S(2)}) collective-permute-start(bf16[256,1024]{1,0:T(8,128)(2,1)S(1)} %collective-permute-done.9.refs_1_), channel_id=1, source_target_pairs={{0,1},{1,2},{2,3},{3,4},{4,5},{5,6},{6,7},{7,0},{8,15},{9,8},{10,9... | collective-permute-start | bytes 1572872 | tf_op jit(solution)/shard_map/ppermute | solution.py:242
  63.9 11.2 %collective-permute-start.10 = (bf16[256,1024]{1,0:T(8,128)(2,1)S(1)}, bf16[256,1024]{1,0:T(8,128)(2,1)S(1)}, u32[]{:S(2)}, u32[]{:S(2)}) collective-permute-start(bf16[256,1024]{1,0:T(8,128)(2,1)S(1)} %collective-permute-done.8.refs_1_), channel_id=1, source_target_pairs={{0,1},{1,2},{2,3},{3,4},{4,5},{5,6},{6,7},{7,0},{8,15},{9,8},{10,9... | collective-permute-start | bytes 1572872 | tf_op jit(solution)/shard_map/ppermute | solution.py:242
  69.5 11.2 %collective-permute-start.13 = (bf16[256,1024]{1,0:T(8,128)(2,1)S(1)}, bf16[256,1024]{1,0:T(8,128)(2,1)S(1)}, u32[]{:S(2)}, u32[]{:S(2)}) collective-permute-start(bf16[256,1024]{1,0:T(8,128)(2,1)S(1)} %collective-permute-done.11.refs_1_), channel_id=1, source_target_pairs={{0,1},{1,2},{2,3},{3,4},{4,5},{5,6},{6,7},{7,0},{8,15},{9,8},{10,9... | collective-permute-start | bytes 1572872 | tf_op jit(solution)/shard_map/ppermute | solution.py:242
  75.1 11.2 %collective-permute-start.12 = (bf16[256,1024]{1,0:T(8,128)(2,1)S(1)}, bf16[256,1024]{1,0:T(8,128)(2,1)S(1)}, u32[]{:S(2)}, u32[]{:S(2)}) collective-permute-start(bf16[256,1024]{1,0:T(8,128)(2,1)S(1)} %collective-permute-done.10.refs_1_), channel_id=1, source_target_pairs={{0,1},{1,2},{2,3},{3,4},{4,5},{5,6},{6,7},{7,0},{8,15},{9,8},{10,9... | collective-permute-start | bytes 1572872 | tf_op jit(solution)/shard_map/ppermute | solution.py:242
  87.6 2.7 %collective-permute-start.14 = (bf16[32,128,128]{2,1,0:T(8,128)(2,1)S(1)}, bf16[32,128,128]{2,1,0:T(8,128)(2,1)S(1)}, u32[]{:S(2)}, u32[]{:S(2)}) collective-permute-start(bf16[32,128,128]{2,1,0:T(8,128)(2,1)S(1)} %get-tuple-element.273), channel_id=1, source_target_pairs={{0,8},{8,0},{16,24},{24,16},{32,40},{40,32},{48,56},{56,48},{64,72... | collective-permute-start | bytes 3145736 | tf_op jit(solution)/shard_map/ppermute | solution.py:146
  90.3 2.7 %collective-permute-start.15 = (bf16[32,128,128]{2,1,0:T(8,128)(2,1)S(1)}, bf16[32,128,128]{2,1,0:T(8,128)(2,1)S(1)}, u32[]{:S(2)}, u32[]{:S(2)}) collective-permute-start(bf16[32,128,128]{2,1,0:T(8,128)(2,1)S(1)} %get-tuple-element.274), channel_id=1, source_target_pairs={{0,8},{8,0},{16,24},{24,16},{32,40},{40,32},{48,56},{56,48},{64,72... | collective-permute-start | bytes 3145736 | tf_op jit(solution)/shard_map/ppermute | solution.py:146
  90.9 9.3 %collective-permute-start.16 = (bf16[16,128,128]{2,1,0:T(8,128)(2,1)S(1)}, bf16[16,128,128]{2,1,0:T(8,128)(2,1)S(1)}, u32[]{:S(2)}, u32[]{:S(2)}) collective-permute-start(bf16[16,128,128]{2,1,0:T(8,128)(2,1)S(1)} %get-tuple-element.277), channel_id=1, source_target_pairs={{0,64},{8,24},{16,80},{24,40},{32,96},{40,56},{48,112},{56,8},{64,... | collective-permute-start | bytes 1572872 | tf_op jit(solution)/shard_map/ppermute | solution.py:146
  91.5 10.4 %collective-permute-start.17 = (bf16[16,128,128]{2,1,0:T(8,128)(2,1)S(1)}, bf16[16,128,128]{2,1,0:T(8,128)(2,1)S(1)}, u32[]{:S(2)}, u32[]{:S(2)}) collective-permute-start(bf16[16,128,128]{2,1,0:T(8,128)(2,1)S(1)} %get-tuple-element.278), channel_id=1, source_target_pairs={{0,192},{8,56},{16,208},{24,8},{32,224},{40,24},{48,240},{56,40},{... | collective-permute-start | bytes 1572872 | tf_op jit(solution)/shard_map/ppermute | solution.py:146
  102.0 6.4 %collective-permute-start.18 = (bf16[8,128,128]{2,1,0:T(8,128)(2,1)S(1)}, bf16[8,128,128]{2,1,0:T(8,128)(2,1)S(1)}, u32[]{:S(2)}, u32[]{:S(2)}) collective-permute-start(bf16[8,128,128]{2,1,0:T(8,128)(2,1)S(1)} %get-tuple-element.282), channel_id=1, source_target_pairs={{0,64},{8,24},{16,80},{24,40},{32,96},{40,56},{48,112},{56,8},{64,... | collective-permute-start | bytes 786440 | tf_op jit(solution)/shard_map/ppermute | solution.py:146
  102.4 7.6 %collective-permute-start.19 = (bf16[8,128,128]{2,1,0:T(8,128)(2,1)S(1)}, bf16[8,128,128]{2,1,0:T(8,128)(2,1)S(1)}, u32[]{:S(2)}, u32[]{:S(2)}) collective-permute-start(bf16[8,128,128]{2,1,0:T(8,128)(2,1)S(1)} %get-tuple-element.283), channel_id=1, source_target_pairs={{0,192},{8,56},{16,208},{24,8},{32,224},{40,24},{48,240},{56,40},{... | collective-permute-start | bytes 786440 | tf_op jit(solution)/shard_map/ppermute | solution.py:146
  110.2 6.6 %collective-permute-start.20 = (bf16[4,128,128]{2,1,0:T(8,128)(2,1)S(1)}, bf16[4,128,128]{2,1,0:T(8,128)(2,1)S(1)}, u32[]{:S(2)}, u32[]{:S(2)}) collective-permute-start(bf16[4,128,128]{2,1,0:T(8,128)(2,1)S(1)} %get-tuple-element.287), channel_id=1, source_target_pairs={{0,32},{8,136},{16,48},{24,152},{32,0},{40,168},{48,16},{56,184},{... | collective-permute-start | bytes 393224 | tf_op jit(solution)/shard_map/ppermute | solution.py:146
  113.5 5.0 %collective-permute-start.21 = (bf16[4,128,128]{2,1,0:T(8,128)(2,1)S(1)}, bf16[4,128,128]{2,1,0:T(8,128)(2,1)S(1)}, u32[]{:S(2)}, u32[]{:S(2)}) collective-permute-start(bf16[4,128,128]{2,1,0:T(8,128)(2,1)S(1)} %unstack.25), channel_id=1, source_target_pairs={{0,16},{8,72},{16,0},{24,88},{32,48},{40,104},{48,32},{56,120},{64... | collective-permute-start | bytes 393224 | tf_op jit(solution)/shard_map/ppermute | solution.py:146
  114.2 6.2 %collective-permute-start.22 = (bf16[4,128,128]{2,1,0:T(8,128)(2,1)S(1)}, bf16[4,128,128]{2,1,0:T(8,128)(2,1)S(1)}, u32[]{:S(2)}, u32[]{:S(2)}) collective-permute-start(bf16[4,128,128]{2,1,0:T(8,128)(2,1)S(1)} %get-tuple-element.289), channel_id=1, source_target_pairs={{0,48},{8,200},{16,32},{24,216},{32,16},{40,232},{48,0},{56,248},{... | collective-permute-start | bytes 393224 | tf_op jit(solution)/shard_map/ppermute | solution.py:146
  (4 other events, 4.6 us)

commit v6 on v5

--- a/solution.py
+++ b/solution.py
@@ -12,7 +12,7 @@
 CAPO = 4
 UNROLL = 4
 PLACES = NX * NY * NC * CAPO
-GROUPS = ((0, 32), (32, 32), (64, 32), (96, 32))
+GROUPS = ((0, 16), (16, 48), (64, 16), (80, 48))
 F32, BF16 = jnp.float32, jnp.bfloat16
 ANY = pl.BlockSpec(memory_space=pl.ANY)
 
@@ -150,8 +150,8 @@
     x, y, c = place()
     p = jnp.arange(PLACES, dtype=jnp.int32)
     b = (p // 8) % 8
-    d1 = jnp.where((b == 1) | (b == 4), 1, jnp.where((b == 0) | (b == 2), 2, jnp.where(b < 6, 3, 0)))
-    upper = (b == 1) | (b == 2) | (b == 5) | (b == 7)
+    d1 = jnp.where(b < 2, 2, jnp.where(b < 4, 1, jnp.where(b < 6, 3, 0)))
+    upper = (b == 1) | (b == 3) | (b == 4) | (b == 7)
     d2 = (p // CAPO) % 2 + 2 * upper.astype(jnp.int32)
     to_c = jnp.where(p < 64, 1 - c, c)
     to_x = jnp.where(to_c == 0, (x + d1) % NX, x ^ d2)
@@ -186,23 +186,23 @@
     send_rest, got_now = tie((send_rest, got_now))
     got_rest = shift(send_rest, "core", 1)
     now = (own_now + got_now.astype(F32)).astype(BF16)
-    up, down = tie((now[:16], now[16:]))
+    up, down = tie((now[:8], now[8:]))
     up = shift(up, "first", 1)
     down = shift(down, "first", -1)
     rest = own_rest + got_rest.astype(F32)
     rest, up, down = tie((rest, up, down))
+    none = jnp.zeros_like(up)
     low, high = tie(
         (
-            (rest[:8] + up[:8].astype(F32)).astype(BF16),
-            (rest[8:16] + down[:8].astype(F32)).astype(BF16),
+            (rest[:16] + jnp.concatenate([up, none]).astype(F32)).astype(BF16),
+            (rest[16:32] + jnp.concatenate([down, none]).astype(F32)).astype(BF16),
         )
     )
     low = shift(low, "first", 1)
     high = shift(high, "first", -1)
     low, high = tie((low, high))
-    low = rest[16:24] + low.astype(F32) + down[8:].astype(F32)
-    high = rest[24:] + high.astype(F32) + up[8:].astype(F32)
-    total = (*low.reshape(2, CAPO, BS, BS), *high.reshape(2, CAPO, BS, BS))
+    here = rest[32:] + low.astype(F32) + jnp.concatenate([high[8:], high[:8]]).astype(F32)
+    total = here.reshape(4, CAPO, BS, BS)
     out, *sent = tie((total[0], *(total[k].astype(BF16) for k in (2, 1, 3))))
     got = tie(tuple(shift(value, "second", k) for value, k in zip(sent, (2, 1, 3))))
     for value in got:

time: 121 us -> 121 us (level)
  Pallas kernels: 25.6 us -> 24.2 us
    ppermute x14, waiting for transfers between devices: 50 us -> 51.5 us  [on_device(): chunks.append(lax.ppermute(value, ('tok', 'col'), ring))]
    pallas_call x16, Pallas kernels: 24 us -> 22.7 us  [make_tiles(): pl.pallas_call(body, in_specs=[pl.BlockSpec(memory_space=pltpu.SMEM), pl....]
    unnamed x12 -> x10, local copies, waits for them, and re-layouts: 4.43 us -> 3.54 us
  transfers between devices with their start and end apart: 23 -> 23, of which waited for: 22 -> 23; matrix products, arithmetic and copies ran while one was open for 3% -> 3% of each run, Pallas kernels for 20% -> 19%
where the time goes in v6:
time: 121 us; the launch traced here: 120 us
  waiting for transfers between devices  73.3 us (61%)
  Pallas kernels  24.2 us (20%)
  starting transfers between devices  13.7 us (11%)
  local copies, waits for them, and re-layouts  5.44 us (4%)
  other arithmetic  3.48 us (3%)
    ppermute x14, waiting for transfers between devices, on_device(): chunks.append(lax.ppermute(value, ('tok', 'col'), ring))  51.5 us
    pallas_call x16, Pallas kernels, make_tiles(): pl.pallas_call(body, in_specs=[pl.BlockSpec(memory_space=pltpu.SMEM), pl....  22.7 us
    ppermute x9, waiting for transfers between devices, shift(): return lax.ppermute(value, 'tok', pairs)  21.8 us
    ppermute x9, starting transfers between devices, shift(): return lax.ppermute(value, 'tok', pairs)  9 us
    ppermute x14, starting transfers between devices, on_device(): chunks.append(lax.ppermute(value, ('tok', 'col'), ring))  4.71 us
    unnamed x10, local copies, waits for them, and re-layouts  3.54 us
  transfers between devices with their start and end apart: 23, of which 23 were waited for; matrix products, arithmetic and copies ran while one was open for 3% of the time, Pallas kernels for 19%

profile of v6, /device:TPU:6, one launch (start us, length us, event | category | flops | bytes accessed | tf_op | source)
XLA Modules:
  0.0 120.5 jit_solution(9320696296364436899)
XLA Ops:
  0.0 1.9 %collective-permute-start = (bf16[256,1024]{1,0:T(8,128)(2,1)}, bf16[256,1024]{1,0:T(8,128)(2,1)S(1)}, u32[]{:S(2)}, u32[]{:S(2)}) collective-permute-start(bf16[256,1024]{1,0:T(8,128)(2,1)} %refs_1_.2), channel_id=1, source_target_pairs={{0,1},{1,2},{2,3},{3,4},{4,5},{5,6},{6,7},{7,0},{8,15},{9,8},{10,9... | collective-permute-start | bytes 1572872 | tf_op jit(solution)/shard_map/ppermute | solution.py:242
  1.9 1.9 %collective-permute-start.1 = (bf16[256,1024]{1,0:T(8,128)(2,1)}, bf16[256,1024]{1,0:T(8,128)(2,1)S(1)}, u32[]{:S(2)}, u32[]{:S(2)}) collective-permute-start(bf16[256,1024]{1,0:T(8,128)(2,1)} %refs_1_.3), channel_id=1, source_target_pairs={{0,1},{1,2},{2,3},{3,4},{4,5},{5,6},{6,7},{7,0},{8,15},{9,8},{10,9... | collective-permute-start | bytes 1572872 | tf_op jit(solution)/shard_map/ppermute | solution.py:242
  11.3 1.9 %collective-permute-done.refs_1_ = bf16[256,1024]{1,0:T(8,128)(2,1)S(1)} collective-permute-done((bf16[256,1024]{1,0:T(8,128)(2,1)}, bf16[256,1024]{1,0:T(8,128)(2,1)S(1)}, u32[]{:S(2)}, u32[]{:S(2)}) %collective-permute-start) | collective-permute-done | bytes 524320 | tf_op jit(solution)/shard_map/ppermute | solution.py:242
  15.7 3.2 %collective-permute-done.1.refs_1_ = bf16[256,1024]{1,0:T(8,128)(2,1)S(1)} collective-permute-done((bf16[256,1024]{1,0:T(8,128)(2,1)}, bf16[256,1024]{1,0:T(8,128)(2,1)S(1)}, u32[]{:S(2)}, u32[]{:S(2)}) %collective-permute-start.1) | collective-permute-done | bytes 524320 | tf_op jit(solution)/shard_map/ppermute | solution.py:242
  21.0 3.5 %collective-permute-done.3.refs_1_ = bf16[256,1024]{1,0:T(8,128)(2,1)S(1)} collective-permute-done((bf16[256,1024]{1,0:T(8,128)(2,1)S(1)}, bf16[256,1024]{1,0:T(8,128)(2,1)S(1)}, u32[]{:S(2)}, u32[]{:S(2)}) %collective-permute-start.3) | collective-permute-done | bytes 524320 | tf_op jit(solution)/shard_map/ppermute | solution.py:242
  25.7 4.3 %collective-permute-done.2.refs_1_ = bf16[256,1024]{1,0:T(8,128)(2,1)S(1)} collective-permute-done((bf16[256,1024]{1,0:T(8,128)(2,1)S(1)}, bf16[256,1024]{1,0:T(8,128)(2,1)S(1)}, u32[]{:S(2)}, u32[]{:S(2)}) %collective-permute-start.2) | collective-permute-done | bytes 524320 | tf_op jit(solution)/shard_map/ppermute | solution.py:242
  31.5 4.2 %collective-permute-done.5.refs_1_ = bf16[256,1024]{1,0:T(8,128)(2,1)S(1)} collective-permute-done((bf16[256,1024]{1,0:T(8,128)(2,1)S(1)}, bf16[256,1024]{1,0:T(8,128)(2,1)S(1)}, u32[]{:S(2)}, u32[]{:S(2)}) %collective-permute-start.5) | collective-permute-done | bytes 524320 | tf_op jit(solution)/shard_map/ppermute | solution.py:242
  37.0 4.3 %collective-permute-done.4.refs_1_ = bf16[256,1024]{1,0:T(8,128)(2,1)S(1)} collective-permute-done((bf16[256,1024]{1,0:T(8,128)(2,1)S(1)}, bf16[256,1024]{1,0:T(8,128)(2,1)S(1)}, u32[]{:S(2)}, u32[]{:S(2)}) %collective-permute-start.4) | collective-permute-done | bytes 524320 | tf_op jit(solution)/shard_map/ppermute | solution.py:242
  42.8 4.2 %collective-permute-done.7.refs_1_ = bf16[256,1024]{1,0:T(8,128)(2,1)S(1)} collective-permute-done((bf16[256,1024]{1,0:T(8,128)(2,1)S(1)}, bf16[256,1024]{1,0:T(8,128)(2,1)S(1)}, u32[]{:S(2)}, u32[]{:S(2)}) %collective-permute-start.7) | collective-permute-done | bytes 524320 | tf_op jit(solution)/shard_map/ppermute | solution.py:242
  48.5 4.1 %collective-permute-done.6.refs_1_ = bf16[256,1024]{1,0:T(8,128)(2,1)S(1)} collective-permute-done((bf16[256,1024]{1,0:T(8,128)(2,1)S(1)}, bf16[256,1024]{1,0:T(8,128)(2,1)S(1)}, u32[]{:S(2)}, u32[]{:S(2)}) %collective-permute-start.6) | collective-permute-done | bytes 524320 | tf_op jit(solution)/shard_map/ppermute | solution.py:242
  53.9 4.2 %collective-permute-done.9.refs_1_ = bf16[256,1024]{1,0:T(8,128)(2,1)S(1)} collective-permute-done((bf16[256,1024]{1,0:T(8,128)(2,1)S(1)}, bf16[256,1024]{1,0:T(8,128)(2,1)S(1)}, u32[]{:S(2)}, u32[]{:S(2)}) %collective-permute-start.9) | collective-permute-done | bytes 524320 | tf_op jit(solution)/shard_map/ppermute | solution.py:242
  59.5 4.3 %collective-permute-done.8.refs_1_ = bf16[256,1024]{1,0:T(8,128)(2,1)S(1)} collective-permute-done((bf16[256,1024]{1,0:T(8,128)(2,1)S(1)}, bf16[256,1024]{1,0:T(8,128)(2,1)S(1)}, u32[]{:S(2)}, u32[]{:S(2)}) %collective-permute-start.8) | collective-permute-done | bytes 524320 | tf_op jit(solution)/shard_map/ppermute | solution.py:242
  65.1 4.3 %collective-permute-done.11.refs_1_ = bf16[256,1024]{1,0:T(8,128)(2,1)S(1)} collective-permute-done((bf16[256,1024]{1,0:T(8,128)(2,1)S(1)}, bf16[256,1024]{1,0:T(8,128)(2,1)S(1)}, u32[]{:S(2)}, u32[]{:S(2)}) %collective-permute-start.11) | collective-permute-done | bytes 524320 | tf_op jit(solution)/shard_map/ppermute | solution.py:242
  70.9 4.1 %collective-permute-done.10.refs_1_ = bf16[256,1024]{1,0:T(8,128)(2,1)S(1)} collective-permute-done((bf16[256,1024]{1,0:T(8,128)(2,1)S(1)}, bf16[256,1024]{1,0:T(8,128)(2,1)S(1)}, u32[]{:S(2)}, u32[]{:S(2)}) %collective-permute-start.10) | collective-permute-done | bytes 524320 | tf_op jit(solution)/shard_map/ppermute | solution.py:242
  76.3 2.2 %tiles_12.1 = (bf16[16,128,128]{2,1,0:T(8,128)(2,1)S(1)}, bf16[48,128,128]{2,1,0:T(8,128)(2,1)S(1)}, f32[16,128,128]{2,1,0:T(8,128)S(1)}, f32[48,128,128]{2,1,0:T(8,128)S(1)}) custom-call(s32[152]{0:T(256)S(1)} %pad_add_fusion.refs_0_, ...), custom_call_target="tpu_custom_call", output_to_operand_aliasing={{0}: (3, {}), {1}: (4, {}), {2}: (5, {}), {3}: (6, {})} | custom-call | bytes 4194304 | tf_op jit(solution)/shard_map/tiles_12/pallas_call | solution.py:108
  80.6 2.0 %tiles_14.1 = (bf16[16,128,128]{2,1,0:T(8,128)(2,1)S(1)}, bf16[48,128,128]{2,1,0:T(8,128)(2,1)S(1)}, f32[16,128,128]{2,1,0:T(8,128)S(1)}, f32[48,128,128]{2,1,0:T(8,128)S(1)}) custom-call(s32[152]{0:T(256)S(1)} %pad_add_fusion.refs_0_, ...), custom_call_target="tpu_custom_call", output_to_operand_aliasing={{0}: (3, {}), {1}: (4, {}), {2}: (5, {}), {3}: (6, {})} | custom-call | bytes 4194304 | tf_op jit(solution)/shard_map/tiles_14/pallas_call | solution.py:108
  82.7 3.6 %collective-permute-done.12.refs_1_ = bf16[256,1024]{1,0:T(8,128)(2,1)S(1)} collective-permute-done((bf16[256,1024]{1,0:T(8,128)(2,1)S(1)}, bf16[256,1024]{1,0:T(8,128)(2,1)S(1)}, u32[]{:S(2)}, u32[]{:S(2)}) %collective-permute-start.12) | collective-permute-done | bytes 524320 | tf_op jit(solution)/shard_map/ppermute | solution.py:242
  87.8 1.9 %collective-permute-done.14 = bf16[16,128,128]{2,1,0:T(8,128)(2,1)S(1)} collective-permute-done((bf16[16,128,128]{2,1,0:T(8,128)(2,1)S(1)}, bf16[16,128,128]{2,1,0:T(8,128)(2,1)S(1)}, u32[]{:S(2)}, u32[]{:S(2)}) %collective-permute-start.14) | collective-permute-done | bytes 524320 | tf_op jit(solution)/shard_map/ppermute | solution.py:146
  93.8 2.7 %collective-permute-done.16 = bf16[8,128,128]{2,1,0:T(8,128)(2,1)S(1)} collective-permute-done((bf16[8,128,128]{2,1,0:T(8,128)(2,1)S(1)}, bf16[8,128,128]{2,1,0:T(8,128)(2,1)S(1)}, u32[]{:S(2)}, u32[]{:S(2)}) %collective-permute-start.16) | collective-permute-done | bytes 262176 | tf_op jit(solution)/shard_map/ppermute | solution.py:146
  98.8 1.7 %collective-permute-start.19 = (bf16[16,128,128]{2,1,0:T(8,128)(2,1)S(1)}, bf16[16,128,128]{2,1,0:T(8,128)(2,1)S(1)}, u32[]{:S(2)}, u32[]{:S(2)}) collective-permute-start(bf16[16,128,128]{2,1,0:T(8,128)(2,1)S(1)} %get-tuple-element.283), channel_id=1, source_target_pairs={{0,192},{8,56},{16,208},{24,8},{32,224},{40,24},{48,240},{56,40},{... | collective-permute-start | bytes 1572872 | tf_op jit(solution)/shard_map/ppermute | solution.py:146
  100.6 7.2 %collective-permute-done.18 = bf16[16,128,128]{2,1,0:T(8,128)(2,1)S(1)} collective-permute-done((bf16[16,128,128]{2,1,0:T(8,128)(2,1)S(1)}, bf16[16,128,128]{2,1,0:T(8,128)(2,1)S(1)}, u32[]{:S(2)}, u32[]{:S(2)}) %collective-permute-start.18) | collective-permute-done | bytes 524320 | tf_op jit(solution)/shard_map/ppermute | solution.py:146
  109.6 3.3 %collective-permute-start.20 = (bf16[4,128,128]{2,1,0:T(8,128)(2,1)S(1)}, bf16[4,128,128]{2,1,0:T(8,128)(2,1)S(1)}, u32[]{:S(2)}, u32[]{:S(2)}) collective-permute-start(bf16[4,128,128]{2,1,0:T(8,128)(2,1)S(1)} %get-tuple-element.287), channel_id=1, source_target_pairs={{0,32},{8,136},{16,48},{24,152},{32,0},{40,168},{48,16},{56,184},{... | collective-permute-start | bytes 393224 | tf_op jit(solution)/shard_map/ppermute | solution.py:146
  113.9 2.2 %collective-permute-done.20 = bf16[4,128,128]{2,1,0:T(8,128)(2,1)S(1)} collective-permute-done((bf16[4,128,128]{2,1,0:T(8,128)(2,1)S(1)}, bf16[4,128,128]{2,1,0:T(8,128)(2,1)S(1)}, u32[]{:S(2)}, u32[]{:S(2)}) %collective-permute-start.20) | collective-permute-done | bytes 131104 | tf_op jit(solution)/shard_map/ppermute | solution.py:146
  117.9 1.8 %collective-permute-done.22 = bf16[4,128,128]{2,1,0:T(8,128)(2,1)S(1)} collective-permute-done((bf16[4,128,128]{2,1,0:T(8,128)(2,1)S(1)}, bf16[4,128,128]{2,1,0:T(8,128)(2,1)S(1)}, u32[]{:S(2)}, u32[]{:S(2)}) %collective-permute-start.22) | collective-permute-done | bytes 131104 | tf_op jit(solution)/shard_map/ppermute | solution.py:146
  (75 shorter events, 41.2 us)
Async XLA Ops:
  0.0 13.2 %collective-permute-start = (bf16[256,1024]{1,0:T(8,128)(2,1)}, bf16[256,1024]{1,0:T(8,128)(2,1)S(1)}, u32[]{:S(2)}, u32[]{:S(2)}) collective-permute-start(bf16[256,1024]{1,0:T(8,128)(2,1)} %refs_1_.2), channel_id=1, source_target_pairs={{0,1},{1,2},{2,3},{3,4},{4,5},{5,6},{6,7},{7,0},{8,15},{9,8},{10,9... | collective-permute-start | bytes 1572872 | tf_op jit(solution)/shard_map/ppermute | solution.py:242
  1.9 16.9 %collective-permute-start.1 = (bf16[256,1024]{1,0:T(8,128)(2,1)}, bf16[256,1024]{1,0:T(8,128)(2,1)S(1)}, u32[]{:S(2)}, u32[]{:S(2)}) collective-permute-start(bf16[256,1024]{1,0:T(8,128)(2,1)} %refs_1_.3), channel_id=1, source_target_pairs={{0,1},{1,2},{2,3},{3,4},{4,5},{5,6},{6,7},{7,0},{8,15},{9,8},{10,9... | collective-permute-start | bytes 1572872 | tf_op jit(solution)/shard_map/ppermute | solution.py:242
  13.2 11.2 %collective-permute-start.3 = (bf16[256,1024]{1,0:T(8,128)(2,1)S(1)}, bf16[256,1024]{1,0:T(8,128)(2,1)S(1)}, u32[]{:S(2)}, u32[]{:S(2)}) collective-permute-start(bf16[256,1024]{1,0:T(8,128)(2,1)S(1)} %collective-permute-done.refs_1_), channel_id=1, source_target_pairs={{0,1},{1,2},{2,3},{3,4},{4,5},{5,6},{6,7},{7,0},{8,15},{9,8},{10,9... | collective-permute-start | bytes 1572872 | tf_op jit(solution)/shard_map/ppermute | solution.py:242
  14.3 5.3 %copy-start.4 = (bf16[256,1024]{1,0:T(8,128)(2,1)S(1)}, bf16[256,1024]{1,0:T(8,128)(2,1)}, u32[]{:S(2)}) copy-start(bf16[256,1024]{1,0:T(8,128)(2,1)} %refs_1_.3) | copy-start | bytes 1572868
  18.8 11.2 %collective-permute-start.2 = (bf16[256,1024]{1,0:T(8,128)(2,1)S(1)}, bf16[256,1024]{1,0:T(8,128)(2,1)S(1)}, u32[]{:S(2)}, u32[]{:S(2)}) collective-permute-start(bf16[256,1024]{1,0:T(8,128)(2,1)S(1)} %collective-permute-done.1.refs_1_), channel_id=1, source_target_pairs={{0,1},{1,2},{2,3},{3,4},{4,5},{5,6},{6,7},{7,0},{8,15},{9,8},{10,9... | collective-permute-start | bytes 1572872 | tf_op jit(solution)/shard_map/ppermute | solution.py:242
  24.5 11.2 %collective-permute-start.5 = (bf16[256,1024]{1,0:T(8,128)(2,1)S(1)}, bf16[256,1024]{1,0:T(8,128)(2,1)S(1)}, u32[]{:S(2)}, u32[]{:S(2)}) collective-permute-start(bf16[256,1024]{1,0:T(8,128)(2,1)S(1)} %collective-permute-done.3.refs_1_), channel_id=1, source_target_pairs={{0,1},{1,2},{2,3},{3,4},{4,5},{5,6},{6,7},{7,0},{8,15},{9,8},{10,9... | collective-permute-start | bytes 1572872 | tf_op jit(solution)/shard_map/ppermute | solution.py:242
  30.1 11.2 %collective-permute-start.4 = (bf16[256,1024]{1,0:T(8,128)(2,1)S(1)}, bf16[256,1024]{1,0:T(8,128)(2,1)S(1)}, u32[]{:S(2)}, u32[]{:S(2)}) collective-permute-start(bf16[256,1024]{1,0:T(8,128)(2,1)S(1)} %collective-permute-done.2.refs_1_), channel_id=1, source_target_pairs={{0,1},{1,2},{2,3},{3,4},{4,5},{5,6},{6,7},{7,0},{8,15},{9,8},{10,9... | collective-permute-start | bytes 1572872 | tf_op jit(solution)/shard_map/ppermute | solution.py:242
  35.7 11.2 %collective-permute-start.7 = (bf16[256,1024]{1,0:T(8,128)(2,1)S(1)}, bf16[256,1024]{1,0:T(8,128)(2,1)S(1)}, u32[]{:S(2)}, u32[]{:S(2)}) collective-permute-start(bf16[256,1024]{1,0:T(8,128)(2,1)S(1)} %collective-permute-done.5.refs_1_), channel_id=1, source_target_pairs={{0,1},{1,2},{2,3},{3,4},{4,5},{5,6},{6,7},{7,0},{8,15},{9,8},{10,9... | collective-permute-start | bytes 1572872 | tf_op jit(solution)/shard_map/ppermute | solution.py:242
  41.3 11.2 %collective-permute-start.6 = (bf16[256,1024]{1,0:T(8,128)(2,1)S(1)}, bf16[256,1024]{1,0:T(8,128)(2,1)S(1)}, u32[]{:S(2)}, u32[]{:S(2)}) collective-permute-start(bf16[256,1024]{1,0:T(8,128)(2,1)S(1)} %collective-permute-done.4.refs_1_), channel_id=1, source_target_pairs={{0,1},{1,2},{2,3},{3,4},{4,5},{5,6},{6,7},{7,0},{8,15},{9,8},{10,9... | collective-permute-start | bytes 1572872 | tf_op jit(solution)/shard_map/ppermute | solution.py:242
  46.9 11.2 %collective-permute-start.9 = (bf16[256,1024]{1,0:T(8,128)(2,1)S(1)}, bf16[256,1024]{1,0:T(8,128)(2,1)S(1)}, u32[]{:S(2)}, u32[]{:S(2)}) collective-permute-start(bf16[256,1024]{1,0:T(8,128)(2,1)S(1)} %collective-permute-done.7.refs_1_), channel_id=1, source_target_pairs={{0,1},{1,2},{2,3},{3,4},{4,5},{5,6},{6,7},{7,0},{8,15},{9,8},{10,9... | collective-permute-start | bytes 1572872 | tf_op jit(solution)/shard_map/ppermute | solution.py:242
  52.5 11.2 %collective-permute-start.8 = (bf16[256,1024]{1,0:T(8,128)(2,1)S(1)}, bf16[256,1024]{1,0:T(8,128)(2,1)S(1)}, u32[]{:S(2)}, u32[]{:S(2)}) collective-permute-start(bf16[256,1024]{1,0:T(8,128)(2,1)S(1)} %collective-permute-done.6.refs_1_), channel_id=1, source_target_pairs={{0,1},{1,2},{2,3},{3,4},{4,5},{5,6},{6,7},{7,0},{8,15},{9,8},{10,9... | collective-permute-start | bytes 1572872 | tf_op jit(solution)/shard_map/ppermute | solution.py:242
  58.2 11.2 %collective-permute-start.11 = (bf16[256,1024]{1,0:T(8,128)(2,1)S(1)}, bf16[256,1024]{1,0:T(8,128)(2,1)S(1)}, u32[]{:S(2)}, u32[]{:S(2)}) collective-permute-start(bf16[256,1024]{1,0:T(8,128)(2,1)S(1)} %collective-permute-done.9.refs_1_), channel_id=1, source_target_pairs={{0,1},{1,2},{2,3},{3,4},{4,5},{5,6},{6,7},{7,0},{8,15},{9,8},{10,9... | collective-permute-start | bytes 1572872 | tf_op jit(solution)/shard_map/ppermute | solution.py:242
  63.8 11.2 %collective-permute-start.10 = (bf16[256,1024]{1,0:T(8,128)(2,1)S(1)}, bf16[256,1024]{1,0:T(8,128)(2,1)S(1)}, u32[]{:S(2)}, u32[]{:S(2)}) collective-permute-start(bf16[256,1024]{1,0:T(8,128)(2,1)S(1)} %collective-permute-done.8.refs_1_), channel_id=1, source_target_pairs={{0,1},{1,2},{2,3},{3,4},{4,5},{5,6},{6,7},{7,0},{8,15},{9,8},{10,9... | collective-permute-start | bytes 1572872 | tf_op jit(solution)/shard_map/ppermute | solution.py:242
  69.4 11.2 %collective-permute-start.13 = (bf16[256,1024]{1,0:T(8,128)(2,1)S(1)}, bf16[256,1024]{1,0:T(8,128)(2,1)S(1)}, u32[]{:S(2)}, u32[]{:S(2)}) collective-permute-start(bf16[256,1024]{1,0:T(8,128)(2,1)S(1)} %collective-permute-done.11.refs_1_), channel_id=1, source_target_pairs={{0,1},{1,2},{2,3},{3,4},{4,5},{5,6},{6,7},{7,0},{8,15},{9,8},{10,9... | collective-permute-start | bytes 1572872 | tf_op jit(solution)/shard_map/ppermute | solution.py:242
  75.0 11.2 %collective-permute-start.12 = (bf16[256,1024]{1,0:T(8,128)(2,1)S(1)}, bf16[256,1024]{1,0:T(8,128)(2,1)S(1)}, u32[]{:S(2)}, u32[]{:S(2)}) collective-permute-start(bf16[256,1024]{1,0:T(8,128)(2,1)S(1)} %collective-permute-done.10.refs_1_), channel_id=1, source_target_pairs={{0,1},{1,2},{2,3},{3,4},{4,5},{5,6},{6,7},{7,0},{8,15},{9,8},{10,9... | collective-permute-start | bytes 1572872 | tf_op jit(solution)/shard_map/ppermute | solution.py:242
  87.5 2.2 %collective-permute-start.14 = (bf16[16,128,128]{2,1,0:T(8,128)(2,1)S(1)}, bf16[16,128,128]{2,1,0:T(8,128)(2,1)S(1)}, u32[]{:S(2)}, u32[]{:S(2)}) collective-permute-start(bf16[16,128,128]{2,1,0:T(8,128)(2,1)S(1)} %get-tuple-element.273), channel_id=1, source_target_pairs={{0,8},{8,0},{16,24},{24,16},{32,40},{40,32},{48,56},{56,48},{64,72... | collective-permute-start | bytes 1572872 | tf_op jit(solution)/shard_map/ppermute | solution.py:146
  89.7 3.4 %collective-permute-start.15 = (bf16[48,128,128]{2,1,0:T(8,128)(2,1)S(1)}, bf16[48,128,128]{2,1,0:T(8,128)(2,1)S(1)}, u32[]{:S(2)}, u32[]{:S(2)}) collective-permute-start(bf16[48,128,128]{2,1,0:T(8,128)(2,1)S(1)} %get-tuple-element.274), channel_id=1, source_target_pairs={{0,8},{8,0},{16,24},{24,16},{32,40},{40,32},{48,56},{56,48},{64,72... | collective-permute-start | bytes 4718600 | tf_op jit(solution)/shard_map/ppermute | solution.py:146
  90.1 6.4 %collective-permute-start.16 = (bf16[8,128,128]{2,1,0:T(8,128)(2,1)S(1)}, bf16[8,128,128]{2,1,0:T(8,128)(2,1)S(1)}, u32[]{:S(2)}, u32[]{:S(2)}) collective-permute-start(bf16[8,128,128]{2,1,0:T(8,128)(2,1)S(1)} %get-tuple-element.277), channel_id=1, source_target_pairs={{0,64},{8,24},{16,80},{24,40},{32,96},{40,56},{48,112},{56,8},{64,... | collective-permute-start | bytes 786440 | tf_op jit(solution)/shard_map/ppermute | solution.py:146
  90.6 7.6 %collective-permute-start.17 = (bf16[8,128,128]{2,1,0:T(8,128)(2,1)S(1)}, bf16[8,128,128]{2,1,0:T(8,128)(2,1)S(1)}, u32[]{:S(2)}, u32[]{:S(2)}) collective-permute-start(bf16[8,128,128]{2,1,0:T(8,128)(2,1)S(1)} %get-tuple-element.278), channel_id=1, source_target_pairs={{0,192},{8,56},{16,208},{24,8},{32,224},{40,24},{48,240},{56,40},{... | collective-permute-start | bytes 786440 | tf_op jit(solution)/shard_map/ppermute | solution.py:146
  98.5 9.3 %collective-permute-start.18 = (bf16[16,128,128]{2,1,0:T(8,128)(2,1)S(1)}, bf16[16,128,128]{2,1,0:T(8,128)(2,1)S(1)}, u32[]{:S(2)}, u32[]{:S(2)}) collective-permute-start(bf16[16,128,128]{2,1,0:T(8,128)(2,1)S(1)} %get-tuple-element.282), channel_id=1, source_target_pairs={{0,64},{8,24},{16,80},{24,40},{32,96},{40,56},{48,112},{56,8},{64,... | collective-permute-start | bytes 1572872 | tf_op jit(solution)/shard_map/ppermute | solution.py:146
  98.8 10.4 %collective-permute-start.19 = (bf16[16,128,128]{2,1,0:T(8,128)(2,1)S(1)}, bf16[16,128,128]{2,1,0:T(8,128)(2,1)S(1)}, u32[]{:S(2)}, u32[]{:S(2)}) collective-permute-start(bf16[16,128,128]{2,1,0:T(8,128)(2,1)S(1)} %get-tuple-element.283), channel_id=1, source_target_pairs={{0,192},{8,56},{16,208},{24,8},{32,224},{40,24},{48,240},{56,40},{... | collective-permute-start | bytes 1572872 | tf_op jit(solution)/shard_map/ppermute | solution.py:146
  109.6 6.6 %collective-permute-start.20 = (bf16[4,128,128]{2,1,0:T(8,128)(2,1)S(1)}, bf16[4,128,128]{2,1,0:T(8,128)(2,1)S(1)}, u32[]{:S(2)}, u32[]{:S(2)}) collective-permute-start(bf16[4,128,128]{2,1,0:T(8,128)(2,1)S(1)} %get-tuple-element.287), channel_id=1, source_target_pairs={{0,32},{8,136},{16,48},{24,152},{32,0},{40,168},{48,16},{56,184},{... | collective-permute-start | bytes 393224 | tf_op jit(solution)/shard_map/ppermute | solution.py:146
  112.9 5.0 %collective-permute-start.21 = (bf16[4,128,128]{2,1,0:T(8,128)(2,1)S(1)}, bf16[4,128,128]{2,1,0:T(8,128)(2,1)S(1)}, u32[]{:S(2)}, u32[]{:S(2)}) collective-permute-start(bf16[4,128,128]{2,1,0:T(8,128)(2,1)S(1)} %get-tuple-element.288), channel_id=1, source_target_pairs={{0,16},{8,72},{16,0},{24,88},{32,48},{40,104},{48,32},{56,120},{64... | collective-permute-start | bytes 393224 | tf_op jit(solution)/shard_map/ppermute | solution.py:146
  113.5 6.2 %collective-permute-start.22 = (bf16[4,128,128]{2,1,0:T(8,128)(2,1)S(1)}, bf16[4,128,128]{2,1,0:T(8,128)(2,1)S(1)}, u32[]{:S(2)}, u32[]{:S(2)}) collective-permute-start(bf16[4,128,128]{2,1,0:T(8,128)(2,1)S(1)} %get-tuple-element.289), channel_id=1, source_target_pairs={{0,48},{8,200},{16,32},{24,216},{32,16},{40,232},{48,0},{56,248},{... | collective-permute-start | bytes 393224 | tf_op jit(solution)/shard_map/ppermute | solution.py:146
  (4 other events, 4.6 us)

commit v7 on v6

--- a/solution.py
+++ b/solution.py
@@ -50,8 +50,9 @@
 
 def tile_kernel(segment, scale, tab_ref, chunk_ref, hid_ref, *refs):
     outs, (stage, stage16, sems) = refs[-7:-3], refs[-3:]
+    unroll = 2 if segment % 2 else UNROLL
     begin, end = tab_ref[PLACES + segment], tab_ref[PLACES + segment + 1]
-    rounds = (end - begin + UNROLL - 1) // UNROLL
+    rounds = (end - begin + unroll - 1) // unroll
 
     def tile(i):
         entry = tab_ref[jnp.minimum(i, end - 1)] // PLACES
@@ -62,8 +63,8 @@
         return out * scale
 
     def each_copy(n, k, act):
-        i = begin + n * UNROLL + k
-        at = (n % 2) * UNROLL + k
+        i = begin + n * unroll + k
+        at = (n % 2) * unroll + k
         p = tab_ref[jnp.minimum(i, end - 1)] % PLACES
         for g, (base, size) in enumerate(GROUPS):
 
@@ -81,14 +82,14 @@
     def body(n, carry):
         @pl.when(n >= 2)
         def _():
-            for k in range(UNROLL):
+            for k in range(unroll):
                 each_copy(n - 2, k, wait)
 
-        made = [tile(begin + n * UNROLL + k) for k in range(UNROLL)]
-        for k in range(UNROLL):
-            stage[(n % 2) * UNROLL + k] = made[k]
-            stage16[(n % 2) * UNROLL + k] = made[k].astype(BF16)
-        for k in range(UNROLL):
+        made = [tile(begin + n * unroll + k) for k in range(unroll)]
+        for k in range(unroll):
+            stage[(n % 2) * unroll + k] = made[k]
+            stage16[(n % 2) * unroll + k] = made[k].astype(BF16)
+        for k in range(unroll):
             each_copy(n, k, start)
         return carry
 
@@ -97,7 +98,7 @@
 
         @pl.when(rounds >= back)
         def _():
-            for k in range(UNROLL):
+            for k in range(unroll):
                 each_copy(rounds - back, k, wait)
 
 

time: 121 us -> 120 us (level)
  transfers between devices with their start and end apart: 23 -> 23, of which waited for: 23 -> 23; matrix products, arithmetic and copies ran while one was open for 3% -> 3% of each run, Pallas kernels for 19% -> 20%
where the time goes in v7:
time: 120 us
  waiting for transfers between devices  72.9 us (61%)
  Pallas kernels  25.2 us (21%)
  starting transfers between devices  12.9 us (11%)
  local copies, waits for them, and re-layouts  5.44 us (5%)
  other arithmetic  3.48 us (3%)
    ppermute x14, waiting for transfers between devices, on_device(): chunks.append(lax.ppermute(value, ('tok', 'col'), ring))  51.1 us
    pallas_call x16, Pallas kernels, make_tiles(): pl.pallas_call(body, in_specs=[pl.BlockSpec(memory_space=pltpu.SMEM), pl....  23.6 us
    ppermute x9, waiting for transfers between devices, shift(): return lax.ppermute(value, 'tok', pairs)  21.8 us
    ppermute x9, starting transfers between devices, shift(): return lax.ppermute(value, 'tok', pairs)  8.77 us
    ppermute x14, starting transfers between devices, on_device(): chunks.append(lax.ppermute(value, ('tok', 'col'), ring))  4.11 us
    unnamed x10, local copies, waits for them, and re-layouts  3.54 us
  transfers between devices with their start and end apart: 23, of which 23 were waited for; matrix products, arithmetic and copies ran while one was open for 3% of the time, Pallas kernels for 20%

profile of v7, /device:TPU:6, one launch (start us, length us, event | category | flops | bytes accessed | tf_op | source)
XLA Modules:
  0.0 120.2 jit_solution(986275386405880453)
XLA Ops:
  0.0 1.9 %collective-permute-start = (bf16[256,1024]{1,0:T(8,128)(2,1)}, bf16[256,1024]{1,0:T(8,128)(2,1)S(1)}, u32[]{:S(2)}, u32[]{:S(2)}) collective-permute-start(bf16[256,1024]{1,0:T(8,128)(2,1)} %refs_1_.2), channel_id=1, source_target_pairs={{0,1},{1,2},{2,3},{3,4},{4,5},{5,6},{6,7},{7,0},{8,15},{9,8},{10,9... | collective-permute-start | bytes 1572872 | tf_op jit(solution)/shard_map/ppermute | solution.py:243
  1.9 1.9 %collective-permute-start.1 = (bf16[256,1024]{1,0:T(8,128)(2,1)}, bf16[256,1024]{1,0:T(8,128)(2,1)S(1)}, u32[]{:S(2)}, u32[]{:S(2)}) collective-permute-start(bf16[256,1024]{1,0:T(8,128)(2,1)} %refs_1_.3), channel_id=1, source_target_pairs={{0,1},{1,2},{2,3},{3,4},{4,5},{5,6},{6,7},{7,0},{8,15},{9,8},{10,9... | collective-permute-start | bytes 1572872 | tf_op jit(solution)/shard_map/ppermute | solution.py:243
  11.3 1.9 %collective-permute-done.refs_1_ = bf16[256,1024]{1,0:T(8,128)(2,1)S(1)} collective-permute-done((bf16[256,1024]{1,0:T(8,128)(2,1)}, bf16[256,1024]{1,0:T(8,128)(2,1)S(1)}, u32[]{:S(2)}, u32[]{:S(2)}) %collective-permute-start) | collective-permute-done | bytes 524320 | tf_op jit(solution)/shard_map/ppermute | solution.py:243
  14.3 2.2 %tiles_0.1 = (bf16[16,128,128]{2,1,0:T(8,128)(2,1)S(1)}, bf16[48,128,128]{2,1,0:T(8,128)(2,1)S(1)}, f32[16,128,128]{2,1,0:T(8,128)S(1)}, f32[48,128,128]{2,1,0:T(8,128)S(1)}) custom-call(s32[152]{0:T(256)S(1)} %pad_add_fusion.refs_0_, bf16[256,1024]{1,0:T(8,128)(2,1)S(1)} %copy-done.3, ...), custom_call_target="tpu_custom_call", output_to_operand_aliasing={{0}: (3, {}), {1}: (4, {}), {2}: (5, {}), {3}: (6, {})} | custom-call | bytes 4194304 | tf_op jit(solution)/shard_map/tiles_0/pallas_call | solution.py:109
  16.5 2.4 %collective-permute-done.1.refs_1_ = bf16[256,1024]{1,0:T(8,128)(2,1)S(1)} collective-permute-done((bf16[256,1024]{1,0:T(8,128)(2,1)}, bf16[256,1024]{1,0:T(8,128)(2,1)S(1)}, u32[]{:S(2)}, u32[]{:S(2)}) %collective-permute-start.1) | collective-permute-done | bytes 524320 | tf_op jit(solution)/shard_map/ppermute | solution.py:243
  20.3 4.2 %collective-permute-done.3.refs_1_ = bf16[256,1024]{1,0:T(8,128)(2,1)S(1)} collective-permute-done((bf16[256,1024]{1,0:T(8,128)(2,1)S(1)}, bf16[256,1024]{1,0:T(8,128)(2,1)S(1)}, u32[]{:S(2)}, u32[]{:S(2)}) %collective-permute-start.3) | collective-permute-done | bytes 524320 | tf_op jit(solution)/shard_map/ppermute | solution.py:243
  24.5 2.1 %tiles_2.1 = (bf16[16,128,128]{2,1,0:T(8,128)(2,1)S(1)}, bf16[48,128,128]{2,1,0:T(8,128)(2,1)S(1)}, f32[16,128,128]{2,1,0:T(8,128)S(1)}, f32[48,128,128]{2,1,0:T(8,128)S(1)}) custom-call(s32[152]{0:T(256)S(1)} %pad_add_fusion.refs_0_, ...), custom_call_target="tpu_custom_call", output_to_operand_aliasing={{0}: (3, {}), {1}: (4, {}), {2}: (5, {}), {3}: (6, {})} | custom-call | bytes 4194304 | tf_op jit(solution)/shard_map/tiles_2/pallas_call | solution.py:109
  26.5 3.5 %collective-permute-done.2.refs_1_ = bf16[256,1024]{1,0:T(8,128)(2,1)S(1)} collective-permute-done((bf16[256,1024]{1,0:T(8,128)(2,1)S(1)}, bf16[256,1024]{1,0:T(8,128)(2,1)S(1)}, u32[]{:S(2)}, u32[]{:S(2)}) %collective-permute-start.2) | collective-permute-done | bytes 524320 | tf_op jit(solution)/shard_map/ppermute | solution.py:243
  31.3 4.4 %collective-permute-done.5.refs_1_ = bf16[256,1024]{1,0:T(8,128)(2,1)S(1)} collective-permute-done((bf16[256,1024]{1,0:T(8,128)(2,1)S(1)}, bf16[256,1024]{1,0:T(8,128)(2,1)S(1)}, u32[]{:S(2)}, u32[]{:S(2)}) %collective-permute-start.5) | collective-permute-done | bytes 524320 | tf_op jit(solution)/shard_map/ppermute | solution.py:243
  37.0 4.3 %collective-permute-done.4.refs_1_ = bf16[256,1024]{1,0:T(8,128)(2,1)S(1)} collective-permute-done((bf16[256,1024]{1,0:T(8,128)(2,1)S(1)}, bf16[256,1024]{1,0:T(8,128)(2,1)S(1)}, u32[]{:S(2)}, u32[]{:S(2)}) %collective-permute-start.4) | collective-permute-done | bytes 524320 | tf_op jit(solution)/shard_map/ppermute | solution.py:243
  42.6 4.4 %collective-permute-done.7.refs_1_ = bf16[256,1024]{1,0:T(8,128)(2,1)S(1)} collective-permute-done((bf16[256,1024]{1,0:T(8,128)(2,1)S(1)}, bf16[256,1024]{1,0:T(8,128)(2,1)S(1)}, u32[]{:S(2)}, u32[]{:S(2)}) %collective-permute-start.7) | collective-permute-done | bytes 524320 | tf_op jit(solution)/shard_map/ppermute | solution.py:243
  48.3 4.3 %collective-permute-done.6.refs_1_ = bf16[256,1024]{1,0:T(8,128)(2,1)S(1)} collective-permute-done((bf16[256,1024]{1,0:T(8,128)(2,1)S(1)}, bf16[256,1024]{1,0:T(8,128)(2,1)S(1)}, u32[]{:S(2)}, u32[]{:S(2)}) %collective-permute-start.6) | collective-permute-done | bytes 524320 | tf_op jit(solution)/shard_map/ppermute | solution.py:243
  52.6 2.2 %tiles_7.1 = (bf16[16,128,128]{2,1,0:T(8,128)(2,1)S(1)}, bf16[48,128,128]{2,1,0:T(8,128)(2,1)S(1)}, f32[16,128,128]{2,1,0:T(8,128)S(1)}, f32[48,128,128]{2,1,0:T(8,128)S(1)}) custom-call(s32[152]{0:T(256)S(1)} %pad_add_fusion.refs_0_, ...), custom_call_target="tpu_custom_call", output_to_operand_aliasing={{0}: (3, {}), {1}: (4, {}), {2}: (5, {}), {3}: (6, {})} | custom-call | bytes 4194304 | tf_op jit(solution)/shard_map/tiles_7/pallas_call | solution.py:109
  54.7 3.4 %collective-permute-done.9.refs_1_ = bf16[256,1024]{1,0:T(8,128)(2,1)S(1)} collective-permute-done((bf16[256,1024]{1,0:T(8,128)(2,1)S(1)}, bf16[256,1024]{1,0:T(8,128)(2,1)S(1)}, u32[]{:S(2)}, u32[]{:S(2)}) %collective-permute-start.9) | collective-permute-done | bytes 524320 | tf_op jit(solution)/shard_map/ppermute | solution.py:243
  58.2 2.0 %tiles_8.1 = (bf16[16,128,128]{2,1,0:T(8,128)(2,1)S(1)}, bf16[48,128,128]{2,1,0:T(8,128)(2,1)S(1)}, f32[16,128,128]{2,1,0:T(8,128)S(1)}, f32[48,128,128]{2,1,0:T(8,128)S(1)}) custom-call(s32[152]{0:T(256)S(1)} %pad_add_fusion.refs_0_, ...), custom_call_target="tpu_custom_call", output_to_operand_aliasing={{0}: (3, {}), {1}: (4, {}), {2}: (5, {}), {3}: (6, {})} | custom-call | bytes 4194304 | tf_op jit(solution)/shard_map/tiles_8/pallas_call | solution.py:109
  60.1 3.7 %collective-permute-done.8.refs_1_ = bf16[256,1024]{1,0:T(8,128)(2,1)S(1)} collective-permute-done((bf16[256,1024]{1,0:T(8,128)(2,1)S(1)}, bf16[256,1024]{1,0:T(8,128)(2,1)S(1)}, u32[]{:S(2)}, u32[]{:S(2)}) %collective-permute-start.8) | collective-permute-done | bytes 524320 | tf_op jit(solution)/shard_map/ppermute | solution.py:243
  65.0 4.4 %collective-permute-done.11.refs_1_ = bf16[256,1024]{1,0:T(8,128)(2,1)S(1)} collective-permute-done((bf16[256,1024]{1,0:T(8,128)(2,1)S(1)}, bf16[256,1024]{1,0:T(8,128)(2,1)S(1)}, u32[]{:S(2)}, u32[]{:S(2)}) %collective-permute-start.11) | collective-permute-done | bytes 524320 | tf_op jit(solution)/shard_map/ppermute | solution.py:243
  70.8 4.3 %collective-permute-done.10.refs_1_ = bf16[256,1024]{1,0:T(8,128)(2,1)S(1)} collective-permute-done((bf16[256,1024]{1,0:T(8,128)(2,1)S(1)}, bf16[256,1024]{1,0:T(8,128)(2,1)S(1)}, u32[]{:S(2)}, u32[]{:S(2)}) %collective-permute-start.10) | collective-permute-done | bytes 524320 | tf_op jit(solution)/shard_map/ppermute | solution.py:243
  82.1 4.1 %collective-permute-done.12.refs_1_ = bf16[256,1024]{1,0:T(8,128)(2,1)S(1)} collective-permute-done((bf16[256,1024]{1,0:T(8,128)(2,1)S(1)}, bf16[256,1024]{1,0:T(8,128)(2,1)S(1)}, u32[]{:S(2)}, u32[]{:S(2)}) %collective-permute-start.12) | collective-permute-done | bytes 524320 | tf_op jit(solution)/shard_map/ppermute | solution.py:243
  87.5 1.9 %collective-permute-done.14 = bf16[16,128,128]{2,1,0:T(8,128)(2,1)S(1)} collective-permute-done((bf16[16,128,128]{2,1,0:T(8,128)(2,1)S(1)}, bf16[16,128,128]{2,1,0:T(8,128)(2,1)S(1)}, u32[]{:S(2)}, u32[]{:S(2)}) %collective-permute-start.14) | collective-permute-done | bytes 524320 | tf_op jit(solution)/shard_map/ppermute | solution.py:147
  93.5 2.7 %collective-permute-done.16 = bf16[8,128,128]{2,1,0:T(8,128)(2,1)S(1)} collective-permute-done((bf16[8,128,128]{2,1,0:T(8,128)(2,1)S(1)}, bf16[8,128,128]{2,1,0:T(8,128)(2,1)S(1)}, u32[]{:S(2)}, u32[]{:S(2)}) %collective-permute-start.16) | collective-permute-done | bytes 262176 | tf_op jit(solution)/shard_map/ppermute | solution.py:147
  100.3 7.2 %collective-permute-done.18 = bf16[16,128,128]{2,1,0:T(8,128)(2,1)S(1)} collective-permute-done((bf16[16,128,128]{2,1,0:T(8,128)(2,1)S(1)}, bf16[16,128,128]{2,1,0:T(8,128)(2,1)S(1)}, u32[]{:S(2)}, u32[]{:S(2)}) %collective-permute-start.18) | collective-permute-done | bytes 524320 | tf_op jit(solution)/shard_map/ppermute | solution.py:147
  109.3 3.3 %collective-permute-start.20 = (bf16[4,128,128]{2,1,0:T(8,128)(2,1)S(1)}, bf16[4,128,128]{2,1,0:T(8,128)(2,1)S(1)}, u32[]{:S(2)}, u32[]{:S(2)}) collective-permute-start(bf16[4,128,128]{2,1,0:T(8,128)(2,1)S(1)} %get-tuple-element.287), channel_id=1, source_target_pairs={{0,32},{8,136},{16,48},{24,152},{32,0},{40,168},{48,16},{56,184},{... | collective-permute-start | bytes 393224 | tf_op jit(solution)/shard_map/ppermute | solution.py:147
  113.6 2.2 %collective-permute-done.20 = bf16[4,128,128]{2,1,0:T(8,128)(2,1)S(1)} collective-permute-done((bf16[4,128,128]{2,1,0:T(8,128)(2,1)S(1)}, bf16[4,128,128]{2,1,0:T(8,128)(2,1)S(1)}, u32[]{:S(2)}, u32[]{:S(2)}) %collective-permute-start.20) | collective-permute-done | bytes 131104 | tf_op jit(solution)/shard_map/ppermute | solution.py:147
  (75 shorter events, 41.1 us)
Async XLA Ops:
  0.0 13.2 %collective-permute-start = (bf16[256,1024]{1,0:T(8,128)(2,1)}, bf16[256,1024]{1,0:T(8,128)(2,1)S(1)}, u32[]{:S(2)}, u32[]{:S(2)}) collective-permute-start(bf16[256,1024]{1,0:T(8,128)(2,1)} %refs_1_.2), channel_id=1, source_target_pairs={{0,1},{1,2},{2,3},{3,4},{4,5},{5,6},{6,7},{7,0},{8,15},{9,8},{10,9... | collective-permute-start | bytes 1572872 | tf_op jit(solution)/shard_map/ppermute | solution.py:243
  1.9 16.9 %collective-permute-start.1 = (bf16[256,1024]{1,0:T(8,128)(2,1)}, bf16[256,1024]{1,0:T(8,128)(2,1)S(1)}, u32[]{:S(2)}, u32[]{:S(2)}) collective-permute-start(bf16[256,1024]{1,0:T(8,128)(2,1)} %refs_1_.3), channel_id=1, source_target_pairs={{0,1},{1,2},{2,3},{3,4},{4,5},{5,6},{6,7},{7,0},{8,15},{9,8},{10,9... | collective-permute-start | bytes 1572872 | tf_op jit(solution)/shard_map/ppermute | solution.py:243
  13.2 11.2 %collective-permute-start.3 = (bf16[256,1024]{1,0:T(8,128)(2,1)S(1)}, bf16[256,1024]{1,0:T(8,128)(2,1)S(1)}, u32[]{:S(2)}, u32[]{:S(2)}) collective-permute-start(bf16[256,1024]{1,0:T(8,128)(2,1)S(1)} %collective-permute-done.refs_1_), channel_id=1, source_target_pairs={{0,1},{1,2},{2,3},{3,4},{4,5},{5,6},{6,7},{7,0},{8,15},{9,8},{10,9... | collective-permute-start | bytes 1572872 | tf_op jit(solution)/shard_map/ppermute | solution.py:243
  14.3 4.7 %copy-start.4 = (bf16[256,1024]{1,0:T(8,128)(2,1)S(1)}, bf16[256,1024]{1,0:T(8,128)(2,1)}, u32[]{:S(2)}) copy-start(bf16[256,1024]{1,0:T(8,128)(2,1)} %refs_1_.3) | copy-start | bytes 1572868
  18.8 11.2 %collective-permute-start.2 = (bf16[256,1024]{1,0:T(8,128)(2,1)S(1)}, bf16[256,1024]{1,0:T(8,128)(2,1)S(1)}, u32[]{:S(2)}, u32[]{:S(2)}) collective-permute-start(bf16[256,1024]{1,0:T(8,128)(2,1)S(1)} %collective-permute-done.1.refs_1_), channel_id=1, source_target_pairs={{0,1},{1,2},{2,3},{3,4},{4,5},{5,6},{6,7},{7,0},{8,15},{9,8},{10,9... | collective-permute-start | bytes 1572872 | tf_op jit(solution)/shard_map/ppermute | solution.py:243
  24.5 11.2 %collective-permute-start.5 = (bf16[256,1024]{1,0:T(8,128)(2,1)S(1)}, bf16[256,1024]{1,0:T(8,128)(2,1)S(1)}, u32[]{:S(2)}, u32[]{:S(2)}) collective-permute-start(bf16[256,1024]{1,0:T(8,128)(2,1)S(1)} %collective-permute-done.3.refs_1_), channel_id=1, source_target_pairs={{0,1},{1,2},{2,3},{3,4},{4,5},{5,6},{6,7},{7,0},{8,15},{9,8},{10,9... | collective-permute-start | bytes 1572872 | tf_op jit(solution)/shard_map/ppermute | solution.py:243
  30.1 11.2 %collective-permute-start.4 = (bf16[256,1024]{1,0:T(8,128)(2,1)S(1)}, bf16[256,1024]{1,0:T(8,128)(2,1)S(1)}, u32[]{:S(2)}, u32[]{:S(2)}) collective-permute-start(bf16[256,1024]{1,0:T(8,128)(2,1)S(1)} %collective-permute-done.2.refs_1_), channel_id=1, source_target_pairs={{0,1},{1,2},{2,3},{3,4},{4,5},{5,6},{6,7},{7,0},{8,15},{9,8},{10,9... | collective-permute-start | bytes 1572872 | tf_op jit(solution)/shard_map/ppermute | solution.py:243
  35.7 11.2 %collective-permute-start.7 = (bf16[256,1024]{1,0:T(8,128)(2,1)S(1)}, bf16[256,1024]{1,0:T(8,128)(2,1)S(1)}, u32[]{:S(2)}, u32[]{:S(2)}) collective-permute-start(bf16[256,1024]{1,0:T(8,128)(2,1)S(1)} %collective-permute-done.5.refs_1_), channel_id=1, source_target_pairs={{0,1},{1,2},{2,3},{3,4},{4,5},{5,6},{6,7},{7,0},{8,15},{9,8},{10,9... | collective-permute-start | bytes 1572872 | tf_op jit(solution)/shard_map/ppermute | solution.py:243
  41.3 11.2 %collective-permute-start.6 = (bf16[256,1024]{1,0:T(8,128)(2,1)S(1)}, bf16[256,1024]{1,0:T(8,128)(2,1)S(1)}, u32[]{:S(2)}, u32[]{:S(2)}) collective-permute-start(bf16[256,1024]{1,0:T(8,128)(2,1)S(1)} %collective-permute-done.4.refs_1_), channel_id=1, source_target_pairs={{0,1},{1,2},{2,3},{3,4},{4,5},{5,6},{6,7},{7,0},{8,15},{9,8},{10,9... | collective-permute-start | bytes 1572872 | tf_op jit(solution)/shard_map/ppermute | solution.py:243
  46.9 11.2 %collective-permute-start.9 = (bf16[256,1024]{1,0:T(8,128)(2,1)S(1)}, bf16[256,1024]{1,0:T(8,128)(2,1)S(1)}, u32[]{:S(2)}, u32[]{:S(2)}) collective-permute-start(bf16[256,1024]{1,0:T(8,128)(2,1)S(1)} %collective-permute-done.7.refs_1_), channel_id=1, source_target_pairs={{0,1},{1,2},{2,3},{3,4},{4,5},{5,6},{6,7},{7,0},{8,15},{9,8},{10,9... | collective-permute-start | bytes 1572872 | tf_op jit(solution)/shard_map/ppermute | solution.py:243
  52.5 11.2 %collective-permute-start.8 = (bf16[256,1024]{1,0:T(8,128)(2,1)S(1)}, bf16[256,1024]{1,0:T(8,128)(2,1)S(1)}, u32[]{:S(2)}, u32[]{:S(2)}) collective-permute-start(bf16[256,1024]{1,0:T(8,128)(2,1)S(1)} %collective-permute-done.6.refs_1_), channel_id=1, source_target_pairs={{0,1},{1,2},{2,3},{3,4},{4,5},{5,6},{6,7},{7,0},{8,15},{9,8},{10,9... | collective-permute-start | bytes 1572872 | tf_op jit(solution)/shard_map/ppermute | solution.py:243
  58.2 11.2 %collective-permute-start.11 = (bf16[256,1024]{1,0:T(8,128)(2,1)S(1)}, bf16[256,1024]{1,0:T(8,128)(2,1)S(1)}, u32[]{:S(2)}, u32[]{:S(2)}) collective-permute-start(bf16[256,1024]{1,0:T(8,128)(2,1)S(1)} %collective-permute-done.9.refs_1_), channel_id=1, source_target_pairs={{0,1},{1,2},{2,3},{3,4},{4,5},{5,6},{6,7},{7,0},{8,15},{9,8},{10,9... | collective-permute-start | bytes 1572872 | tf_op jit(solution)/shard_map/ppermute | solution.py:243
  63.8 11.2 %collective-permute-start.10 = (bf16[256,1024]{1,0:T(8,128)(2,1)S(1)}, bf16[256,1024]{1,0:T(8,128)(2,1)S(1)}, u32[]{:S(2)}, u32[]{:S(2)}) collective-permute-start(bf16[256,1024]{1,0:T(8,128)(2,1)S(1)} %collective-permute-done.8.refs_1_), channel_id=1, source_target_pairs={{0,1},{1,2},{2,3},{3,4},{4,5},{5,6},{6,7},{7,0},{8,15},{9,8},{10,9... | collective-permute-start | bytes 1572872 | tf_op jit(solution)/shard_map/ppermute | solution.py:243
  69.4 11.2 %collective-permute-start.13 = (bf16[256,1024]{1,0:T(8,128)(2,1)S(1)}, bf16[256,1024]{1,0:T(8,128)(2,1)S(1)}, u32[]{:S(2)}, u32[]{:S(2)}) collective-permute-start(bf16[256,1024]{1,0:T(8,128)(2,1)S(1)} %collective-permute-done.11.refs_1_), channel_id=1, source_target_pairs={{0,1},{1,2},{2,3},{3,4},{4,5},{5,6},{6,7},{7,0},{8,15},{9,8},{10,9... | collective-permute-start | bytes 1572872 | tf_op jit(solution)/shard_map/ppermute | solution.py:243
  75.0 11.2 %collective-permute-start.12 = (bf16[256,1024]{1,0:T(8,128)(2,1)S(1)}, bf16[256,1024]{1,0:T(8,128)(2,1)S(1)}, u32[]{:S(2)}, u32[]{:S(2)}) collective-permute-start(bf16[256,1024]{1,0:T(8,128)(2,1)S(1)} %collective-permute-done.10.refs_1_), channel_id=1, source_target_pairs={{0,1},{1,2},{2,3},{3,4},{4,5},{5,6},{6,7},{7,0},{8,15},{9,8},{10,9... | collective-permute-start | bytes 1572872 | tf_op jit(solution)/shard_map/ppermute | solution.py:243
  87.4 2.0 %collective-permute-start.14 = (bf16[16,128,128]{2,1,0:T(8,128)(2,1)S(1)}, bf16[16,128,128]{2,1,0:T(8,128)(2,1)S(1)}, u32[]{:S(2)}, u32[]{:S(2)}) collective-permute-start(bf16[16,128,128]{2,1,0:T(8,128)(2,1)S(1)} %get-tuple-element.273), channel_id=1, source_target_pairs={{0,8},{8,0},{16,24},{24,16},{32,40},{40,32},{48,56},{56,48},{64,72... | collective-permute-start | bytes 1572872 | tf_op jit(solution)/shard_map/ppermute | solution.py:147
  89.4 3.4 %collective-permute-start.15 = (bf16[48,128,128]{2,1,0:T(8,128)(2,1)S(1)}, bf16[48,128,128]{2,1,0:T(8,128)(2,1)S(1)}, u32[]{:S(2)}, u32[]{:S(2)}) collective-permute-start(bf16[48,128,128]{2,1,0:T(8,128)(2,1)S(1)} %get-tuple-element.274), channel_id=1, source_target_pairs={{0,8},{8,0},{16,24},{24,16},{32,40},{40,32},{48,56},{56,48},{64,72... | collective-permute-start | bytes 4718600 | tf_op jit(solution)/shard_map/ppermute | solution.py:147
  89.8 6.4 %collective-permute-start.16 = (bf16[8,128,128]{2,1,0:T(8,128)(2,1)S(1)}, bf16[8,128,128]{2,1,0:T(8,128)(2,1)S(1)}, u32[]{:S(2)}, u32[]{:S(2)}) collective-permute-start(bf16[8,128,128]{2,1,0:T(8,128)(2,1)S(1)} %get-tuple-element.277), channel_id=1, source_target_pairs={{0,64},{8,24},{16,80},{24,40},{32,96},{40,56},{48,112},{56,8},{64,... | collective-permute-start | bytes 786440 | tf_op jit(solution)/shard_map/ppermute | solution.py:147
  90.3 7.6 %collective-permute-start.17 = (bf16[8,128,128]{2,1,0:T(8,128)(2,1)S(1)}, bf16[8,128,128]{2,1,0:T(8,128)(2,1)S(1)}, u32[]{:S(2)}, u32[]{:S(2)}) collective-permute-start(bf16[8,128,128]{2,1,0:T(8,128)(2,1)S(1)} %get-tuple-element.278), channel_id=1, source_target_pairs={{0,192},{8,56},{16,208},{24,8},{32,224},{40,24},{48,240},{56,40},{... | collective-permute-start | bytes 786440 | tf_op jit(solution)/shard_map/ppermute | solution.py:147
  98.2 9.3 %collective-permute-start.18 = (bf16[16,128,128]{2,1,0:T(8,128)(2,1)S(1)}, bf16[16,128,128]{2,1,0:T(8,128)(2,1)S(1)}, u32[]{:S(2)}, u32[]{:S(2)}) collective-permute-start(bf16[16,128,128]{2,1,0:T(8,128)(2,1)S(1)} %get-tuple-element.282), channel_id=1, source_target_pairs={{0,64},{8,24},{16,80},{24,40},{32,96},{40,56},{48,112},{56,8},{64,... | collective-permute-start | bytes 1572872 | tf_op jit(solution)/shard_map/ppermute | solution.py:147
  98.5 10.4 %collective-permute-start.19 = (bf16[16,128,128]{2,1,0:T(8,128)(2,1)S(1)}, bf16[16,128,128]{2,1,0:T(8,128)(2,1)S(1)}, u32[]{:S(2)}, u32[]{:S(2)}) collective-permute-start(bf16[16,128,128]{2,1,0:T(8,128)(2,1)S(1)} %get-tuple-element.283), channel_id=1, source_target_pairs={{0,192},{8,56},{16,208},{24,8},{32,224},{40,24},{48,240},{56,40},{... | collective-permute-start | bytes 1572872 | tf_op jit(solution)/shard_map/ppermute | solution.py:147
  109.3 6.6 %collective-permute-start.20 = (bf16[4,128,128]{2,1,0:T(8,128)(2,1)S(1)}, bf16[4,128,128]{2,1,0:T(8,128)(2,1)S(1)}, u32[]{:S(2)}, u32[]{:S(2)}) collective-permute-start(bf16[4,128,128]{2,1,0:T(8,128)(2,1)S(1)} %get-tuple-element.287), channel_id=1, source_target_pairs={{0,32},{8,136},{16,48},{24,152},{32,0},{40,168},{48,16},{56,184},{... | collective-permute-start | bytes 393224 | tf_op jit(solution)/shard_map/ppermute | solution.py:147
  112.6 5.0 %collective-permute-start.21 = (bf16[4,128,128]{2,1,0:T(8,128)(2,1)S(1)}, bf16[4,128,128]{2,1,0:T(8,128)(2,1)S(1)}, u32[]{:S(2)}, u32[]{:S(2)}) collective-permute-start(bf16[4,128,128]{2,1,0:T(8,128)(2,1)S(1)} %get-tuple-element.288), channel_id=1, source_target_pairs={{0,16},{8,72},{16,0},{24,88},{32,48},{40,104},{48,32},{56,120},{64... | collective-permute-start | bytes 393224 | tf_op jit(solution)/shard_map/ppermute | solution.py:147
  113.2 6.2 %collective-permute-start.22 = (bf16[4,128,128]{2,1,0:T(8,128)(2,1)S(1)}, bf16[4,128,128]{2,1,0:T(8,128)(2,1)S(1)}, u32[]{:S(2)}, u32[]{:S(2)}) collective-permute-start(bf16[4,128,128]{2,1,0:T(8,128)(2,1)S(1)} %get-tuple-element.289), channel_id=1, source_target_pairs={{0,48},{8,200},{16,32},{24,216},{32,16},{40,232},{48,0},{56,248},{... | collective-permute-start | bytes 393224 | tf_op jit(solution)/shard_map/ppermute | solution.py:147
  (4 other events, 4.6 us)
